TPU v7x, 32 devices: a whole 2x2x4 slice. The times are simulated.
32 devices in a mesh: gx: 16 (over z, x, core), gy: 2 (over y).
Axes of the slice: x: 2, y: 2, z: 4, core: 2. Of those that a mesh axis runs over, the one named last changes fastest.
Arguments:
- features: bfloat16 [96, 256, 256], P('gy', 'gx'), may hold values from -6 to 6
- first_filter: bfloat16 [256, 3, 3, 256], P('gy'), may hold values from -0.125 to 0.125
- second_filter: bfloat16 [256, 3, 3, 256], P('gy'), may hold values from -0.125 to 0.125
- cotangent: bfloat16 [256, 256, 96], P('gy', 'gx'), may hold values from -6 to 6
Outputs:
- output: bfloat16 [256, 256, 96], P('gy', 'gx')
- input_grad: bfloat16 [96, 256, 256], P('gy', 'gx')
- first_grad: float32 [256, 3, 3, 256], P('gy')
- second_grad: float32 [256, 3, 3, 256], P('gy')
All inputs are finite; a program needn't handle non-finite values.
Results may differ from a plain program's by a relative error of at most 0.0059.
Values may be sent and summed in bfloat16 or wider, within the bound.
No kernel may reach another device: no remote copies, remote signals or barrier semaphores. Data moves between devices by JAX's collectives and lax.ppermute only.
A program may use at most 128 MiB of HBM per device.

v0:
```python
import math

import jax
import jax.numpy as jnp
from jax import lax
from jax.sharding import PartitionSpec as P


def padded_2(block, sides, width):
    for axis, dim in sides:
        count = lax.axis_size(axis)
        forward = [(i, i + 1) for i in range(count - 1)]
        backward = [(target, source) for source, target in forward]
        low = lax.ppermute(
            lax.slice_in_dim(block, block.shape[dim] - width, None, axis=dim), axis, forward
        )
        high = lax.ppermute(lax.slice_in_dim(block, 0, width, axis=dim), axis, backward)
        block = jnp.concatenate([low, block, high], axis=dim)
    return block


def silu_parts(pre):
    sigma = jax.nn.sigmoid(pre)
    return (pre * sigma, sigma * (1.0 + pre * (1.0 - sigma)))


def conv_taps(padded, weight, height, width):
    total = jnp.zeros((height * width, weight.shape[3]), jnp.float32)
    for i in range(3):
        for j in range(3):
            window = padded[i : i + height, j : j + width, :].reshape(
                height * width, padded.shape[2]
            )
            total = total + jnp.dot(window, weight[i, j], preferred_element_type=jnp.float32)
    return total.reshape(height, width, weight.shape[3])


def flipped(weight):
    return jnp.transpose(weight[::-1, ::-1], (0, 1, 3, 2))


def filter_grad(padded, grad, height, width):
    flat_grad = grad.reshape(height * width, grad.shape[2])
    tap_list = []
    for i in range(3):
        for j in range(3):
            window = padded[i : i + height, j : j + width, :].reshape(
                height * width, padded.shape[2]
            )
            tap_list.append(
                lax.dot_general(
                    window, flat_grad, (((0,), (0,)), ((), ())), preferred_element_type=jnp.float32
                )
            )
    return jnp.stack(tap_list).reshape(3, 3, padded.shape[2], grad.shape[2])


def to_taps(weight):
    return jnp.transpose(weight, (1, 2, 3, 0))


def from_taps(weight):
    return jnp.transpose(weight, (3, 0, 1, 2))


def pad_rows(field):
    return jnp.pad(field, ((1, 1), (0, 0), (0, 0)))


def body(features, first_filter, second_filter, cotangent):
    band_count = lax.axis_size("gy")
    strip_count = lax.axis_size("gx")
    total_rows = features.shape[0] * band_count
    strip_width = features.shape[1]
    channels = features.shape[2]
    scale_factor = 1.0 / math.sqrt(total_rows * strip_width * strip_count)
    first_taps = to_taps(first_filter)
    second_taps = to_taps(second_filter)
    strip_input = lax.all_gather(features, "gy", axis=0, tiled=True)
    feat_padded = pad_rows(padded_2(strip_input, (("gx", 1),), 1))
    first_pre = conv_taps(feat_padded, first_taps, total_rows, strip_width)
    first_act, first_slope = silu_parts(first_pre)
    hidden = first_act.astype(jnp.bfloat16)
    hidden_all = lax.all_gather(hidden, "gy", axis=2, tiled=True)
    hidden_padded = pad_rows(padded_2(hidden_all, (("gx", 1),), 1))
    second_pre = conv_taps(hidden_padded, second_taps, total_rows, strip_width)
    second_act, second_slope = silu_parts(second_pre)
    output = jnp.transpose(second_act.astype(jnp.bfloat16), (2, 1, 0))
    cot_map = jnp.transpose(cotangent, (2, 1, 0))
    outer_grad = (cot_map.astype(jnp.float32) * second_slope).astype(jnp.bfloat16)
    second_grad = filter_grad(hidden_padded, outer_grad, total_rows, strip_width) * scale_factor
    second_grad = lax.psum(second_grad, "gx")
    outer_padded = pad_rows(padded_2(outer_grad, (("gx", 1),), 1))
    pixel_count = total_rows * strip_width
    total = jnp.zeros((channels // band_count * lax.axis_size("gy"), pixel_count), jnp.float32)
    for i in range(3):
        for j in range(3):
            window = outer_padded[i : i + total_rows, j : j + strip_width, :].reshape(
                pixel_count, outer_padded.shape[2]
            )
            total = total + lax.dot_general(
                second_taps[2 - i, 2 - j],
                window,
                (((1,), (1,)), ((), ())),
                preferred_element_type=jnp.float32,
            )
    hidden_share = lax.psum_scatter(total, "gy", scatter_dimension=0, tiled=True)
    hidden_grad = jnp.transpose(hidden_share).reshape(
        total_rows, strip_width, hidden_share.shape[0]
    )
    inner_grad = (hidden_grad * first_slope).astype(jnp.bfloat16)
    first_grad = filter_grad(feat_padded, inner_grad, total_rows, strip_width) * scale_factor
    inner_padded = pad_rows(padded_2(inner_grad, (("gx", 1),), 1))
    first_flipped = flipped(first_taps)
    input_grad = lax.psum_scatter(
        conv_taps(
            inner_padded, first_flipped, total_rows // band_count * lax.axis_size("gy"), strip_width
        ),
        "gy",
        scatter_dimension=0,
        tiled=True,
    ).astype(jnp.bfloat16)
    first_grad = lax.psum(first_grad, "gx")
    first_grad = from_taps(first_grad)
    second_grad = from_taps(second_grad)
    return (output, input_grad, first_grad, second_grad)


def solution(mesh):
    in_specs = (
        P("gy", "gx", None),
        P("gy", None, None, None),
        P("gy", None, None, None),
        P("gy", "gx", None),
    )
    out_specs = (
        P("gy", "gx", None),
        P("gy", "gx", None),
        P("gy", None, None, None),
        P("gy", None, None, None),
    )
    return jax.shard_map(body, mesh=mesh, in_specs=in_specs, out_specs=out_specs, check_vma=False)
```

profile of v0, /device:TPU:0, one launch (start us, length us, event | category | flops | bytes accessed | tf_op | source)
XLA Modules:
  0.0 266.9 jit_solution(18296116085584252017)
XLA Ops:
  7.2 1.1 copy.19
  8.3 12.8 %all_gather.6 = bf16[96,16,256]{2,0,1:T(8,128)(2,1)S(1)} all-gather(bf16[48,16,256]{2,0,1:T(8,128)(2,1)S(1)} %copy.19), channel_id=1, replica_groups=mesh['gx'=16,'gy'=2] {'gy'}, dimensions={0}, use_global_device_ids=true | all-gather | bytes 1179648 | tf_op jit(solution)/shard_map/all_gather | solution.py:79
  21.1 1.3 collective-permute-start.1
  22.4 3.0 %collective-permute-start = (bf16[96,1,256]{2,0,1:T(8,128)(2,1)S(1)}, bf16[96,1,256]{2,0,1:T(8,128)(2,1)S(1)}, u32[]{:S(2)}, u32[]{:S(2)}) collective-permute-start(bf16[96,1,256]{2,0,1:T(8,128)(2,1)S(1)} %get-tuple-element.26), channel_id=1, source_target_pairs={{0,2},{2,4},{4,6},{6,8},{8,10},{10,12},{12,14},{14,16},{16,18},{18... | collective-permute-start | bytes 147464 | tf_op jit(solution)/shard_map/ppermute | solution.py:14
  36.0 12.0 %all_gather.7 = bf16[96,16,256]{2,0,1:T(8,128)(2,1)S(1)} all-gather(bf16[96,16,128]{2,0,1:T(8,128)(2,1)S(1)} %multiply_convert_fusion.1), channel_id=1, replica_groups=mesh['gx'=16,'gy'=2] {'gy'}, dimensions={2}, use_global_device_ids=true | all-gather | bytes 1179648 | tf_op jit(solution)/shard_map/all_gather | solution.py:84
  48.0 1.3 collective-permute-start.3
  49.3 3.2 %collective-permute-start.2 = (bf16[96,1,256]{2,0,1:T(8,128)(2,1)S(1)}, bf16[96,1,256]{2,0,1:T(8,128)(2,1)S(1)}, u32[]{:S(2)}, u32[]{:S(2)}) collective-permute-start(bf16[96,1,256]{2,0,1:T(8,128)(2,1)S(1)} %get-tuple-element.22), channel_id=1, source_target_pairs={{0,2},{2,4},{4,6},{6,8},{8,10},{10,12},{12,14},{14,16},{16,18},{18... | collective-permute-start | bytes 147464 | tf_op jit(solution)/shard_map/ppermute | solution.py:14
  63.2 1.2 fusion.27
  64.4 1.3 collective-permute-start.5
  65.7 5.5 %collective-permute-start.4 = (bf16[96,1,128]{2,0,1:T(8,128)(2,1)S(1)}, bf16[96,1,128]{2,0,1:T(8,128)(2,1)S(1)}, u32[]{:S(2)}, u32[]{:S(2)}) collective-permute-start(bf16[96,1,128]{2,0,1:T(8,128)(2,1)S(1)} %get-tuple-element.46), channel_id=1, source_target_pairs={{0,2},{2,4},{4,6},{6,8},{8,10},{10,12},{12,14},{14,16},{16,18},{18... | collective-permute-start | bytes 73736 | tf_op jit(solution)/shard_map/ppermute | solution.py:14
  76.5 1.5 fusion
  78.1 2.0 reverse_bitcast_fusion
  80.1 2.1 fusion.12
  82.2 1.1 fusion.11
  83.2 1.1 fusion.10
  85.4 1.1 fusion.9
  86.5 1.1 fusion.2
  87.5 22.0 %reduce-scatter.3.cloned.1.call-done = f32[128,1536]{0,1:T(8,128)} async-done(((f32[256,1536]{0,1:T(8,128)}), f32[128,1536]{0,1:T(8,128)}) %reduce-scatter.3.cloned.1.call-update) | async-done | bytes 786448 | tf_op jit(solution)/shard_map/reduce_scatter | solution.py:107
  109.5 2.0 fusion.28
  111.5 1.3 collective-permute-start.7
  112.8 3.3 %collective-permute-start.6 = (bf16[96,1,128]{2,0,1:T(8,128)(2,1)S(1)}, bf16[96,1,128]{2,0,1:T(8,128)(2,1)S(1)}, u32[]{:S(2)}, u32[]{:S(2)}) collective-permute-start(bf16[96,1,128]{2,0,1:T(8,128)(2,1)S(1)} %get-tuple-element.42), channel_id=1, source_target_pairs={{0,2},{2,4},{4,6},{6,8},{8,10},{10,12},{12,14},{14,16},{16,18},{18... | collective-permute-start | bytes 73736 | tf_op jit(solution)/shard_map/ppermute | solution.py:14
  116.1 1.1 fusion.8
  123.5 1.5 convolution_add_fusion
  125.1 1.1 fusion.7
  126.2 1.1 fusion.6
  127.2 2.4 broadcast_multiply_fusion
  129.6 2.7 copy.64
  137.0 1.4 copy.63
  138.4 15.1 %reduce-scatter.5.cloned.1.call-done = f32[48,16,256]{2,1,0:T(8,128)} async-done(((f32[96,16,256]{2,1,0:T(8,128)}), f32[48,16,256]{2,1,0:T(8,128)}) %reduce-scatter.5.cloned.1.call-update) | async-done | bytes 786448 | tf_op jit(solution)/shard_map/reduce_scatter | solution.py:115
  153.5 1.9 convert_element_type.37
  155.4 101.5 %all-reduce.7.cloned.1.call-done = (f32[128,3,3,256]{3,0,2,1:T(8,128)}, f32[128,3,3,256]{3,0,2,1:T(8,128)}) async-done(((f32[128,3,3,256]{3,0,2,1:T(8,128)}, f32[128,3,3,256]{3,0,2,1:T(8,128)}), (f32[128,3,3,256]{3,0,2,1:T(8,128)}, f32[128,3,3,256]{3,0,2,1:T(8,128)})) %all-reduce.7.cloned.1.call-update) | async-done | bytes 2359312 | tf_op jit(solution)/shard_map/psum | solution.py:123
  256.9 2.5 copy.98
  (158 shorter events, 39.1 us)
Async XLA Ops:
  7.2 102.4 %reduce-scatter.3.cloned.1.call-start = ((), (), s32[]{:S(2)}) async-start(), calls=%async_computation.2 | async-start | bytes 2359296 | tf_op jit(solution)/shard_map/reduce_scatter | solution.py:107
  21.1 4.8 %collective-permute-start.1 = (bf16[96,1,256]{2,0,1:T(8,128)(2,1)S(1)}, bf16[96,1,256]{2,0,1:T(8,128)(2,1)S(1)}, u32[]{:S(2)}, u32[]{:S(2)}) collective-permute-start(bf16[96,1,256]{2,0,1:T(8,128)(2,1)S(1)} %get-tuple-element.27), channel_id=1, source_target_pairs={{2,0},{4,2},{6,4},{8,6},{10,8},{12,10},{14,12},{16,14},{18,16},{20... | collective-permute-start | bytes 147464 | tf_op jit(solution)/shard_map/ppermute | solution.py:17
  22.4 3.9 %collective-permute-start = (bf16[96,1,256]{2,0,1:T(8,128)(2,1)S(1)}, bf16[96,1,256]{2,0,1:T(8,128)(2,1)S(1)}, u32[]{:S(2)}, u32[]{:S(2)}) collective-permute-start(bf16[96,1,256]{2,0,1:T(8,128)(2,1)S(1)} %get-tuple-element.26), channel_id=1, source_target_pairs={{0,2},{2,4},{4,6},{6,8},{8,10},{10,12},{12,14},{14,16},{16,18},{18... | collective-permute-start | bytes 147464 | tf_op jit(solution)/shard_map/ppermute | solution.py:14
  29.0 0.9 copy-start.9
  29.9 0.9 copy-start.5
  31.2 1.1 copy-start.16
  35.6 17.3 %copy-start.3 = (f32[1536,128]{1,0:T(8,128)}, f32[1536,128]{1,0:T(8,128)S(1)}, u32[]{:S(2)}) copy-start(f32[1536,128]{1,0:T(8,128)S(1)} %convolution_add_fusion.24) | copy-start | bytes 2359300
  48.0 5.0 %collective-permute-start.3 = (bf16[96,1,256]{2,0,1:T(8,128)(2,1)S(1)}, bf16[96,1,256]{2,0,1:T(8,128)(2,1)S(1)}, u32[]{:S(2)}, u32[]{:S(2)}) collective-permute-start(bf16[96,1,256]{2,0,1:T(8,128)(2,1)S(1)} %get-tuple-element.23), channel_id=1, source_target_pairs={{2,0},{4,2},{6,4},{8,6},{10,8},{12,10},{14,12},{16,14},{18,16},{20... | collective-permute-start | bytes 147464 | tf_op jit(solution)/shard_map/ppermute | solution.py:17
  49.3 3.9 %collective-permute-start.2 = (bf16[96,1,256]{2,0,1:T(8,128)(2,1)S(1)}, bf16[96,1,256]{2,0,1:T(8,128)(2,1)S(1)}, u32[]{:S(2)}, u32[]{:S(2)}) collective-permute-start(bf16[96,1,256]{2,0,1:T(8,128)(2,1)S(1)} %get-tuple-element.22), channel_id=1, source_target_pairs={{0,2},{2,4},{4,6},{6,8},{8,10},{10,12},{12,14},{14,16},{16,18},{18... | collective-permute-start | bytes 147464 | tf_op jit(solution)/shard_map/ppermute | solution.py:14
  55.9 0.9 copy-start.11
  56.8 0.9 copy-start.7
  58.1 1.1 copy-start.14
  62.2 1.0 copy-start.18
  64.4 8.8 %copy-start = (bf16[96,16,128]{2,0,1:T(8,128)(2,1)}, bf16[96,16,128]{2,0,1:T(8,128)(2,1)S(1)}, u32[]{:S(2)}) copy-start(bf16[96,16,128]{2,0,1:T(8,128)(2,1)S(1)} %get-tuple-element.18) | copy-start | bytes 1179652
  64.4 7.0 %collective-permute-start.5 = (bf16[96,1,128]{2,0,1:T(8,128)(2,1)S(1)}, bf16[96,1,128]{2,0,1:T(8,128)(2,1)S(1)}, u32[]{:S(2)}, u32[]{:S(2)}) collective-permute-start(bf16[96,1,128]{2,0,1:T(8,128)(2,1)S(1)} %get-tuple-element.47), channel_id=1, source_target_pairs={{2,0},{4,2},{6,4},{8,6},{10,8},{12,10},{14,12},{16,14},{18,16},{20... | collective-permute-start | bytes 73736 | tf_op jit(solution)/shard_map/ppermute | solution.py:17
  65.7 6.1 %collective-permute-start.4 = (bf16[96,1,128]{2,0,1:T(8,128)(2,1)S(1)}, bf16[96,1,128]{2,0,1:T(8,128)(2,1)S(1)}, u32[]{:S(2)}, u32[]{:S(2)}) collective-permute-start(bf16[96,1,128]{2,0,1:T(8,128)(2,1)S(1)} %get-tuple-element.46), channel_id=1, source_target_pairs={{0,2},{2,4},{4,6},{6,8},{8,10},{10,12},{12,14},{14,16},{16,18},{18... | collective-permute-start | bytes 73736 | tf_op jit(solution)/shard_map/ppermute | solution.py:14
  78.1 75.4 %reduce-scatter.5.cloned.1.call-start = ((), (), s32[]{:S(2)}) async-start(), calls=%async_computation.3 | async-start | bytes 2359296 | tf_op jit(solution)/shard_map/reduce_scatter | solution.py:115
  78.1 4.1 %copy-start.1 = (bf16[96,16,128]{2,0,1:T(8,128)(2,1)S(1)}, bf16[96,16,128]{2,0,1:T(8,128)(2,1)}, u32[]{:S(2)}) copy-start(bf16[96,16,128]{2,0,1:T(8,128)(2,1)} %copy-done) | copy-start | bytes 1179652
  82.2 2.1 copy-start.12
  84.3 2.1 copy-start.8
  86.5 29.7 %copy-start.2 = (bf16[96,16,128]{2,0,1:T(8,128)(2,1)S(1)}, bf16[96,16,128]{2,0,1:T(8,128)(2,1)}, u32[]{:S(2)}) copy-start(bf16[96,16,128]{2,0,1:T(8,128)(2,1)} %copy-done) | copy-start | bytes 1179652
  111.5 5.7 %collective-permute-start.7 = (bf16[96,1,128]{2,0,1:T(8,128)(2,1)S(1)}, bf16[96,1,128]{2,0,1:T(8,128)(2,1)S(1)}, u32[]{:S(2)}, u32[]{:S(2)}) collective-permute-start(bf16[96,1,128]{2,0,1:T(8,128)(2,1)S(1)} %get-tuple-element.43), channel_id=1, source_target_pairs={{2,0},{4,2},{6,4},{8,6},{10,8},{12,10},{14,12},{16,14},{18,16},{20... | collective-permute-start | bytes 73736 | tf_op jit(solution)/shard_map/ppermute | solution.py:17
  112.8 4.4 %collective-permute-start.6 = (bf16[96,1,128]{2,0,1:T(8,128)(2,1)S(1)}, bf16[96,1,128]{2,0,1:T(8,128)(2,1)S(1)}, u32[]{:S(2)}, u32[]{:S(2)}) collective-permute-start(bf16[96,1,128]{2,0,1:T(8,128)(2,1)S(1)} %get-tuple-element.42), channel_id=1, source_target_pairs={{0,2},{2,4},{4,6},{6,8},{8,10},{10,12},{12,14},{14,16},{16,18},{18... | collective-permute-start | bytes 73736 | tf_op jit(solution)/shard_map/ppermute | solution.py:14
  118.4 1.1 copy-start.15
  120.5 1.1 copy-start.4
  120.5 1.4 copy-start.13
  125.0 131.9 %all-reduce.7.cloned.1.call-start = ((), (), s32[]{:S(2)}) async-start(), calls=%async_computation.4 | async-start | bytes 4718592 | tf_op jit(solution)/shard_map/psum | solution.py:123
  132.7 1.4 copy-start.10
  134.1 1.1 copy-start.6
  256.9 2.5 copy-start.17
Sparse Core Ops, SparseCore 0:
  78.2 31.3 reduce-scatter.2
  125.1 28.3 reduce-scatter.4
  157.7 99.1 all-reduce.6
where the time goes:
time: 268 us; the launch traced here: 267 us
  waiting for transfers between devices  140 us (52%)
  matrix products  29.7 us (11%)
  local copies, waits for them, and re-layouts  28.8 us (11%)
  blocking collectives  24.8 us (9%)
  starting transfers between devices  20.3 us (8%)
  between operations  14.6 us (5%)
  other arithmetic  9.07 us (3%)
    psum x1, waiting for transfers between devices, body(): first_grad = lax.psum(first_grad, 'gx')  101 us
    reduce_scatter x1, waiting for transfers between devices, body(): lax.psum_scatter(total, 'gy', scatter_dimension=0, tiled=True)  22 us
    reduce_scatter x1, waiting for transfers between devices, body(): lax.psum_scatter(conv_taps(inner_padded, first_flipped, total_rows // ban...  15.1 us
    ppermute x4, starting transfers between devices, padded_2(): lax.ppermute(lax.slice_in_dim(block, block.shape[dim] - width, None, axis...  15.1 us
    dot_general x18, matrix products, filter_grad(): lax.dot_general(window, flat_grad, (((0,), (0,)), ((), ())), preferred_el...  14.3 us
    all_gather x1, blocking collectives, body(): strip_input = lax.all_gather(features, 'gy', axis=0, tiled=True)  12.8 us
    all_gather x1, blocking collectives, body(): hidden_all = lax.all_gather(hidden, 'gy', axis=2, tiled=True)  12 us
    dot_general x27, matrix products, conv_taps(): jnp.dot(window, weight[i, j], preferred_element_type=jnp.float32)  11.1 us
  transfers between devices with their start and end apart: 11, of which 6 were waited for; matrix products, arithmetic and copies ran while one was open for 10% of the time, Pallas kernels for 0%

commit v1 on v0

v1 whole, which is shorter than its diff:
```python
import functools
import math

import jax
import jax.numpy as jnp
from jax import lax
from jax.experimental import pallas as pl
from jax.experimental.pallas import tpu as pltpu
from jax.sharding import PartitionSpec as P

F32, BF16 = jnp.float32, jnp.bfloat16
OFF = 8
VMEM_LIMIT = 56 * 1024 * 1024
NT = (((1,), (1,)), ((), ()))


def call(kernel, outs, args, scratch=(), flops=0, smem_args=1):
    specs = [pl.BlockSpec(memory_space=pltpu.SMEM)] * smem_args
    specs += [pl.BlockSpec(memory_space=pltpu.VMEM)] * (len(args) - smem_args)
    nbytes = sum(a.size * a.dtype.itemsize for a in args[smem_args:])
    nbytes += sum(math.prod(s) * jnp.dtype(t).itemsize for s, t in outs)
    return pl.pallas_call(
        kernel,
        out_shape=[jax.ShapeDtypeStruct(s, t) for s, t in outs],
        in_specs=specs,
        out_specs=[pl.BlockSpec(memory_space=pltpu.VMEM)] * len(outs),
        scratch_shapes=list(scratch),
        compiler_params=pltpu.CompilerParams(vmem_limit_bytes=VMEM_LIMIT),
        cost_estimate=pl.CostEstimate(flops=flops, bytes_accessed=nbytes, transcendentals=0),
    )(*args)


def silu_parts(pre):
    sigma = 1.0 / (1.0 + jnp.exp(-pre))
    return pre * sigma, sigma * (1.0 + pre * (1.0 - sigma))


def row_mask(first, rows, total):
    at = lax.broadcasted_iota(jnp.int32, (rows, 1), 0) + (first - OFF)
    return (at >= 0) & (at < total)


def shifted_rows(x):
    n = x.shape[0]
    return pltpu.roll(x, 1, 0), x, pltpu.roll(x, n - 1, 0)


def fill_shifted(buf, c, x):
    ch = x.shape[1]
    for i, part in enumerate(shifted_rows(x)):
        buf[c, :, i * ch : (i + 1) * ch] = part.astype(BF16)


def conv_chunk(buf, w, c0, n, backward):
    rows, ch = buf.shape[1], w.shape[1]
    total = None
    for j in range(3):
        for i in range(3):
            lhs = buf[c0 + j : c0 + j + n, :, i * ch : (i + 1) * ch].reshape(n * rows, ch)
            if backward:
                term = jnp.dot(lhs, w[(2 - j) * 3 + (2 - i)], preferred_element_type=F32)
            else:
                term = lax.dot_general(lhs, w[j * 3 + i], NT, preferred_element_type=F32)
            total = term if total is None else total + term
    return total.reshape(n, rows, ch)


def chunks(total, most):
    parts = -(-total // most)
    base, extra = divmod(total, parts)
    out, at = [], 0
    for p in range(parts):
        n = base + (p < extra)
        out.append((at, n))
        at += n
    return out


def assemble_filter(w, own, pieces, iy, core, ny):
    co = own.shape[1]
    half = co // 2
    w[:, pl.ds(pl.multiple_of(iy * co, co), co), :] = own[...]
    for d in range(1, ny):
        src = lax.rem(iy - d + ny, ny)
        mine, other = pieces
        at = pl.multiple_of(src * co + core * half, half)
        w[:, pl.ds(at, half), :] = mine[d - 1]
        at = pl.multiple_of(src * co + (1 - core) * half, half)
        w[:, pl.ds(at, half), :] = other[d - 1]


def conv1_kernel(dims, where, ft, left, right, up, down, own, mine, other, hidden, slope, fbuf, w, buf):
    ny, hl, wl, height, width = dims
    iy, ix = where[0], where[1]
    rows = fbuf.shape[1]
    ok = row_mask(iy * hl, rows, height)
    for c in range(wl + 8):
        mid = left[c] if c < 4 else (ft[c - 4] if c < wl + 4 else right[c - wl - 4])
        x = jnp.concatenate([up[c].astype(F32), mid.astype(F32), down[c].astype(F32)], axis=0)
        x = jnp.where(ok, x, 0.0)
        fbuf[c] = x.astype(BF16)
        fill_shifted(buf, c, x)
    assemble_filter(w, own, (mine, other), iy, ix % 2, ny)
    for c0, n in chunks(wl + 6, 11):
        pre = conv_chunk(buf, w, c0, n, False)
        for q in range(n):
            c = c0 + q
            col = ix * wl + c - 3
            act, grad = silu_parts(pre[q])
            inside = ok & (col >= 0) & (col < width)
            hidden[c] = jnp.where(inside, act, 0.0).astype(BF16)
            if 2 <= c < wl + 4:
                slope[c - 2] = jnp.where(inside, grad, 0.0)


def conv2_kernel(dims, where, hidden, own, mine, other, act_out, slope, w, buf):
    ny, hl, wl, height, width = dims
    iy, ix = where[0], where[1]
    rows = hidden.shape[1]
    ok = row_mask(iy * hl, rows, height)
    for c in range(wl + 6):
        fill_shifted(buf, c, hidden[c].astype(F32))
    assemble_filter(w, own, (mine, other), iy, ix % 2, ny)
    for c0, n in chunks(wl + 4, 10):
        pre = conv_chunk(buf, w, c0, n, False)
        for q in range(n):
            c = c0 + q
            col = ix * wl + c - 2
            act, grad = silu_parts(pre[q])
            inside = ok & (col >= 0) & (col < width)
            slope[c] = jnp.where(inside, grad, 0.0)
            if 2 <= c < wl + 2:
                act_out[c - 2] = act[OFF : OFF + hl].astype(BF16)


def own_rows(rows, hl):
    at = lax.broadcasted_iota(jnp.int32, (rows, 1), 0)
    return (at >= OFF) & (at < OFF + hl)


def filter_grad(where, buf, first, grad_t, wl, keep, send):
    core = where[1] % 2
    rows, ch = buf.shape[1], grad_t.shape[0]
    half = ch // 2
    for j in range(3):
        for i in range(3):
            rhs = buf[first + j : first + j + wl, :, i * ch : (i + 1) * ch].reshape(wl * rows, ch)
            g = jnp.dot(grad_t, rhs, preferred_element_type=F32)
            low, high = g[:, :half], g[:, half:]
            keep[j * 3 + i] = jnp.where(core == 0, low, high)
            send[j * 3 + i] = jnp.where(core == 0, high, low).astype(BF16)


def outer_kernel(dims, count, where, hidden, slope, *refs):
    cots, (outer, keep, send, buf, gt) = refs[:count], refs[count:]
    ny, hl, wl, height, width = dims
    iy = where[0]
    rows = hidden.shape[1]
    own = own_rows(rows, hl)
    for c in range(wl + 2):
        fill_shifted(buf, c, hidden[c + 2].astype(F32))
    for c in range(wl + 4):
        parts = [ref[c].astype(F32) for ref in cots]
        if len(parts) == 2:
            a, b = parts
            parts = [jnp.where(iy == 0, a, b), jnp.where(iy == 0, b, a)]
        outer[c] = (jnp.concatenate(parts, axis=1) * slope[c]).astype(BF16)
    for c in range(wl):
        val = jnp.where(own, outer[c + 2].astype(F32), 0.0)
        gt[:, c * rows : (c + 1) * rows] = val.T.astype(BF16)
    filter_grad(where, buf, 0, gt[...], wl, keep, send)


def inner_kernel(dims, where, outer, own, mine, other, slope, fbuf, inner, keep, send, w, buf, gt):
    ny, hl, wl, height, width = dims
    iy, ix = where[0], where[1]
    rows = fbuf.shape[1]
    for c in range(wl + 4):
        fill_shifted(buf, c, outer[c].astype(F32))
    assemble_filter(w, own, (mine, other), iy, ix % 2, ny)
    mine_rows = own_rows(rows, hl)
    for c0, n in chunks(wl + 2, 9):
        grad = conv_chunk(buf, w, c0, n, True)
        for q in range(n):
            c = c0 + q
            val = grad[q] * slope[c]
            inner[c] = val.astype(BF16)
            if 1 <= c < wl + 1:
                val = jnp.where(mine_rows, val, 0.0)
                gt[:, (c - 1) * rows : c * rows] = val.T.astype(BF16)
    for c in range(wl + 2):
        fill_shifted(buf, c, fbuf[c + 3].astype(F32))
    filter_grad(where, buf, 0, gt[...], wl, keep, send)


def input_kernel(dims, where, inner, own, mine, other, out, w, buf):
    ny, hl, wl, height, width = dims
    iy, ix = where[0], where[1]
    for c in range(wl + 2):
        fill_shifted(buf, c, inner[c].astype(F32))
    assemble_filter(w, own, (mine, other), iy, ix % 2, ny)
    for c0, n in chunks(wl, 8):
        grad = conv_chunk(buf, w, c0, n, True)
        for q in range(n):
            out[c0 + q] = grad[q, OFF : OFF + hl].astype(BF16)


def split_kernel(blocks, where, keep, came, own, *messages):
    iy, ix = where[0], where[1]
    ny = blocks // 2
    size = keep.shape[1] // blocks
    x = lax.rem(lax.div(ix, 2), 2)

    def block(y, b):
        at = pl.multiple_of((y * 2 + b) * size, size)
        return keep[:, pl.ds(at, size), :] + came[:, pl.ds(at, size), :].astype(F32)

    own[...] = block(iy, x)
    m = 0
    for d in range(ny):
        for b in range(2):
            if d or b:
                y = lax.rem(iy + d, ny)
                messages[m][...] = block(y, x if b == 0 else 1 - x).astype(BF16)
                m += 1


def reduce_filter(where, keep, send, nx, ny, iy, ix):
    other_core = [(i, i ^ 1) for i in range(nx)]
    came = lax.ppermute(send, "gx", other_core)
    blocks = 2 * ny
    taps, ch, half = keep.shape
    size = ch // blocks
    outs = [((taps, size, half), F32)] + [((taps, size, half), BF16)] * (blocks - 1)
    parts = call(functools.partial(split_kernel, blocks), outs, (where, keep, came))
    total, messages = parts[0], parts[1:]
    arrived = []
    m = 0
    for d in range(ny):
        for b in range(2):
            if d or b:
                pairs = [
                    (g * ny + y, (g ^ (2 * b)) * ny + (y + d) % ny) for g in range(nx) for y in range(ny)
                ]
                arrived.append(lax.ppermute(messages[m], ("gx", "gy"), pairs))
                m += 1
    for part in arrived:
        total = total + part.astype(F32)
    total = total.astype(BF16)
    bits = [1 << b for b in range(2, nx.bit_length() - 1)]
    for step in range(len(bits)):
        near, far = bits[step], bits[len(bits) - 1 - step]
        pairs = [(g, g ^ (near if g % 2 == 0 else far)) for g in range(nx)]
        part = lax.ppermute(total, "gx", pairs)
        total = (total.astype(F32) + part.astype(F32)).astype(BF16)
    beside = lax.ppermute(total, "gx", [(g, g ^ 2) for g in range(nx)])
    first = (ix // 2) % 2 == 0
    both = jnp.concatenate(
        [jnp.where(first, total, beside), jnp.where(first, beside, total)], axis=1
    )
    rest = lax.ppermute(both, "gx", other_core)
    low = ix % 2 == 0
    return jnp.concatenate([jnp.where(low, both, rest), jnp.where(low, rest, both)], axis=2)


def body(features, first_filter, second_filter, cotangent):
    ny, nx = lax.axis_size("gy"), lax.axis_size("gx")
    iy, ix = lax.axis_index("gy"), lax.axis_index("gx")
    hl, wl, ch = features.shape
    co = first_filter.shape[0]
    height, width = hl * ny, wl * nx
    rows = -(-(hl + 2 * OFF) // 16) * 16
    dims = (ny, hl, wl, height, width)
    scale_factor = 1.0 / math.sqrt(height * width)
    where = jnp.stack([iy, ix]).astype(jnp.int32)
    core = ix % 2
    forward = [(i, i + 1) for i in range(nx - 1)]
    backward = [(i + 1, i) for i in range(nx - 1)]

    def round_y(x, d):
        return lax.ppermute(x, "gy", [(i, (i + d) % ny) for i in range(ny)])

    def gathered(taps):
        half = co // 2
        send = lax.dynamic_slice_in_dim(taps, core * half, half, 1)
        mine = jnp.stack([round_y(send, d) for d in range(1, ny)])
        return mine, lax.ppermute(mine, "gx", [(i, i ^ 1) for i in range(nx)])

    first_own = jnp.transpose(first_filter, (2, 1, 0, 3)).reshape(9, co, ch)
    second_own = jnp.transpose(second_filter, (2, 1, 0, 3)).reshape(9, co, ch)
    first_in = gathered(first_own)
    second_in = gathered(second_own)

    ft = jnp.transpose(features, (1, 0, 2))
    left = lax.ppermute(ft[wl - 4 :], "gx", forward)
    right = lax.ppermute(ft[:4], "gx", backward)
    strip = jnp.concatenate([left, ft, right], axis=0)
    if ny == 2:
        up = down = round_y(jnp.where(iy == 0, strip[:, hl - OFF :], strip[:, :OFF]), 1)
    else:
        up = round_y(strip[:, hl - OFF :], 1)
        down = round_y(strip[:, :OFF], ny - 1)

    ct = jnp.transpose(cotangent, (1, 2, 0))
    ct = jnp.concatenate(
        [lax.ppermute(ct[wl - 2 :], "gx", forward), ct, lax.ppermute(ct[:2], "gx", backward)], axis=0
    )
    ct = jnp.pad(ct, ((0, 0), (OFF, rows - OFF - hl), (0, 0)))

    def rows_of(y):
        return lax.dynamic_slice_in_dim(ct, y * hl, rows, 1)

    cots = [rows_of(iy)] + [round_y(rows_of((iy + d) % ny), d) for d in range(1, ny)]
    if ny != 2:
        full = jnp.zeros((wl + 4, rows, ch), BF16)
        for d, part in enumerate(cots):
            full = lax.dynamic_update_slice_in_dim(full, part, ((iy - d) % ny) * co, 2)
        cots = [full]

    bf = lambda *s: pltpu.VMEM(s, BF16)
    weights = bf(9, ch, ch)
    tap_flops = 2 * 9 * ch * ch * rows

    fbuf_shape = ((wl + 8, rows, ch), BF16)
    hidden, slope1, fbuf = call(
        functools.partial(conv1_kernel, dims),
        [((wl + 6, rows, ch), BF16), ((wl + 2, rows, ch), F32), fbuf_shape],
        (where, ft, left, right, up, down, first_own, *first_in),
        [weights, bf(wl + 8, rows, 3 * ch)],
        tap_flops * (wl + 6),
    )
    act, slope2 = call(
        functools.partial(conv2_kernel, dims),
        [((wl, hl, ch), BF16), ((wl + 4, rows, ch), F32)],
        (where, hidden, second_own, *second_in),
        [weights, bf(wl + 6, rows, 3 * ch)],
        tap_flops * (wl + 4),
    )
    grad_shapes = [((9, ch, ch // 2), F32), ((9, ch, ch // 2), BF16)]
    outer, keep2, send2 = call(
        functools.partial(outer_kernel, dims, len(cots)),
        [((wl + 4, rows, ch), BF16)] + grad_shapes,
        (where, hidden, slope2, *cots),
        [bf(wl + 2, rows, 3 * ch), bf(ch, wl * rows)],
        tap_flops * wl,
    )
    inner, keep1, send1 = call(
        functools.partial(inner_kernel, dims),
        [((wl + 2, rows, ch), BF16)] + grad_shapes,
        (where, outer, second_own, *second_in, slope1, fbuf),
        [weights, bf(wl + 4, rows, 3 * ch), bf(ch, wl * rows)],
        tap_flops * (2 * wl + 2),
    )
    (input_grad,) = call(
        functools.partial(input_kernel, dims),
        [((wl, hl, ch), BF16)],
        (where, inner, first_own, *first_in),
        [weights, bf(wl + 2, rows, 3 * ch)],
        tap_flops * wl,
    )
    input_grad = jnp.transpose(input_grad, (1, 0, 2))

    def channels_of(y):
        return lax.dynamic_slice_in_dim(act, y * co, co, 2)

    parts = [channels_of(iy)] + [round_y(channels_of((iy + d) % ny), d) for d in range(1, ny)]
    output = jnp.zeros((wl, height, co), BF16)
    for d, part in enumerate(parts):
        output = lax.dynamic_update_slice_in_dim(output, part, ((iy - d) % ny) * hl, 1)
    output = jnp.transpose(output, (2, 0, 1))

    grads = []
    for keep, send in ((keep1, send1), (keep2, send2)):
        total = reduce_filter(where, keep, send, nx, ny, iy, ix)
        total = total.astype(F32) * scale_factor
        grads.append(jnp.transpose(total.reshape(3, 3, co, ch), (2, 1, 0, 3)))
    return output, input_grad, grads[0], grads[1]


def solution(mesh):
    in_specs = (
        P("gy", "gx", None),
        P("gy", None, None, None),
        P("gy", None, None, None),
        P("gy", "gx", None),
    )
    out_specs = (
        P("gy", "gx", None),
        P("gy", "gx", None),
        P("gy", None, None, None),
        P("gy", None, None, None),
    )
    return jax.shard_map(body, mesh=mesh, in_specs=in_specs, out_specs=out_specs, check_vma=False)
```

time: 268 us -> 112 us (0.42)
  waiting for transfers between devices: 140 us -> 26.4 us
  Pallas kernels: 0 us -> 30.6 us
  matrix products: 29.7 us -> 0 us
  blocking collectives: 24.8 us -> 0 us
  starting transfers between devices: 20.3 us -> 40.1 us
  local copies, waits for them, and re-layouts: 28.8 us -> 9.57 us
  between operations: 14.6 us -> 1.11 us
  other arithmetic: 9.07 us -> 4.03 us
    psum x1 -> x0, waiting for transfers between devices: 101 us -> none  [body(): first_grad = lax.psum(first_grad, 'gx')]
    reduce_scatter x2 -> x0, waiting for transfers between devices: 37.1 us -> none  [the longest x1 22 us: body(): lax.psum_scatter(total, 'gy', scatter_dimension=0, tiled=True)]
    pallas_call x0 -> x7, Pallas kernels: none -> 30.6 us  [call(): pl.pallas_call(kernel, out_shape=[jax.ShapeDtypeStruct(s, t) for s, t in...]
    dot_general x54 -> x0, matrix products: 29.7 us -> none  [the longest x18 14.3 us: filter_grad(): lax.dot_general(window, flat_grad, (((0,), (0,)), ((), ())), preferred_el...]
    ppermute x8 -> x27, waiting for transfers between devices: 1.07 us -> 26.4 us  [the longest x4 8.02 us: reduce_filter(): part = lax.ppermute(total, 'gx', pairs)]
    all_gather x2 -> x0, blocking collectives: 24.8 us -> none  [the longest x1 12.8 us: body(): strip_input = lax.all_gather(features, 'gy', axis=0, tiled=True)]
    ppermute x8 -> x27, starting transfers between devices: 20.2 us -> 40.1 us  [the longest x5 8.58 us: round_y(): return lax.ppermute(x, 'gy', [(i, (i + d) % ny) for i in range(ny)])]
    slice x44 -> x2, local copies, waits for them, and re-layouts: 11.9 us -> 0.91 us  [the longest x1 0.89 us: body(): ct[wl - 2:]]
  transfers between devices with their start and end apart: 11 -> 27, of which waited for: 6 -> 10; matrix products, arithmetic and copies ran while one was open for 10% -> 6% of each run, Pallas kernels for 0% -> 17%
where the time goes in v1:
time: 112 us
  starting transfers between devices  40.1 us (36%)
  Pallas kernels  30.6 us (27%)
  waiting for transfers between devices  26.4 us (24%)
  local copies, waits for them, and re-layouts  9.57 us (9%)
  other arithmetic  4.03 us (4%)
    pallas_call x7, Pallas kernels, call(): pl.pallas_call(kernel, out_shape=[jax.ShapeDtypeStruct(s, t) for s, t in...  30.6 us
    ppermute x5, starting transfers between devices, round_y(): return lax.ppermute(x, 'gy', [(i, (i + d) % ny) for i in range(ny)])  8.58 us
    ppermute x6, starting transfers between devices, reduce_filter(): arrived.append(lax.ppermute(messages[m], ('gx', 'gy'), pairs))  8.54 us
    ppermute x4, waiting for transfers between devices, reduce_filter(): part = lax.ppermute(total, 'gx', pairs)  8.02 us
    ppermute x4, starting transfers between devices, reduce_filter(): part = lax.ppermute(total, 'gx', pairs)  6.76 us
    unnamed x42, local copies, waits for them, and re-layouts  6.47 us
    ppermute x5, waiting for transfers between devices, round_y(): return lax.ppermute(x, 'gy', [(i, (i + d) % ny) for i in range(ny)])  5.98 us
    ppermute x2, waiting for transfers between devices, reduce_filter(): beside = lax.ppermute(total, 'gx', [(g, g ^ 2) for g in range(nx)])  4.99 us
  transfers between devices with their start and end apart: 27, of which 10 were waited for; matrix products, arithmetic and copies ran while one was open for 6% of the time, Pallas kernels for 17%

profile of v1, /device:TPU:0, one launch (start us, length us, event | category | flops | bytes accessed | tf_op | source)
XLA Modules:
  0.0 111.8 jit_solution(9128282135079723593)
XLA Ops:
  1.5 2.3 %collective-permute-start.8 = (bf16[2,96,128]{2,1,0:T(8,128)(2,1)S(1)}, bf16[2,96,128]{2,1,0:T(8,128)(2,1)S(1)}, u32[]{:S(2)}, u32[]{:S(2)}) collective-permute-start(bf16[2,96,128]{2,1,0:T(8,128)(2,1)S(1)} %get-tuple-element.52), channel_id=1, source_target_pairs={{0,2},{2,4},{4,6},{6,8},{8,10},{10,12},{12,14},{14,16},{16,18},{18... | collective-permute-start | bytes 147464 | tf_op jit(solution)/shard_map/ppermute | solution.py:306
  6.4 2.4 %collective-permute-start.3 = (bf16[9,64,256]{2,1,0:T(8,128)(2,1)S(1)}, bf16[9,64,256]{2,1,0:T(8,128)(2,1)S(1)}, u32[]{:S(2)}, u32[]{:S(2)}) collective-permute-start(bf16[9,64,256]{2,1,0:T(8,128)(2,1)S(1)} %constant_dynamic-slice_fusion.4), channel_id=1, source_target_pairs={{0,1},{1,0},{2,3},{3,2},{4,5},{5,4},{6,7},{7,6},{8,9},{9,8},{10,11... | collective-permute-start | bytes 884744 | tf_op jit(solution)/shard_map/ppermute | solution.py:281
  9.6 1.3 %collective-permute-start.1 = (bf16[4,48,256]{2,1,0:T(8,128)(2,1)S(1)}, bf16[4,48,256]{2,1,0:T(8,128)(2,1)S(1)}, u32[]{:S(2)}, u32[]{:S(2)}) collective-permute-start(bf16[4,48,256]{2,1,0:T(8,128)(2,1)S(1)} %get-tuple-element.56), channel_id=1, source_target_pairs={{2,0},{4,2},{6,4},{8,6},{10,8},{12,10},{14,12},{16,14},{18,16},{20... | collective-permute-start | bytes 294920 | tf_op jit(solution)/shard_map/ppermute | solution.py:296
  11.0 4.7 %collective-permute-start = (bf16[4,48,256]{2,1,0:T(8,128)(2,1)S(1)}, bf16[4,48,256]{2,1,0:T(8,128)(2,1)S(1)}, u32[]{:S(2)}, u32[]{:S(2)}) collective-permute-start(bf16[4,48,256]{2,1,0:T(8,128)(2,1)S(1)} %get-tuple-element.57), channel_id=1, source_target_pairs={{0,2},{2,4},{4,6},{6,8},{8,10},{10,12},{12,14},{14,16},{16,18},{18... | collective-permute-start | bytes 294920 | tf_op jit(solution)/shard_map/ppermute | solution.py:295
  15.8 3.0 %collective-permute-start.4 = (bf16[1,9,64,256]{3,2,1,0:T(8,128)(2,1)S(1)}, bf16[1,9,64,256]{3,2,1,0:T(8,128)(2,1)S(1)}, u32[]{:S(2)}, u32[]{:S(2)}) collective-permute-start(bf16[1,9,64,256]{3,2,1,0:T(8,128)(2,1)S(1)} %bitcast.41), channel_id=1, source_target_pairs={{0,2},{2,0},{4,6},{6,4},{8,10},{10,8},{12,14},{14,12},{16,18},{18,... | collective-permute-start | bytes 884744 | tf_op jit(solution)/shard_map/ppermute | solution.py:287
  19.6 1.5 %collective-permute-start.10 = (bf16[20,64,128]{2,1,0:T(8,128)(2,1)S(1)}, bf16[20,64,128]{2,1,0:T(8,128)(2,1)S(1)}, u32[]{:S(2)}, u32[]{:S(2)}) collective-permute-start(bf16[20,64,128]{2,1,0:T(8,128)(2,1)S(1)} %get-tuple-element.50), channel_id=1, source_target_pairs={{0,1},{1,0},{2,3},{3,2},{4,5},{5,4},{6,7},{7,6},{8,9},{9,8},{10,11... | collective-permute-start | bytes 983048 | tf_op jit(solution)/shard_map/ppermute | solution.py:281
  21.1 1.8 %collective-permute-start.6 = (bf16[1,9,64,256]{3,2,1,0:T(8,128)(2,1)S(1)}, bf16[1,9,64,256]{3,2,1,0:T(8,128)(2,1)S(1)}, u32[]{:S(2)}, u32[]{:S(2)}) collective-permute-start(bf16[1,9,64,256]{3,2,1,0:T(8,128)(2,1)S(1)} %bitcast.44), channel_id=1, source_target_pairs={{0,2},{2,0},{4,6},{6,4},{8,10},{10,8},{12,14},{14,12},{16,18},{18,... | collective-permute-start | bytes 884744 | tf_op jit(solution)/shard_map/ppermute | solution.py:287
  23.0 2.5 %collective-permute-start.2 = (bf16[24,8,256]{2,1,0:T(8,128)(2,1)S(1)}, bf16[24,8,256]{2,1,0:T(8,128)(2,1)S(1)}, u32[]{:S(2)}, u32[]{:S(2)}) collective-permute-start(bf16[24,8,256]{2,1,0:T(8,128)(2,1)S(1)} %fusion.6), channel_id=1, source_target_pairs={{0,1},{1,0},{2,3},{3,2},{4,5},{5,4},{6,7},{7,6},{8,9},{9,8},{10,11... | collective-permute-start | bytes 294920 | tf_op jit(solution)/shard_map/ppermute | solution.py:281
  26.1 6.0 %collective-permute-done.2.up.down = bf16[24,8,256]{2,1,0:T(8,128)(2,1)S(1)} collective-permute-done((bf16[24,8,256]{2,1,0:T(8,128)(2,1)S(1)}, bf16[24,8,256]{2,1,0:T(8,128)(2,1)S(1)}, u32[]{:S(2)}, u32[]{:S(2)}) %collective-permute-start.2) | collective-permute-done | bytes 98336 | tf_op jit(solution)/shard_map/ppermute | solution.py:281
  33.5 5.5 %shard_map.75 = (bf16[22,64,256]{2,1,0:T(8,128)(2,1)}, f32[18,64,256]{2,1,0:T(8,128)}, bf16[24,64,256]{2,1,0:T(8,128)(2,1)}) custom-call(s32[2]{0:T(128)} %pad_add_fusion.where, bf16[16,48,256]{2,1,0:T(8,128)(2,1)} %bitcast.24, bf16[4,48,256]{2,1,0:T(8,128)(2,1)} %copy-done.12, bf16[4,48,256]{2,1,0:T(8,128)(2,1)} %copy-done.11, ...), custom_call_target="tpu_custom_call" | custom-call | flops 1660944384 | bytes 4653056 | tf_op jit(solution)/shard_map/pallas_call | solution.py:22
  39.6 4.9 %shard_map.76 = (bf16[16,48,256]{2,1,0:T(8,128)(2,1)}, f32[20,64,256]{2,1,0:T(8,128)}) custom-call(s32[2]{0:T(128)} %pad_add_fusion.where, bf16[22,64,256]{2,1,0:T(8,128)(2,1)} %get-tuple-element.23.hidden, bf16[9,128,256]{2,1,0:T(8,128)(2,1)} %bitcast.29, bf16[1,9,64,256]{3,2,1,0:T(8,128)(2,1)} %bitcast.45, bf16[1,9,64,256]{3,2,1,0:T(8,128)(2,1)} %copy-done.18), custom_call_target="tpu_custom_call" | custom-call | flops 1509949440 | bytes 3604480 | tf_op jit(solution)/shard_map/pallas_call | solution.py:22
  45.2 5.1 %shard_map.77 = (bf16[20,64,256]{2,1,0:T(8,128)(2,1)}, f32[9,256,128]{2,1,0:T(8,128)}, bf16[9,256,128]{2,1,0:T(8,128)(2,1)}) custom-call(s32[2]{0:T(128)} %pad_add_fusion.where, bf16[22,64,256]{2,1,0:T(8,128)(2,1)} %get-tuple-element.23.hidden, f32[20,64,256]{2,1,0:T(8,128)} %get-tuple-element.25.slope, bf16[20,64,128]{2,1,0:T(8,128)(2,1)} %get-tuple-element.51.refs_0_, ...), custom_call_target="tpu_custom_call" | custom-call | flops 1207959552 | bytes 5111808 | tf_op jit(solution)/shard_map/pallas_call | solution.py:22
  50.3 6.9 %shard_map.78 = (bf16[18,64,256]{2,1,0:T(8,128)(2,1)}, f32[9,256,128]{2,1,0:T(8,128)}, bf16[9,256,128]{2,1,0:T(8,128)(2,1)}) custom-call(s32[2]{0:T(128)} %pad_add_fusion.where, bf16[20,64,256]{2,1,0:T(8,128)(2,1)} %get-tuple-element.26.outer, bf16[9,128,256]{2,1,0:T(8,128)(2,1)} %bitcast.30, bf16[1,9,64,256]{3,2,1,0:T(8,128)(2,1)} %bitcast.46, ...), custom_call_target="tpu_custom_call" | custom-call | flops 2566914048 | bytes 6160384 | tf_op jit(solution)/shard_map/pallas_call | solution.py:22
  57.7 1.7 %collective-permute-done.11.came = bf16[9,256,128]{2,1,0:T(8,128)(2,1)S(1)} collective-permute-done((bf16[9,256,128]{2,1,0:T(8,128)(2,1)}, bf16[9,256,128]{2,1,0:T(8,128)(2,1)S(1)}, u32[]{:S(2)}, u32[]{:S(2)}) %collective-permute-start.11) | collective-permute-done | bytes 589856 | tf_op jit(solution)/shard_map/ppermute | solution.py:230
  60.3 2.4 %shard_map.80 = (f32[9,64,128]{2,1,0:T(8,128)}, bf16[9,64,128]{2,1,0:T(8,128)(2,1)}, bf16[9,64,128]{2,1,0:T(8,128)(2,1)}, bf16[9,64,128]{2,1,0:T(8,128)(2,1)}) custom-call(s32[2]{0:T(128)} %pad_add_fusion.where, f32[9,256,128]{2,1,0:T(8,128)} %get-tuple-element.30.keep, bf16[9,256,128]{2,1,0:T(8,128)(2,1)} %copy-done.6), custom_call_target="tpu_custom_call" | custom-call | bytes 2506752 | tf_op jit(solution)/shard_map/pallas_call | solution.py:22
  62.6 3.5 %collective-permute-start.12 = (bf16[9,64,128]{2,1,0:T(8,128)(2,1)}, bf16[9,64,128]{2,1,0:T(8,128)(2,1)S(1)}, u32[]{:S(2)}, u32[]{:S(2)}) collective-permute-start(bf16[9,64,128]{2,1,0:T(8,128)(2,1)} %get-tuple-element.33), channel_id=1, source_target_pairs={{0,4},{1,5},{2,6},{3,7},{4,0},{5,1},{6,2},{7,3},{8,12},{9,13},{10,... | collective-permute-start | bytes 442376 | tf_op jit(solution)/shard_map/ppermute | solution.py:245
  66.1 1.5 %collective-permute-start.13 = (bf16[9,64,128]{2,1,0:T(8,128)(2,1)}, bf16[9,64,128]{2,1,0:T(8,128)(2,1)S(1)}, u32[]{:S(2)}, u32[]{:S(2)}) collective-permute-start(bf16[9,64,128]{2,1,0:T(8,128)(2,1)} %get-tuple-element.34), channel_id=1, source_target_pairs={{0,1},{1,0},{2,3},{3,2},{4,5},{5,4},{6,7},{7,6},{8,9},{9,8},{10,11... | collective-permute-start | bytes 442376 | tf_op jit(solution)/shard_map/ppermute | solution.py:245
  67.8 1.5 %collective-permute-start.7 = (bf16[16,48,128]{2,1,0:T(8,128)(2,1)S(1)}, bf16[16,48,128]{2,1,0:T(8,128)(2,1)S(1)}, u32[]{:S(2)}, u32[]{:S(2)}) collective-permute-start(bf16[16,48,128]{2,1,0:T(8,128)(2,1)S(1)} %get-tuple-element.54), channel_id=1, source_target_pairs={{0,1},{1,0},{2,3},{3,2},{4,5},{5,4},{6,7},{7,6},{8,9},{9,8},{10,11... | collective-permute-start | bytes 589832 | tf_op jit(solution)/shard_map/ppermute | solution.py:281
  69.3 3.6 %shard_map.79 = bf16[16,48,256]{2,1,0:T(8,128)(2,1)} custom-call(s32[2]{0:T(128)} %pad_add_fusion.where, bf16[18,64,256]{2,1,0:T(8,128)(2,1)} %get-tuple-element.29.inner, bf16[9,128,256]{2,1,0:T(8,128)(2,1)} %bitcast.27, bf16[1,9,64,256]{3,2,1,0:T(8,128)(2,1)} %bitcast.43, bf16[1,9,64,256]{3,2,1,0:T(8,128)(2,1)} %copy-done.16), custom_call_target="tpu_custom_call" | custom-call | flops 1207959552 | bytes 2162688 | tf_op jit(solution)/shard_map/pallas_call | solution.py:22
  72.9 1.9 %copy.15 = bf16[48,16,256]{2,1,0:T(8,128)(2,1)} copy(bf16[48,16,256]{2,0,1:T(8,128)(2,1)} %bitcast.40) | data formatting | bytes 786432
  75.7 2.4 %shard_map.81 = (f32[9,64,128]{2,1,0:T(8,128)}, bf16[9,64,128]{2,1,0:T(8,128)(2,1)}, bf16[9,64,128]{2,1,0:T(8,128)(2,1)}, bf16[9,64,128]{2,1,0:T(8,128)(2,1)}) custom-call(s32[2]{0:T(128)} %pad_add_fusion.where, f32[9,256,128]{2,1,0:T(8,128)} %get-tuple-element.36.keep, bf16[9,256,128]{2,1,0:T(8,128)(2,1)} %copy-done.5), custom_call_target="tpu_custom_call" | custom-call | bytes 2506752 | tf_op jit(solution)/shard_map/pallas_call | solution.py:22
  78.0 2.0 %collective-permute-start.20 = (bf16[9,64,128]{2,1,0:T(8,128)(2,1)}, bf16[9,64,128]{2,1,0:T(8,128)(2,1)S(1)}, u32[]{:S(2)}, u32[]{:S(2)}) collective-permute-start(bf16[9,64,128]{2,1,0:T(8,128)(2,1)} %get-tuple-element.39), channel_id=1, source_target_pairs={{0,4},{1,5},{2,6},{3,7},{4,0},{5,1},{6,2},{7,3},{8,12},{9,13},{10,... | collective-permute-start | bytes 442376 | tf_op jit(solution)/shard_map/ppermute | solution.py:245
  81.7 2.1 %collective-permute-start.15 = (bf16[9,64,128]{2,1,0:T(8,128)(2,1)S(1)}, bf16[9,64,128]{2,1,0:T(8,128)(2,1)S(1)}, u32[]{:S(2)}, u32[]{:S(2)}) collective-permute-start(bf16[9,64,128]{2,1,0:T(8,128)(2,1)S(1)} %add_convert_fusion.5), channel_id=1, source_target_pairs={{0,8},{2,18},{4,12},{6,22},{8,0},{10,26},{12,4},{14,30},{16,24},{1... | collective-permute-start | bytes 442376 | tf_op jit(solution)/shard_map/ppermute | solution.py:254
  84.2 3.8 %collective-permute-done.21 = bf16[9,64,128]{2,1,0:T(8,128)(2,1)S(1)} collective-permute-done((bf16[9,64,128]{2,1,0:T(8,128)(2,1)}, bf16[9,64,128]{2,1,0:T(8,128)(2,1)S(1)}, u32[]{:S(2)}, u32[]{:S(2)}) %collective-permute-start.21) | collective-permute-done | bytes 147488 | tf_op jit(solution)/shard_map/ppermute | solution.py:245
  89.1 1.6 %collective-permute-start.23 = (bf16[9,64,128]{2,1,0:T(8,128)(2,1)S(1)}, bf16[9,64,128]{2,1,0:T(8,128)(2,1)S(1)}, u32[]{:S(2)}, u32[]{:S(2)}) collective-permute-start(bf16[9,64,128]{2,1,0:T(8,128)(2,1)S(1)} %add_convert_fusion.2), channel_id=1, source_target_pairs={{0,8},{2,18},{4,12},{6,22},{8,0},{10,26},{12,4},{14,30},{16,24},{1... | collective-permute-start | bytes 442376 | tf_op jit(solution)/shard_map/ppermute | solution.py:254
  90.7 1.4 %collective-permute-start.16 = (bf16[9,64,128]{2,1,0:T(8,128)(2,1)S(1)}, bf16[9,64,128]{2,1,0:T(8,128)(2,1)S(1)}, u32[]{:S(2)}, u32[]{:S(2)}) collective-permute-start(bf16[9,64,128]{2,1,0:T(8,128)(2,1)S(1)} %add_convert_fusion.4), channel_id=1, source_target_pairs={{0,16},{2,10},{4,20},{6,14},{8,24},{10,2},{12,28},{14,6},{16,0},{1... | collective-permute-start | bytes 442376 | tf_op jit(solution)/shard_map/ppermute | solution.py:254
  92.2 3.1 %collective-permute-done.23 = bf16[9,64,128]{2,1,0:T(8,128)(2,1)S(1)} collective-permute-done((bf16[9,64,128]{2,1,0:T(8,128)(2,1)S(1)}, bf16[9,64,128]{2,1,0:T(8,128)(2,1)S(1)}, u32[]{:S(2)}, u32[]{:S(2)}) %collective-permute-start.23) | collective-permute-done | bytes 147488 | tf_op jit(solution)/shard_map/ppermute | solution.py:254
  95.3 1.6 %collective-permute-start.24 = (bf16[9,64,128]{2,1,0:T(8,128)(2,1)S(1)}, bf16[9,64,128]{2,1,0:T(8,128)(2,1)S(1)}, u32[]{:S(2)}, u32[]{:S(2)}) collective-permute-start(bf16[9,64,128]{2,1,0:T(8,128)(2,1)S(1)} %add_convert_fusion.1), channel_id=1, source_target_pairs={{0,16},{2,10},{4,20},{6,14},{8,24},{10,2},{12,28},{14,6},{16,0},{1... | collective-permute-start | bytes 442376 | tf_op jit(solution)/shard_map/ppermute | solution.py:254
  99.0 4.0 %collective-permute-done.24 = bf16[9,64,128]{2,1,0:T(8,128)(2,1)S(1)} collective-permute-done((bf16[9,64,128]{2,1,0:T(8,128)(2,1)S(1)}, bf16[9,64,128]{2,1,0:T(8,128)(2,1)S(1)}, u32[]{:S(2)}, u32[]{:S(2)}) %collective-permute-start.24) | collective-permute-done | bytes 147488 | tf_op jit(solution)/shard_map/ppermute | solution.py:254
  104.3 4.0 %collective-permute-done.25 = bf16[9,64,128]{2,1,0:T(8,128)(2,1)S(1)} collective-permute-done((bf16[9,64,128]{2,1,0:T(8,128)(2,1)S(1)}, bf16[9,64,128]{2,1,0:T(8,128)(2,1)S(1)}, u32[]{:S(2)}, u32[]{:S(2)}) %collective-permute-start.25) | collective-permute-done | bytes 147488 | tf_op jit(solution)/shard_map/ppermute | solution.py:256
  108.6 1.3 %collective-permute-done.26 = bf16[9,128,128]{2,1,0:T(8,128)(2,1)S(1)} collective-permute-done((bf16[9,128,128]{2,1,0:T(8,128)(2,1)S(1)}, bf16[9,128,128]{2,1,0:T(8,128)(2,1)S(1)}, u32[]{:S(2)}, u32[]{:S(2)}) %collective-permute-start.26) | collective-permute-done | bytes 294944 | tf_op jit(solution)/shard_map/ppermute | solution.py:261
  110.1 1.7 %multiply_bitcast_fusion = (f32[128,3,3,256]{3,0,2,1:T(8,128)}, f32[128,3,3,256]{3,0,2,1:T(8,128)}) fusion(bf16[3,3,128,128]{3,2,1,0:T(8,128)(2,1)S(1)} %bitcast.32, bf16[3,3,128,128]{3,2,1,0:T(8,128)(2,1)S(1)} %bitcast.31, bf16[3,3,128,128]{3,2,1,0:T(8,128)(2,1)S(1)} %bitcast.34, bf16[3,3,128,128]{3,2,1,0:T(8,128)(2,1)S(1)} %bitcast.33), kind=kLoop, calls=%fused_computation.2 | loop fusion | flops 3538944 | bytes 3538944 | tf_op jit(solution)/shard_map/transpose | solution.py:376
  (97 shorter events, 17.7 us)
Async XLA Ops:
  1.5 9.4 %collective-permute-start.8 = (bf16[2,96,128]{2,1,0:T(8,128)(2,1)S(1)}, bf16[2,96,128]{2,1,0:T(8,128)(2,1)S(1)}, u32[]{:S(2)}, u32[]{:S(2)}) collective-permute-start(bf16[2,96,128]{2,1,0:T(8,128)(2,1)S(1)} %get-tuple-element.52), channel_id=1, source_target_pairs={{0,2},{2,4},{4,6},{6,8},{8,10},{10,12},{12,14},{14,16},{16,18},{18... | collective-permute-start | bytes 147464 | tf_op jit(solution)/shard_map/ppermute | solution.py:306
  3.9 11.8 %collective-permute-start.9 = (bf16[2,96,128]{2,1,0:T(8,128)(2,1)S(1)}, bf16[2,96,128]{2,1,0:T(8,128)(2,1)S(1)}, u32[]{:S(2)}, u32[]{:S(2)}) collective-permute-start(bf16[2,96,128]{2,1,0:T(8,128)(2,1)S(1)} %get-tuple-element.53), channel_id=1, source_target_pairs={{2,0},{4,2},{6,4},{8,6},{10,8},{12,10},{14,12},{16,14},{18,16},{20... | collective-permute-start | bytes 147464 | tf_op jit(solution)/shard_map/ppermute | solution.py:306
  6.4 9.4 %collective-permute-start.3 = (bf16[9,64,256]{2,1,0:T(8,128)(2,1)S(1)}, bf16[9,64,256]{2,1,0:T(8,128)(2,1)S(1)}, u32[]{:S(2)}, u32[]{:S(2)}) collective-permute-start(bf16[9,64,256]{2,1,0:T(8,128)(2,1)S(1)} %constant_dynamic-slice_fusion.4), channel_id=1, source_target_pairs={{0,1},{1,0},{2,3},{3,2},{4,5},{5,4},{6,7},{7,6},{8,9},{9,8},{10,11... | collective-permute-start | bytes 884744 | tf_op jit(solution)/shard_map/ppermute | solution.py:281
  8.9 12.2 %collective-permute-start.5 = (bf16[9,64,256]{2,1,0:T(8,128)(2,1)S(1)}, bf16[9,64,256]{2,1,0:T(8,128)(2,1)S(1)}, u32[]{:S(2)}, u32[]{:S(2)}) collective-permute-start(bf16[9,64,256]{2,1,0:T(8,128)(2,1)S(1)} %constant_dynamic-slice_fusion.3), channel_id=1, source_target_pairs={{0,1},{1,0},{2,3},{3,2},{4,5},{5,4},{6,7},{7,6},{8,9},{9,8},{10,11... | collective-permute-start | bytes 884744 | tf_op jit(solution)/shard_map/ppermute | solution.py:281
  9.6 13.3 %copy-start = (bf16[48,16,256]{2,0,1:T(8,128)(2,1)}, bf16[48,16,256]{2,0,1:T(8,128)(2,1)S(1)}, u32[]{:S(2)}) copy-start(bf16[48,16,256]{2,0,1:T(8,128)(2,1)S(1)} %copy.21) | copy-start | bytes 1179652
  9.6 13.3 %collective-permute-start.1 = (bf16[4,48,256]{2,1,0:T(8,128)(2,1)S(1)}, bf16[4,48,256]{2,1,0:T(8,128)(2,1)S(1)}, u32[]{:S(2)}, u32[]{:S(2)}) collective-permute-start(bf16[4,48,256]{2,1,0:T(8,128)(2,1)S(1)} %get-tuple-element.56), channel_id=1, source_target_pairs={{2,0},{4,2},{6,4},{8,6},{10,8},{12,10},{14,12},{16,14},{18,16},{20... | collective-permute-start | bytes 294920 | tf_op jit(solution)/shard_map/ppermute | solution.py:296
  11.0 11.9 %collective-permute-start = (bf16[4,48,256]{2,1,0:T(8,128)(2,1)S(1)}, bf16[4,48,256]{2,1,0:T(8,128)(2,1)S(1)}, u32[]{:S(2)}, u32[]{:S(2)}) collective-permute-start(bf16[4,48,256]{2,1,0:T(8,128)(2,1)S(1)} %get-tuple-element.57), channel_id=1, source_target_pairs={{0,2},{2,4},{4,6},{6,8},{8,10},{10,12},{12,14},{14,16},{16,18},{18... | collective-permute-start | bytes 294920 | tf_op jit(solution)/shard_map/ppermute | solution.py:295
  15.7 16.4 %copy-start.15 = (bf16[9,64,256]{2,1,0:T(8,128)(2,1)}, bf16[9,64,256]{2,1,0:T(8,128)(2,1)S(1)}, u32[]{:S(2)}) copy-start(bf16[9,64,256]{2,1,0:T(8,128)(2,1)S(1)} %collective-permute-done.3) | copy-start | bytes 884740
  15.8 16.4 %collective-permute-start.4 = (bf16[1,9,64,256]{3,2,1,0:T(8,128)(2,1)S(1)}, bf16[1,9,64,256]{3,2,1,0:T(8,128)(2,1)S(1)}, u32[]{:S(2)}, u32[]{:S(2)}) collective-permute-start(bf16[1,9,64,256]{3,2,1,0:T(8,128)(2,1)S(1)} %bitcast.41), channel_id=1, source_target_pairs={{0,2},{2,0},{4,6},{6,4},{8,10},{10,8},{12,14},{14,12},{16,18},{18,... | collective-permute-start | bytes 884744 | tf_op jit(solution)/shard_map/ppermute | solution.py:287
  19.6 24.9 %collective-permute-start.10 = (bf16[20,64,128]{2,1,0:T(8,128)(2,1)S(1)}, bf16[20,64,128]{2,1,0:T(8,128)(2,1)S(1)}, u32[]{:S(2)}, u32[]{:S(2)}) collective-permute-start(bf16[20,64,128]{2,1,0:T(8,128)(2,1)S(1)} %get-tuple-element.50), channel_id=1, source_target_pairs={{0,1},{1,0},{2,3},{3,2},{4,5},{5,4},{6,7},{7,6},{8,9},{9,8},{10,11... | collective-permute-start | bytes 983048 | tf_op jit(solution)/shard_map/ppermute | solution.py:281
  21.1 17.8 %copy-start.17 = (bf16[9,64,256]{2,1,0:T(8,128)(2,1)}, bf16[9,64,256]{2,1,0:T(8,128)(2,1)S(1)}, u32[]{:S(2)}) copy-start(bf16[9,64,256]{2,1,0:T(8,128)(2,1)S(1)} %collective-permute-done.5) | copy-start | bytes 884740
  21.1 17.8 %collective-permute-start.6 = (bf16[1,9,64,256]{3,2,1,0:T(8,128)(2,1)S(1)}, bf16[1,9,64,256]{3,2,1,0:T(8,128)(2,1)S(1)}, u32[]{:S(2)}, u32[]{:S(2)}) collective-permute-start(bf16[1,9,64,256]{3,2,1,0:T(8,128)(2,1)S(1)} %bitcast.44), channel_id=1, source_target_pairs={{0,2},{2,0},{4,6},{6,4},{8,10},{10,8},{12,14},{14,12},{16,18},{18,... | collective-permute-start | bytes 884744 | tf_op jit(solution)/shard_map/ppermute | solution.py:287
  22.9 9.2 %copy-start.11 = (bf16[4,48,256]{2,1,0:T(8,128)(2,1)}, bf16[4,48,256]{2,1,0:T(8,128)(2,1)S(1)}, u32[]{:S(2)}) copy-start(bf16[4,48,256]{2,1,0:T(8,128)(2,1)S(1)} %collective-permute-done.1.right) | copy-start | bytes 294916
  23.0 9.1 %collective-permute-start.2 = (bf16[24,8,256]{2,1,0:T(8,128)(2,1)S(1)}, bf16[24,8,256]{2,1,0:T(8,128)(2,1)S(1)}, u32[]{:S(2)}, u32[]{:S(2)}) collective-permute-start(bf16[24,8,256]{2,1,0:T(8,128)(2,1)S(1)} %fusion.6), channel_id=1, source_target_pairs={{0,1},{1,0},{2,3},{3,2},{4,5},{5,4},{6,7},{7,6},{8,9},{9,8},{10,11... | collective-permute-start | bytes 294920 | tf_op jit(solution)/shard_map/ppermute | solution.py:281
  57.2 10.5 %copy-start.9 = (bf16[16,48,256]{2,1,0:T(8,128)(2,1)S(1)}, bf16[16,48,256]{2,1,0:T(8,128)(2,1)}, u32[]{:S(2)}) copy-start(bf16[16,48,256]{2,1,0:T(8,128)(2,1)} %get-tuple-element.24) | copy-start | bytes 1179652
  57.2 2.2 %collective-permute-start.11 = (bf16[9,256,128]{2,1,0:T(8,128)(2,1)}, bf16[9,256,128]{2,1,0:T(8,128)(2,1)S(1)}, u32[]{:S(2)}, u32[]{:S(2)}) collective-permute-start(bf16[9,256,128]{2,1,0:T(8,128)(2,1)} %get-tuple-element.31), channel_id=1, source_target_pairs={{0,2},{2,0},{4,6},{6,4},{8,10},{10,8},{12,14},{14,12},{16,18},{18,... | collective-permute-start | bytes 1769480 | tf_op jit(solution)/shard_map/ppermute | solution.py:230
  57.2 17.6 %collective-permute-start.19 = (bf16[9,256,128]{2,1,0:T(8,128)(2,1)S(1)}, bf16[9,256,128]{2,1,0:T(8,128)(2,1)S(1)}, u32[]{:S(2)}, u32[]{:S(2)}) collective-permute-start(bf16[9,256,128]{2,1,0:T(8,128)(2,1)S(1)} %copy-done.13), channel_id=1, source_target_pairs={{0,2},{2,0},{4,6},{6,4},{8,10},{10,8},{12,14},{14,12},{16,18},{18,... | collective-permute-start | bytes 1769480 | tf_op jit(solution)/shard_map/ppermute | solution.py:230
  62.6 17.4 %collective-permute-start.12 = (bf16[9,64,128]{2,1,0:T(8,128)(2,1)}, bf16[9,64,128]{2,1,0:T(8,128)(2,1)S(1)}, u32[]{:S(2)}, u32[]{:S(2)}) collective-permute-start(bf16[9,64,128]{2,1,0:T(8,128)(2,1)} %get-tuple-element.33), channel_id=1, source_target_pairs={{0,4},{1,5},{2,6},{3,7},{4,0},{5,1},{6,2},{7,3},{8,12},{9,13},{10,... | collective-permute-start | bytes 442376 | tf_op jit(solution)/shard_map/ppermute | solution.py:245
  66.1 14.5 %collective-permute-start.13 = (bf16[9,64,128]{2,1,0:T(8,128)(2,1)}, bf16[9,64,128]{2,1,0:T(8,128)(2,1)S(1)}, u32[]{:S(2)}, u32[]{:S(2)}) collective-permute-start(bf16[9,64,128]{2,1,0:T(8,128)(2,1)} %get-tuple-element.34), channel_id=1, source_target_pairs={{0,1},{1,0},{2,3},{3,2},{4,5},{5,4},{6,7},{7,6},{8,9},{9,8},{10,11... | collective-permute-start | bytes 442376 | tf_op jit(solution)/shard_map/ppermute | solution.py:245
  67.6 14.0 %collective-permute-start.14 = (bf16[9,64,128]{2,1,0:T(8,128)(2,1)}, bf16[9,64,128]{2,1,0:T(8,128)(2,1)S(1)}, u32[]{:S(2)}, u32[]{:S(2)}) collective-permute-start(bf16[9,64,128]{2,1,0:T(8,128)(2,1)} %get-tuple-element.35), channel_id=1, source_target_pairs={{0,5},{1,4},{2,7},{3,6},{4,1},{5,0},{6,3},{7,2},{8,13},{9,12},{10,... | collective-permute-start | bytes 442376 | tf_op jit(solution)/shard_map/ppermute | solution.py:245
  67.8 40.6 %collective-permute-start.7 = (bf16[16,48,128]{2,1,0:T(8,128)(2,1)S(1)}, bf16[16,48,128]{2,1,0:T(8,128)(2,1)S(1)}, u32[]{:S(2)}, u32[]{:S(2)}) collective-permute-start(bf16[16,48,128]{2,1,0:T(8,128)(2,1)S(1)} %get-tuple-element.54), channel_id=1, source_target_pairs={{0,1},{1,0},{2,3},{3,2},{4,5},{5,4},{6,7},{7,6},{8,9},{9,8},{10,11... | collective-permute-start | bytes 589832 | tf_op jit(solution)/shard_map/ppermute | solution.py:281
  78.0 6.2 %collective-permute-start.20 = (bf16[9,64,128]{2,1,0:T(8,128)(2,1)}, bf16[9,64,128]{2,1,0:T(8,128)(2,1)S(1)}, u32[]{:S(2)}, u32[]{:S(2)}) collective-permute-start(bf16[9,64,128]{2,1,0:T(8,128)(2,1)} %get-tuple-element.39), channel_id=1, source_target_pairs={{0,4},{1,5},{2,6},{3,7},{4,0},{5,1},{6,2},{7,3},{8,12},{9,13},{10,... | collective-permute-start | bytes 442376 | tf_op jit(solution)/shard_map/ppermute | solution.py:245
  80.1 8.0 %collective-permute-start.21 = (bf16[9,64,128]{2,1,0:T(8,128)(2,1)}, bf16[9,64,128]{2,1,0:T(8,128)(2,1)S(1)}, u32[]{:S(2)}, u32[]{:S(2)}) collective-permute-start(bf16[9,64,128]{2,1,0:T(8,128)(2,1)} %get-tuple-element.40), channel_id=1, source_target_pairs={{0,1},{1,0},{2,3},{3,2},{4,5},{5,4},{6,7},{7,6},{8,9},{9,8},{10,11... | collective-permute-start | bytes 442376 | tf_op jit(solution)/shard_map/ppermute | solution.py:245
  80.6 7.4 %collective-permute-start.22 = (bf16[9,64,128]{2,1,0:T(8,128)(2,1)}, bf16[9,64,128]{2,1,0:T(8,128)(2,1)S(1)}, u32[]{:S(2)}, u32[]{:S(2)}) collective-permute-start(bf16[9,64,128]{2,1,0:T(8,128)(2,1)} %get-tuple-element.41), channel_id=1, source_target_pairs={{0,5},{1,4},{2,7},{3,6},{4,1},{5,0},{6,3},{7,2},{8,13},{9,12},{10,... | collective-permute-start | bytes 442376 | tf_op jit(solution)/shard_map/ppermute | solution.py:245
  81.7 9.0 %collective-permute-start.15 = (bf16[9,64,128]{2,1,0:T(8,128)(2,1)S(1)}, bf16[9,64,128]{2,1,0:T(8,128)(2,1)S(1)}, u32[]{:S(2)}, u32[]{:S(2)}) collective-permute-start(bf16[9,64,128]{2,1,0:T(8,128)(2,1)S(1)} %add_convert_fusion.5), channel_id=1, source_target_pairs={{0,8},{2,18},{4,12},{6,22},{8,0},{10,26},{12,4},{14,30},{16,24},{1... | collective-permute-start | bytes 442376 | tf_op jit(solution)/shard_map/ppermute | solution.py:254
  89.1 6.2 %collective-permute-start.23 = (bf16[9,64,128]{2,1,0:T(8,128)(2,1)S(1)}, bf16[9,64,128]{2,1,0:T(8,128)(2,1)S(1)}, u32[]{:S(2)}, u32[]{:S(2)}) collective-permute-start(bf16[9,64,128]{2,1,0:T(8,128)(2,1)S(1)} %add_convert_fusion.2), channel_id=1, source_target_pairs={{0,8},{2,18},{4,12},{6,22},{8,0},{10,26},{12,4},{14,30},{16,24},{1... | collective-permute-start | bytes 442376 | tf_op jit(solution)/shard_map/ppermute | solution.py:254
  90.7 7.1 %collective-permute-start.16 = (bf16[9,64,128]{2,1,0:T(8,128)(2,1)S(1)}, bf16[9,64,128]{2,1,0:T(8,128)(2,1)S(1)}, u32[]{:S(2)}, u32[]{:S(2)}) collective-permute-start(bf16[9,64,128]{2,1,0:T(8,128)(2,1)S(1)} %add_convert_fusion.4), channel_id=1, source_target_pairs={{0,16},{2,10},{4,20},{6,14},{8,24},{10,2},{12,28},{14,6},{16,0},{1... | collective-permute-start | bytes 442376 | tf_op jit(solution)/shard_map/ppermute | solution.py:254
  95.3 7.7 %collective-permute-start.24 = (bf16[9,64,128]{2,1,0:T(8,128)(2,1)S(1)}, bf16[9,64,128]{2,1,0:T(8,128)(2,1)S(1)}, u32[]{:S(2)}, u32[]{:S(2)}) collective-permute-start(bf16[9,64,128]{2,1,0:T(8,128)(2,1)S(1)} %add_convert_fusion.1), channel_id=1, source_target_pairs={{0,16},{2,10},{4,20},{6,14},{8,24},{10,2},{12,28},{14,6},{16,0},{1... | collective-permute-start | bytes 442376 | tf_op jit(solution)/shard_map/ppermute | solution.py:254
  97.9 6.2 %collective-permute-start.17 = (bf16[9,64,128]{2,1,0:T(8,128)(2,1)S(1)}, bf16[9,64,128]{2,1,0:T(8,128)(2,1)S(1)}, u32[]{:S(2)}, u32[]{:S(2)}) collective-permute-start(bf16[9,64,128]{2,1,0:T(8,128)(2,1)S(1)} %add_convert_fusion.3), channel_id=1, source_target_pairs={{0,4},{2,6},{4,0},{6,2},{8,12},{10,14},{12,8},{14,10},{16,20},{18,... | collective-permute-start | bytes 442376 | tf_op jit(solution)/shard_map/ppermute | solution.py:256
  103.0 5.2 %collective-permute-start.25 = (bf16[9,64,128]{2,1,0:T(8,128)(2,1)S(1)}, bf16[9,64,128]{2,1,0:T(8,128)(2,1)S(1)}, u32[]{:S(2)}, u32[]{:S(2)}) collective-permute-start(bf16[9,64,128]{2,1,0:T(8,128)(2,1)S(1)} %add_convert_fusion), channel_id=1, source_target_pairs={{0,4},{2,6},{4,0},{6,2},{8,12},{10,14},{12,8},{14,10},{16,20},{18,... | collective-permute-start | bytes 442376 | tf_op jit(solution)/shard_map/ppermute | solution.py:256
  104.2 4.3 %collective-permute-start.18 = (bf16[9,128,128]{2,1,0:T(8,128)(2,1)S(1)}, bf16[9,128,128]{2,1,0:T(8,128)(2,1)S(1)}, u32[]{:S(2)}, u32[]{:S(2)}) collective-permute-start(bf16[9,128,128]{2,1,0:T(8,128)(2,1)S(1)} %pad_maximum_fusion.2), channel_id=1, source_target_pairs={{0,2},{2,0},{4,6},{6,4},{8,10},{10,8},{12,14},{14,12},{16,18},{18,... | collective-permute-start | bytes 884744 | tf_op jit(solution)/shard_map/ppermute | solution.py:261
  108.3 1.6 %collective-permute-start.26 = (bf16[9,128,128]{2,1,0:T(8,128)(2,1)S(1)}, bf16[9,128,128]{2,1,0:T(8,128)(2,1)S(1)}, u32[]{:S(2)}, u32[]{:S(2)}) collective-permute-start(bf16[9,128,128]{2,1,0:T(8,128)(2,1)S(1)} %pad_maximum_fusion.3), channel_id=1, source_target_pairs={{0,2},{2,0},{4,6},{6,4},{8,10},{10,8},{12,14},{14,12},{16,18},{18,... | collective-permute-start | bytes 884744 | tf_op jit(solution)/shard_map/ppermute | solution.py:261
  (15 other events, 58.4 us)

commit v2 on v1

--- a/solution.py
+++ b/solution.py
@@ -10,8 +10,10 @@
 
 F32, BF16 = jnp.float32, jnp.bfloat16
 OFF = 8
-VMEM_LIMIT = 56 * 1024 * 1024
+HALO = 4
+VMEM_LIMIT = 30 * 1024 * 1024
 NT = (((1,), (1,)), ((), ()))
+TN = (((0,), (0,)), ((), ()))
 
 
 def call(kernel, outs, args, scratch=(), flops=0, smem_args=1):
@@ -40,29 +42,20 @@
     return (at >= 0) & (at < total)
 
 
-def shifted_rows(x):
-    n = x.shape[0]
-    return pltpu.roll(x, 1, 0), x, pltpu.roll(x, n - 1, 0)
-
-
-def fill_shifted(buf, c, x):
-    ch = x.shape[1]
-    for i, part in enumerate(shifted_rows(x)):
-        buf[c, :, i * ch : (i + 1) * ch] = part.astype(BF16)
-
-
-def conv_chunk(buf, w, c0, n, backward):
-    rows, ch = buf.shape[1], w.shape[1]
-    total = None
-    for j in range(3):
-        for i in range(3):
-            lhs = buf[c0 + j : c0 + j + n, :, i * ch : (i + 1) * ch].reshape(n * rows, ch)
+def conv_chunk(x, w, c0, n, backward):
+    rows, ch = x.shape[1], x.shape[2]
+    sums = []
+    for i in range(3):
+        total = None
+        for j in range(3):
+            lhs = x[c0 + j : c0 + j + n].reshape(n * rows, ch)
             if backward:
-                term = jnp.dot(lhs, w[(2 - j) * 3 + (2 - i)], preferred_element_type=F32)
+                term = jnp.dot(lhs, w[(2 - i) * 3 + (2 - j)], preferred_element_type=F32)
             else:
-                term = lax.dot_general(lhs, w[j * 3 + i], NT, preferred_element_type=F32)
+                term = lax.dot_general(lhs, w[i * 3 + j], NT, preferred_element_type=F32)
             total = term if total is None else total + term
-    return total.reshape(n, rows, ch)
+        sums.append(total.reshape(n, rows, ch))
+    return [pltpu.roll(sums[0][q], 1, 0) + sums[1][q] + pltpu.roll(sums[2][q], rows - 1, 0) for q in range(n)]
 
 
 def chunks(total, most):
@@ -89,20 +82,27 @@
         w[:, pl.ds(at, half), :] = other[d - 1]
 
 
-def conv1_kernel(dims, where, ft, left, right, up, down, own, mine, other, hidden, slope, fbuf, w, buf):
+def conv1_kernel(dims, where, ft, left, right, up, down, own, mine, other, hidden, slope, fbuf, w):
     ny, hl, wl, height, width = dims
     iy, ix = where[0], where[1]
-    rows = fbuf.shape[1]
+    rows, ch = fbuf.shape[1], fbuf.shape[2]
     ok = row_mask(iy * hl, rows, height)
-    for c in range(wl + 8):
-        mid = left[c] if c < 4 else (ft[c - 4] if c < wl + 4 else right[c - wl - 4])
-        x = jnp.concatenate([up[c].astype(F32), mid.astype(F32), down[c].astype(F32)], axis=0)
-        x = jnp.where(ok, x, 0.0)
-        fbuf[c] = x.astype(BF16)
-        fill_shifted(buf, c, x)
+    groups = ch // 128
+    gap = jnp.zeros((rows - hl - OFF - HALO, ch), F32)
+    for c in range(wl + 2 * HALO):
+        if HALO <= c < wl + HALO:
+            mid = ft[c - HALO].astype(F32)
+        else:
+            ref, at = (left, c) if c < HALO else (right, c - wl - HALO)
+            mid = jnp.concatenate([ref[g * HALO + at].astype(F32) for g in range(groups)], axis=1)
+        r = (c % 2) * HALO
+        above = up[c // 2].astype(F32)[r : r + HALO]
+        below = down[c // 2].astype(F32)[r : r + HALO]
+        x = jnp.concatenate([gap[: OFF - HALO], above, mid, below, gap], axis=0)
+        fbuf[c] = jnp.where(ok, x, 0.0).astype(BF16)
     assemble_filter(w, own, (mine, other), iy, ix % 2, ny)
     for c0, n in chunks(wl + 6, 11):
-        pre = conv_chunk(buf, w, c0, n, False)
+        pre = conv_chunk(fbuf, w, c0, n, False)
         for q in range(n):
             c = c0 + q
             col = ix * wl + c - 3
@@ -113,16 +113,14 @@
                 slope[c - 2] = jnp.where(inside, grad, 0.0)
 
 
-def conv2_kernel(dims, where, hidden, own, mine, other, act_out, slope, w, buf):
+def conv2_kernel(dims, where, hidden, own, mine, other, act_out, slope, w):
     ny, hl, wl, height, width = dims
     iy, ix = where[0], where[1]
     rows = hidden.shape[1]
     ok = row_mask(iy * hl, rows, height)
-    for c in range(wl + 6):
-        fill_shifted(buf, c, hidden[c].astype(F32))
     assemble_filter(w, own, (mine, other), iy, ix % 2, ny)
     for c0, n in chunks(wl + 4, 10):
-        pre = conv_chunk(buf, w, c0, n, False)
+        pre = conv_chunk(hidden, w, c0, n, False)
         for q in range(n):
             c = c0 + q
             col = ix * wl + c - 2
@@ -138,71 +136,70 @@
     return (at >= OFF) & (at < OFF + hl)
 
 
-def filter_grad(where, buf, first, grad_t, wl, keep, send):
-    core = where[1] % 2
-    rows, ch = buf.shape[1], grad_t.shape[0]
+def put_shifted(shifted, c, grad, own):
+    rows, ch = grad.shape
+    grad = jnp.where(own, grad, 0.0)
+    for i in range(3):
+        part = grad if i == 1 else pltpu.roll(grad, (i - 1) % rows, 0)
+        shifted[c * rows : (c + 1) * rows, i * ch : (i + 1) * ch] = part.astype(BF16)
+
+
+def filter_grad(where, x, first, shifted, wl, keep, send):
+    low_core = where[1] % 2 == 0
+    rows, ch = x.shape[1], x.shape[2]
     half = ch // 2
     for j in range(3):
+        rhs = x[first + j : first + j + wl].reshape(wl * rows, ch)
+        g = lax.dot_general(shifted[...], rhs, TN, preferred_element_type=F32)
         for i in range(3):
-            rhs = buf[first + j : first + j + wl, :, i * ch : (i + 1) * ch].reshape(wl * rows, ch)
-            g = jnp.dot(grad_t, rhs, preferred_element_type=F32)
-            low, high = g[:, :half], g[:, half:]
-            keep[j * 3 + i] = jnp.where(core == 0, low, high)
-            send[j * 3 + i] = jnp.where(core == 0, high, low).astype(BF16)
+            low, high = g[i * ch : (i + 1) * ch, :half], g[i * ch : (i + 1) * ch, half:]
+            keep[i * 3 + j] = jnp.where(low_core, low, high)
+            send[i * 3 + j] = jnp.where(low_core, high, low).astype(BF16)
 
 
 def outer_kernel(dims, count, where, hidden, slope, *refs):
-    cots, (outer, keep, send, buf, gt) = refs[:count], refs[count:]
+    cots, (outer, keep, send, shifted) = refs[:count], refs[count:]
     ny, hl, wl, height, width = dims
     iy = where[0]
     rows = hidden.shape[1]
     own = own_rows(rows, hl)
-    for c in range(wl + 2):
-        fill_shifted(buf, c, hidden[c + 2].astype(F32))
     for c in range(wl + 4):
         parts = [ref[c].astype(F32) for ref in cots]
         if len(parts) == 2:
             a, b = parts
             parts = [jnp.where(iy == 0, a, b), jnp.where(iy == 0, b, a)]
-        outer[c] = (jnp.concatenate(parts, axis=1) * slope[c]).astype(BF16)
-    for c in range(wl):
-        val = jnp.where(own, outer[c + 2].astype(F32), 0.0)
-        gt[:, c * rows : (c + 1) * rows] = val.T.astype(BF16)
-    filter_grad(where, buf, 0, gt[...], wl, keep, send)
-
-
-def inner_kernel(dims, where, outer, own, mine, other, slope, fbuf, inner, keep, send, w, buf, gt):
+        val = (jnp.concatenate(parts, axis=1) * slope[c]).astype(BF16)
+        outer[c] = val
+        if 2 <= c < wl + 2:
+            put_shifted(shifted, c - 2, val.astype(F32), own)
+    filter_grad(where, hidden, 2, shifted, wl, keep, send)
+
+
+def inner_kernel(dims, where, outer, own, mine, other, slope, fbuf, inner, keep, send, w, shifted):
     ny, hl, wl, height, width = dims
     iy, ix = where[0], where[1]
     rows = fbuf.shape[1]
-    for c in range(wl + 4):
-        fill_shifted(buf, c, outer[c].astype(F32))
     assemble_filter(w, own, (mine, other), iy, ix % 2, ny)
     mine_rows = own_rows(rows, hl)
     for c0, n in chunks(wl + 2, 9):
-        grad = conv_chunk(buf, w, c0, n, True)
+        grad = conv_chunk(outer, w, c0, n, True)
         for q in range(n):
             c = c0 + q
-            val = grad[q] * slope[c]
-            inner[c] = val.astype(BF16)
+            val = (grad[q] * slope[c]).astype(BF16)
+            inner[c] = val
             if 1 <= c < wl + 1:
-                val = jnp.where(mine_rows, val, 0.0)
-                gt[:, (c - 1) * rows : c * rows] = val.T.astype(BF16)
-    for c in range(wl + 2):
-        fill_shifted(buf, c, fbuf[c + 3].astype(F32))
-    filter_grad(where, buf, 0, gt[...], wl, keep, send)
-
-
-def input_kernel(dims, where, inner, own, mine, other, out, w, buf):
+                put_shifted(shifted, c - 1, val.astype(F32), mine_rows)
+    filter_grad(where, fbuf, 3, shifted, wl, keep, send)
+
+
+def input_kernel(dims, where, inner, own, mine, other, out, w):
     ny, hl, wl, height, width = dims
     iy, ix = where[0], where[1]
-    for c in range(wl + 2):
-        fill_shifted(buf, c, inner[c].astype(F32))
     assemble_filter(w, own, (mine, other), iy, ix % 2, ny)
     for c0, n in chunks(wl, 8):
-        grad = conv_chunk(buf, w, c0, n, True)
+        grad = conv_chunk(inner, w, c0, n, True)
         for q in range(n):
-            out[c0 + q] = grad[q, OFF : OFF + hl].astype(BF16)
+            out[c0 + q] = grad[q][OFF : OFF + hl].astype(BF16)
 
 
 def split_kernel(blocks, where, keep, came, own, *messages):
@@ -286,31 +283,58 @@
         mine = jnp.stack([round_y(send, d) for d in range(1, ny)])
         return mine, lax.ppermute(mine, "gx", [(i, i ^ 1) for i in range(nx)])
 
-    first_own = jnp.transpose(first_filter, (2, 1, 0, 3)).reshape(9, co, ch)
-    second_own = jnp.transpose(second_filter, (2, 1, 0, 3)).reshape(9, co, ch)
-    first_in = gathered(first_own)
-    second_in = gathered(second_own)
+    def halves(taps):
+        return lax.dynamic_slice_in_dim(taps, core * (co // 2), co // 2, 1)
+
+    def spread(send):
+        mine = jnp.stack([round_y(send, d) for d in range(1, ny)])
+        return mine, lax.ppermute(mine, "gx", [(i, i ^ 1) for i in range(nx)])
+
+    first_own = jnp.transpose(first_filter, (1, 2, 0, 3)).reshape(9, co, ch)
+    second_own = jnp.transpose(second_filter, (1, 2, 0, 3)).reshape(9, co, ch)
+    first_send = halves(first_own)
+    first_send, features, cotangent = lax.optimization_barrier((first_send, features, cotangent))
+    first_in = spread(first_send)
 
     ft = jnp.transpose(features, (1, 0, 2))
-    left = lax.ppermute(ft[wl - 4 :], "gx", forward)
-    right = lax.ppermute(ft[:4], "gx", backward)
-    strip = jnp.concatenate([left, ft, right], axis=0)
+    ct = jnp.transpose(cotangent, (1, 2, 0))
+    groups = ch // 128
+
+    def edge(f, c):
+        planes = [f[:, :, g * 128 : (g + 1) * 128] for g in range(groups)]
+        return jnp.concatenate(planes + [c.reshape(2 * groups, hl, 128)], axis=0)
+
+    left = lax.ppermute(edge(ft[wl - HALO :], ct[wl - 2 :]), "gx", forward)
+    right = lax.ppermute(edge(ft[:HALO], ct[:2]), "gx", backward)
+
+    def edge_rows(h0):
+        def of(planes):
+            return jnp.concatenate([planes[g * HALO : (g + 1) * HALO, h0 : h0 + HALO] for g in range(groups)], axis=2)
+
+        strip = jnp.concatenate([of(left), ft[:, h0 : h0 + HALO], of(right)], axis=0)
+        return strip.reshape(wl // 2 + HALO, 2 * HALO, ch)
+
     if ny == 2:
-        up = down = round_y(jnp.where(iy == 0, strip[:, hl - OFF :], strip[:, :OFF]), 1)
+        row_send = jnp.where(iy == 0, edge_rows(hl - HALO), edge_rows(0))
+        second_own, row_send = lax.optimization_barrier((second_own, row_send))
+        up = down = round_y(row_send, 1)
     else:
-        up = round_y(strip[:, hl - OFF :], 1)
-        down = round_y(strip[:, :OFF], ny - 1)
-
-    ct = jnp.transpose(cotangent, (1, 2, 0))
+        up = round_y(edge_rows(hl - HALO), 1)
+        down = round_y(edge_rows(0), ny - 1)
+    second_in = spread(halves(second_own))
+
+    at = groups * HALO
     ct = jnp.concatenate(
-        [lax.ppermute(ct[wl - 2 :], "gx", forward), ct, lax.ppermute(ct[:2], "gx", backward)], axis=0
+        [left[at:].reshape(2, height, co), ct, right[at:].reshape(2, height, co)], axis=0
     )
     ct = jnp.pad(ct, ((0, 0), (OFF, rows - OFF - hl), (0, 0)))
 
     def rows_of(y):
         return lax.dynamic_slice_in_dim(ct, y * hl, rows, 1)
 
-    cots = [rows_of(iy)] + [round_y(rows_of((iy + d) % ny), d) for d in range(1, ny)]
+    cot_send = [rows_of((iy + d) % ny) for d in range(1, ny)]
+    (cot_send, first_in) = lax.optimization_barrier((cot_send, first_in))
+    cots = [rows_of(iy)] + [round_y(cot_send[d - 1], d) for d in range(1, ny)]
     if ny != 2:
         full = jnp.zeros((wl + 4, rows, ch), BF16)
         for d, part in enumerate(cots):
@@ -326,14 +350,14 @@
         functools.partial(conv1_kernel, dims),
         [((wl + 6, rows, ch), BF16), ((wl + 2, rows, ch), F32), fbuf_shape],
         (where, ft, left, right, up, down, first_own, *first_in),
-        [weights, bf(wl + 8, rows, 3 * ch)],
+        [weights],
         tap_flops * (wl + 6),
     )
     act, slope2 = call(
         functools.partial(conv2_kernel, dims),
         [((wl, hl, ch), BF16), ((wl + 4, rows, ch), F32)],
         (where, hidden, second_own, *second_in),
-        [weights, bf(wl + 6, rows, 3 * ch)],
+        [weights],
         tap_flops * (wl + 4),
     )
     grad_shapes = [((9, ch, ch // 2), F32), ((9, ch, ch // 2), BF16)]
@@ -341,21 +365,21 @@
         functools.partial(outer_kernel, dims, len(cots)),
         [((wl + 4, rows, ch), BF16)] + grad_shapes,
         (where, hidden, slope2, *cots),
-        [bf(wl + 2, rows, 3 * ch), bf(ch, wl * rows)],
+        [bf(wl * rows, 3 * ch)],
         tap_flops * wl,
     )
     inner, keep1, send1 = call(
         functools.partial(inner_kernel, dims),
         [((wl + 2, rows, ch), BF16)] + grad_shapes,
         (where, outer, second_own, *second_in, slope1, fbuf),
-        [weights, bf(wl + 4, rows, 3 * ch), bf(ch, wl * rows)],
+        [weights, bf(wl * rows, 3 * ch)],
         tap_flops * (2 * wl + 2),
     )
     (input_grad,) = call(
         functools.partial(input_kernel, dims),
         [((wl, hl, ch), BF16)],
         (where, inner, first_own, *first_in),
-        [weights, bf(wl + 2, rows, 3 * ch)],
+        [weights],
         tap_flops * wl,
     )
     input_grad = jnp.transpose(input_grad, (1, 0, 2))
@@ -373,7 +397,7 @@
     for keep, send in ((keep1, send1), (keep2, send2)):
         total = reduce_filter(where, keep, send, nx, ny, iy, ix)
         total = total.astype(F32) * scale_factor
-        grads.append(jnp.transpose(total.reshape(3, 3, co, ch), (2, 1, 0, 3)))
+        grads.append(jnp.transpose(total.reshape(3, 3, co, ch), (2, 0, 1, 3)))
     return output, input_grad, grads[0], grads[1]
 
 

time: 112 us -> 93 us (0.83)
  Pallas kernels: 30.6 us -> 16.3 us
  waiting for transfers between devices: 26.4 us -> 30.1 us
  local copies, waits for them, and re-layouts: 9.57 us -> 5.9 us
  starting transfers between devices: 40.1 us -> 36.9 us
  other arithmetic: 4.03 us -> 2.6 us
    pallas_call x7, Pallas kernels: 30.6 us -> 16.3 us  [call(): pl.pallas_call(kernel, out_shape=[jax.ShapeDtypeStruct(s, t) for s, t in...]
    ppermute x6 -> x4, starting transfers between devices: 14.4 us -> 10 us  [the longest x2 7.15 us: spread(): return (mine, lax.ppermute(mine, 'gx', [(i, i ^ 1) for i in range(nx)]))]
    unnamed x42 -> x31, local copies, waits for them, and re-layouts: 6.47 us -> 2.5 us
    ppermute x6 -> x4, waiting for transfers between devices: 0.02 us -> 3.45 us  [the longest x1 3.44 us: body(): right = lax.ppermute(edge(ft[:HALO], ct[:2]), 'gx', backward)]
    ppermute x5, waiting for transfers between devices: 5.98 us -> 3.57 us  [round_y(): return lax.ppermute(x, 'gy', [(i, (i + d) % ny) for i in range(ny)])]
    ppermute x6, waiting for transfers between devices: 4.29 us -> 6.64 us  [reduce_filter(): arrived.append(lax.ppermute(messages[m], ('gx', 'gy'), pairs))]
    ppermute x5, starting transfers between devices: 8.58 us -> 6.27 us  [round_y(): return lax.ppermute(x, 'gy', [(i, (i + d) % ny) for i in range(ny)])]
    ppermute x4, starting transfers between devices: 6.76 us -> 8.54 us  [reduce_filter(): part = lax.ppermute(total, 'gx', pairs)]
  transfers between devices with their start and end apart: 27 -> 25, of which waited for: 10 -> 10; matrix products, arithmetic and copies ran while one was open for 6% -> 4% of each run, Pallas kernels for 17% -> 10%
where the time goes in v2:
time: 93 us; the launch traced here: 92.8 us
  starting transfers between devices  36.9 us (40%)
  waiting for transfers between devices  30.1 us (32%)
  Pallas kernels  16.3 us (18%)
  local copies, waits for them, and re-layouts  5.9 us (6%)
  other arithmetic  2.6 us (3%)
  between operations  1.05 us (1%)
    pallas_call x7, Pallas kernels, call(): pl.pallas_call(kernel, out_shape=[jax.ShapeDtypeStruct(s, t) for s, t in...  16.3 us
    ppermute x4, waiting for transfers between devices, reduce_filter(): part = lax.ppermute(total, 'gx', pairs)  9.45 us
    ppermute x6, starting transfers between devices, reduce_filter(): arrived.append(lax.ppermute(messages[m], ('gx', 'gy'), pairs))  8.57 us
    ppermute x4, starting transfers between devices, reduce_filter(): part = lax.ppermute(total, 'gx', pairs)  8.54 us
    ppermute x2, starting transfers between devices, spread(): return (mine, lax.ppermute(mine, 'gx', [(i, i ^ 1) for i in range(nx)]))  7.15 us
    ppermute x6, waiting for transfers between devices, reduce_filter(): arrived.append(lax.ppermute(messages[m], ('gx', 'gy'), pairs))  6.64 us
    ppermute x5, starting transfers between devices, round_y(): return lax.ppermute(x, 'gy', [(i, (i + d) % ny) for i in range(ny)])  6.27 us
    ppermute x2, waiting for transfers between devices, reduce_filter(): beside = lax.ppermute(total, 'gx', [(g, g ^ 2) for g in range(nx)])  3.89 us
  transfers between devices with their start and end apart: 25, of which 10 were waited for; matrix products, arithmetic and copies ran while one was open for 4% of the time, Pallas kernels for 10%

profile of v2, /device:TPU:0, one launch (start us, length us, event | category | flops | bytes accessed | tf_op | source)
XLA Modules:
  0.0 92.8 jit_solution(33719944989828509)
XLA Ops:
  0.6 1.0 %constant_dynamic-slice_fusion.4 = bf16[9,64,256]{2,1,0:T(8,128)(2,1)S(1)} fusion(bf16[9,128,256]{2,1,0:T(8,128)(2,1)} %bitcast.35, s32[]{:T(128)S(6)} %select_n.110), kind=kLoop, calls=%fused_computation.36 | loop fusion | bytes 589828 | tf_op jit(solution)/shard_map/dynamic_slice | solution.py:287
  1.6 3.0 %collective-permute-start.3 = (bf16[9,64,256]{2,1,0:T(8,128)(2,1)S(1)}, bf16[9,64,256]{2,1,0:T(8,128)(2,1)S(1)}, u32[]{:S(2)}, u32[]{:S(2)}) collective-permute-start(bf16[9,64,256]{2,1,0:T(8,128)(2,1)S(1)} %constant_dynamic-slice_fusion.4), channel_id=1, source_target_pairs={{0,1},{1,0},{2,3},{3,2},{4,5},{5,4},{6,7},{7,6},{8,9},{9,8},{10,11... | collective-permute-start | bytes 884744 | tf_op jit(solution)/shard_map/ppermute | solution.py:278
  5.6 1.1 %copy.11 = bf16[48,16,256]{2,0,1:T(8,128)(2,1)S(1)} copy(bf16[48,16,256]{2,1,0:T(8,128)(2,1)} %param.4) | data formatting | bytes 786432 | tf_op jit(solution)/shard_map/optimization_barrier | solution.py:296
  6.8 1.6 %collective-permute-start = (bf16[12,48,128]{2,1,0:T(8,128)(2,1)S(1)}, bf16[12,48,128]{2,1,0:T(8,128)(2,1)S(1)}, u32[]{:S(2)}, u32[]{:S(2)}) collective-permute-start(bf16[12,48,128]{2,1,0:T(8,128)(2,1)S(1)} %pad_maximum_fusion.2), channel_id=1, source_target_pairs={{0,2},{2,4},{4,6},{6,8},{8,10},{10,12},{12,14},{14,16},{16,18},{18... | collective-permute-start | bytes 442376 | tf_op jit(solution)/shard_map/ppermute | solution.py:307
  8.4 1.3 %collective-permute-start.1 = (bf16[12,48,128]{2,1,0:T(8,128)(2,1)S(1)}, bf16[12,48,128]{2,1,0:T(8,128)(2,1)S(1)}, u32[]{:S(2)}, u32[]{:S(2)}) collective-permute-start(bf16[12,48,128]{2,1,0:T(8,128)(2,1)S(1)} %pad_maximum_fusion.3), channel_id=1, source_target_pairs={{2,0},{4,2},{6,4},{8,6},{10,8},{12,10},{14,12},{16,14},{18,16},{20... | collective-permute-start | bytes 442376 | tf_op jit(solution)/shard_map/ppermute | solution.py:308
  9.8 3.4 %collective-permute-done.1.right = bf16[12,48,128]{2,1,0:T(8,128)(2,1)S(1)} collective-permute-done((bf16[12,48,128]{2,1,0:T(8,128)(2,1)S(1)}, bf16[12,48,128]{2,1,0:T(8,128)(2,1)S(1)}, u32[]{:S(2)}, u32[]{:S(2)}) %collective-permute-start.1) | collective-permute-done | bytes 147488 | tf_op jit(solution)/shard_map/ppermute | solution.py:308
  13.9 3.7 %collective-permute-start.4 = (bf16[1,9,64,256]{3,2,1,0:T(8,128)(2,1)S(1)}, bf16[1,9,64,256]{3,2,1,0:T(8,128)(2,1)S(1)}, u32[]{:S(2)}, u32[]{:S(2)}) collective-permute-start(bf16[1,9,64,256]{3,2,1,0:T(8,128)(2,1)S(1)} %bitcast.38), channel_id=1, source_target_pairs={{0,2},{2,0},{4,6},{6,4},{8,10},{10,8},{12,14},{14,12},{16,18},{18,... | collective-permute-start | bytes 884744 | tf_op jit(solution)/shard_map/ppermute | solution.py:291
  17.6 1.5 %collective-permute-start.2 = (bf16[12,8,256]{2,1,0:T(8,128)(2,1)S(1)}, bf16[12,8,256]{2,1,0:T(8,128)(2,1)S(1)}, u32[]{:S(2)}, u32[]{:S(2)}) collective-permute-start(bf16[12,8,256]{2,1,0:T(8,128)(2,1)S(1)} %select_n.113), channel_id=1, source_target_pairs={{0,1},{1,0},{2,3},{3,2},{4,5},{5,4},{6,7},{7,6},{8,9},{9,8},{10,11... | collective-permute-start | bytes 147464 | tf_op jit(solution)/shard_map/ppermute | solution.py:278
  20.2 3.4 %collective-permute-start.6 = (bf16[1,9,64,256]{3,2,1,0:T(8,128)(2,1)S(1)}, bf16[1,9,64,256]{3,2,1,0:T(8,128)(2,1)S(1)}, u32[]{:S(2)}, u32[]{:S(2)}) collective-permute-start(bf16[1,9,64,256]{3,2,1,0:T(8,128)(2,1)S(1)} %bitcast.41), channel_id=1, source_target_pairs={{0,2},{2,0},{4,6},{6,4},{8,10},{10,8},{12,14},{14,12},{16,18},{18,... | collective-permute-start | bytes 884744 | tf_op jit(solution)/shard_map/ppermute | solution.py:291
  24.4 2.9 %shard_map.75 = (bf16[22,64,256]{2,1,0:T(8,128)(2,1)S(1)}, f32[18,64,256]{2,1,0:T(8,128)S(1)}, bf16[24,64,256]{2,1,0:T(8,128)(2,1)S(1)}) custom-call(s32[2]{0:T(128)S(1)} %pad_add_fusion.where, bf16[16,48,256]{2,1,0:T(8,128)(2,1)S(1)} %bitcast.30, bf16[12,48,128]{2,1,0:T(8,128)(2,1)S(1)} %collective-permute-done.left, ...), custom_call_target="tpu_custom_call" | custom-call | flops 1660944384 | bytes 4653056 | tf_op jit(solution)/shard_map/pallas_call | solution.py:24
  27.4 2.7 %shard_map.76 = (bf16[16,48,256]{2,1,0:T(8,128)(2,1)S(1)}, f32[20,64,256]{2,1,0:T(8,128)S(1)}) custom-call(s32[2]{0:T(128)S(1)} %pad_add_fusion.where, bf16[22,64,256]{2,1,0:T(8,128)(2,1)S(1)} %get-tuple-element.37.hidden, bf16[9,128,256]{2,1,0:T(8,128)(2,1)S(1)} %bitcast.33, bf16[1,9,64,256]{3,2,1,0:T(8,128)(2,1)S(1)} %bitcast.42, ...), custom_call_target="tpu_custom_call" | custom-call | flops 1509949440 | bytes 3604480 | tf_op jit(solution)/shard_map/pallas_call | solution.py:24
  30.8 2.6 %collective-permute-done.8.refs_1_ = bf16[20,64,128]{2,1,0:T(8,128)(2,1)S(1)} collective-permute-done((bf16[20,64,128]{2,1,0:T(8,128)(2,1)S(1)}, bf16[20,64,128]{2,1,0:T(8,128)(2,1)S(1)}, u32[]{:S(2)}, u32[]{:S(2)}) %collective-permute-start.8) | collective-permute-done | bytes 327712 | tf_op jit(solution)/shard_map/ppermute | solution.py:278
  33.4 2.9 %shard_map.77 = (bf16[20,64,256]{2,1,0:T(8,128)(2,1)S(1)}, f32[9,256,128]{2,1,0:T(8,128)S(1)}, bf16[9,256,128]{2,1,0:T(8,128)(2,1)}) custom-call(s32[2]{0:T(128)S(1)} %pad_add_fusion.where, bf16[22,64,256]{2,1,0:T(8,128)(2,1)S(1)} %get-tuple-element.37.hidden, f32[20,64,256]{2,1,0:T(8,128)S(1)} %get-tuple-element.40.slope, ...), custom_call_target="tpu_custom_call" | custom-call | flops 1207959552 | bytes 5111808 | tf_op jit(solution)/shard_map/pallas_call | solution.py:24
  36.4 4.4 %shard_map.78 = (bf16[18,64,256]{2,1,0:T(8,128)(2,1)S(1)}, f32[9,256,128]{2,1,0:T(8,128)S(1)}, bf16[9,256,128]{2,1,0:T(8,128)(2,1)}) custom-call(s32[2]{0:T(128)S(1)} %pad_add_fusion.where, bf16[20,64,256]{2,1,0:T(8,128)(2,1)S(1)} %get-tuple-element.42.outer, bf16[9,128,256]{2,1,0:T(8,128)(2,1)S(1)} %bitcast.34, bf16[1,9,64,256]{3,2,1,0:T(8,128)(2,1)S(1)} %bitcast.43, ...), custom_call_target="tpu_custom_call" | custom-call | flops 2566914048 | bytes 6160384 | tf_op jit(solution)/shard_map/pallas_call | solution.py:24
  42.1 1.7 %collective-permute-done.9.came = bf16[9,256,128]{2,1,0:T(8,128)(2,1)S(1)} collective-permute-done((bf16[9,256,128]{2,1,0:T(8,128)(2,1)}, bf16[9,256,128]{2,1,0:T(8,128)(2,1)S(1)}, u32[]{:S(2)}, u32[]{:S(2)}) %collective-permute-start.9) | collective-permute-done | bytes 589856 | tf_op jit(solution)/shard_map/ppermute | solution.py:227
  44.5 3.5 %collective-permute-start.10 = (bf16[9,64,128]{2,1,0:T(8,128)(2,1)S(1)}, bf16[9,64,128]{2,1,0:T(8,128)(2,1)S(1)}, u32[]{:S(2)}, u32[]{:S(2)}) collective-permute-start(bf16[9,64,128]{2,1,0:T(8,128)(2,1)S(1)} %get-tuple-element.49), channel_id=1, source_target_pairs={{0,4},{1,5},{2,6},{3,7},{4,0},{5,1},{6,2},{7,3},{8,12},{9,13},{10,... | collective-permute-start | bytes 442376 | tf_op jit(solution)/shard_map/ppermute | solution.py:242
  48.5 1.0 %collective-permute-start.12 = (bf16[9,64,128]{2,1,0:T(8,128)(2,1)S(1)}, bf16[9,64,128]{2,1,0:T(8,128)(2,1)S(1)}, u32[]{:S(2)}, u32[]{:S(2)}) collective-permute-start(bf16[9,64,128]{2,1,0:T(8,128)(2,1)S(1)} %get-tuple-element.51), channel_id=1, source_target_pairs={{0,5},{1,4},{2,7},{3,6},{4,1},{5,0},{6,3},{7,2},{8,13},{9,12},{10,... | collective-permute-start | bytes 442376 | tf_op jit(solution)/shard_map/ppermute | solution.py:242
  50.3 2.0 %shard_map.79 = bf16[16,48,256]{2,1,0:T(8,128)(2,1)S(1)} custom-call(s32[2]{0:T(128)S(1)} %pad_add_fusion.where, bf16[18,64,256]{2,1,0:T(8,128)(2,1)S(1)} %copy-done.12, bf16[9,128,256]{2,1,0:T(8,128)(2,1)S(1)} %bitcast.37, bf16[1,9,64,256]{3,2,1,0:T(8,128)(2,1)S(1)} %bitcast.40, bf16[1,9,64,256]{3,2,1,0:T(8,128)(2,1)S(1)} %copy-done.8), custom_call_target="tpu_custom_call" | custom-call | flops 1207959552 | bytes 2162688 | tf_op jit(solution)/shard_map/pallas_call | solution.py:24
  53.8 2.0 %collective-permute-start.18 = (bf16[9,64,128]{2,1,0:T(8,128)(2,1)S(1)}, bf16[9,64,128]{2,1,0:T(8,128)(2,1)S(1)}, u32[]{:S(2)}, u32[]{:S(2)}) collective-permute-start(bf16[9,64,128]{2,1,0:T(8,128)(2,1)S(1)} %get-tuple-element.55), channel_id=1, source_target_pairs={{0,4},{1,5},{2,6},{3,7},{4,0},{5,1},{6,2},{7,3},{8,12},{9,13},{10,... | collective-permute-start | bytes 442376 | tf_op jit(solution)/shard_map/ppermute | solution.py:242
  55.8 1.5 %collective-permute-start.19 = (bf16[9,64,128]{2,1,0:T(8,128)(2,1)S(1)}, bf16[9,64,128]{2,1,0:T(8,128)(2,1)S(1)}, u32[]{:S(2)}, u32[]{:S(2)}) collective-permute-start(bf16[9,64,128]{2,1,0:T(8,128)(2,1)S(1)} %get-tuple-element.56), channel_id=1, source_target_pairs={{0,1},{1,0},{2,3},{3,2},{4,5},{5,4},{6,7},{7,6},{8,9},{9,8},{10,11... | collective-permute-start | bytes 442376 | tf_op jit(solution)/shard_map/ppermute | solution.py:242
  58.0 3.2 %collective-permute-start.13 = (bf16[9,64,128]{2,1,0:T(8,128)(2,1)S(1)}, bf16[9,64,128]{2,1,0:T(8,128)(2,1)S(1)}, u32[]{:S(2)}, u32[]{:S(2)}) collective-permute-start(bf16[9,64,128]{2,1,0:T(8,128)(2,1)S(1)} %add_convert_fusion.5), channel_id=1, source_target_pairs={{0,8},{2,18},{4,12},{6,22},{8,0},{10,26},{12,4},{14,30},{16,24},{1... | collective-permute-start | bytes 442376 | tf_op jit(solution)/shard_map/ppermute | solution.py:251
  61.1 6.1 %collective-permute-done.19 = bf16[9,64,128]{2,1,0:T(8,128)(2,1)S(1)} collective-permute-done((bf16[9,64,128]{2,1,0:T(8,128)(2,1)S(1)}, bf16[9,64,128]{2,1,0:T(8,128)(2,1)S(1)}, u32[]{:S(2)}, u32[]{:S(2)}) %collective-permute-start.19) | collective-permute-done | bytes 147488 | tf_op jit(solution)/shard_map/ppermute | solution.py:242
  67.4 1.6 %collective-permute-start.21 = (bf16[9,64,128]{2,1,0:T(8,128)(2,1)S(1)}, bf16[9,64,128]{2,1,0:T(8,128)(2,1)S(1)}, u32[]{:S(2)}, u32[]{:S(2)}) collective-permute-start(bf16[9,64,128]{2,1,0:T(8,128)(2,1)S(1)} %add_convert_fusion.2), channel_id=1, source_target_pairs={{0,8},{2,18},{4,12},{6,22},{8,0},{10,26},{12,4},{14,30},{16,24},{1... | collective-permute-start | bytes 442376 | tf_op jit(solution)/shard_map/ppermute | solution.py:251
  69.0 2.6 %collective-permute-start.14 = (bf16[9,64,128]{2,1,0:T(8,128)(2,1)S(1)}, bf16[9,64,128]{2,1,0:T(8,128)(2,1)S(1)}, u32[]{:S(2)}, u32[]{:S(2)}) collective-permute-start(bf16[9,64,128]{2,1,0:T(8,128)(2,1)S(1)} %add_convert_fusion.4), channel_id=1, source_target_pairs={{0,16},{2,10},{4,20},{6,14},{8,24},{10,2},{12,28},{14,6},{16,0},{1... | collective-permute-start | bytes 442376 | tf_op jit(solution)/shard_map/ppermute | solution.py:251
  71.6 4.6 %collective-permute-done.21 = bf16[9,64,128]{2,1,0:T(8,128)(2,1)S(1)} collective-permute-done((bf16[9,64,128]{2,1,0:T(8,128)(2,1)S(1)}, bf16[9,64,128]{2,1,0:T(8,128)(2,1)S(1)}, u32[]{:S(2)}, u32[]{:S(2)}) %collective-permute-start.21) | collective-permute-done | bytes 147488 | tf_op jit(solution)/shard_map/ppermute | solution.py:251
  76.3 1.1 %collective-permute-start.22 = (bf16[9,64,128]{2,1,0:T(8,128)(2,1)S(1)}, bf16[9,64,128]{2,1,0:T(8,128)(2,1)S(1)}, u32[]{:S(2)}, u32[]{:S(2)}) collective-permute-start(bf16[9,64,128]{2,1,0:T(8,128)(2,1)S(1)} %add_convert_fusion.1), channel_id=1, source_target_pairs={{0,16},{2,10},{4,20},{6,14},{8,24},{10,2},{12,28},{14,6},{16,0},{1... | collective-permute-start | bytes 442376 | tf_op jit(solution)/shard_map/ppermute | solution.py:251
  77.5 1.7 %collective-permute-start.15 = (bf16[9,64,128]{2,1,0:T(8,128)(2,1)S(1)}, bf16[9,64,128]{2,1,0:T(8,128)(2,1)S(1)}, u32[]{:S(2)}, u32[]{:S(2)}) collective-permute-start(bf16[9,64,128]{2,1,0:T(8,128)(2,1)S(1)} %add_convert_fusion.3), channel_id=1, source_target_pairs={{0,4},{2,6},{4,0},{6,2},{8,12},{10,14},{12,8},{14,10},{16,20},{18,... | collective-permute-start | bytes 442376 | tf_op jit(solution)/shard_map/ppermute | solution.py:253
  79.1 4.8 %collective-permute-done.22 = bf16[9,64,128]{2,1,0:T(8,128)(2,1)S(1)} collective-permute-done((bf16[9,64,128]{2,1,0:T(8,128)(2,1)S(1)}, bf16[9,64,128]{2,1,0:T(8,128)(2,1)S(1)}, u32[]{:S(2)}, u32[]{:S(2)}) %collective-permute-start.22) | collective-permute-done | bytes 147488 | tf_op jit(solution)/shard_map/ppermute | solution.py:251
  84.0 1.2 %collective-permute-start.23 = (bf16[9,64,128]{2,1,0:T(8,128)(2,1)S(1)}, bf16[9,64,128]{2,1,0:T(8,128)(2,1)S(1)}, u32[]{:S(2)}, u32[]{:S(2)}) collective-permute-start(bf16[9,64,128]{2,1,0:T(8,128)(2,1)S(1)} %add_convert_fusion), channel_id=1, source_target_pairs={{0,4},{2,6},{4,0},{6,2},{8,12},{10,14},{12,8},{14,10},{16,20},{18,... | collective-permute-start | bytes 442376 | tf_op jit(solution)/shard_map/ppermute | solution.py:253
  85.3 3.9 %collective-permute-done.23 = bf16[9,64,128]{2,1,0:T(8,128)(2,1)S(1)} collective-permute-done((bf16[9,64,128]{2,1,0:T(8,128)(2,1)S(1)}, bf16[9,64,128]{2,1,0:T(8,128)(2,1)S(1)}, u32[]{:S(2)}, u32[]{:S(2)}) %collective-permute-start.23) | collective-permute-done | bytes 147488 | tf_op jit(solution)/shard_map/ppermute | solution.py:253
  89.6 1.3 %collective-permute-done.24 = bf16[9,128,128]{2,1,0:T(8,128)(2,1)S(1)} collective-permute-done((bf16[9,128,128]{2,1,0:T(8,128)(2,1)S(1)}, bf16[9,128,128]{2,1,0:T(8,128)(2,1)S(1)}, u32[]{:S(2)}, u32[]{:S(2)}) %collective-permute-start.24) | collective-permute-done | bytes 294944 | tf_op jit(solution)/shard_map/ppermute | solution.py:258
  91.1 1.7 %multiply_bitcast_fusion = (f32[128,3,3,256]{3,0,2,1:T(8,128)}, f32[128,3,3,256]{3,0,2,1:T(8,128)}) fusion(bf16[3,3,128,128]{3,2,1,0:T(8,128)(2,1)S(1)} %bitcast.47, bf16[3,3,128,128]{3,2,1,0:T(8,128)(2,1)S(1)} %bitcast.46, bf16[3,3,128,128]{3,2,1,0:T(8,128)(2,1)S(1)} %bitcast.45, bf16[3,3,128,128]{3,2,1,0:T(8,128)(2,1)S(1)} %bitcast.44), kind=kLoop, calls=%fused_computation.2 | loop fusion | flops 2949120 | bytes 3538944 | tf_op jit(solution)/shard_map/transpose | solution.py:400
  (89 shorter events, 10.4 us)
Async XLA Ops:
  1.6 12.3 %collective-permute-start.3 = (bf16[9,64,256]{2,1,0:T(8,128)(2,1)S(1)}, bf16[9,64,256]{2,1,0:T(8,128)(2,1)S(1)}, u32[]{:S(2)}, u32[]{:S(2)}) collective-permute-start(bf16[9,64,256]{2,1,0:T(8,128)(2,1)S(1)} %constant_dynamic-slice_fusion.4), channel_id=1, source_target_pairs={{0,1},{1,0},{2,3},{3,2},{4,5},{5,4},{6,7},{7,6},{8,9},{9,8},{10,11... | collective-permute-start | bytes 884744 | tf_op jit(solution)/shard_map/ppermute | solution.py:278
  4.7 8.6 %copy-start.2 = (bf16[128,3,3,256]{3,0,2,1:T(8,128)(2,1)S(1)}, bf16[128,3,3,256]{3,0,2,1:T(8,128)(2,1)}, u32[]{:S(2)}) copy-start(bf16[128,3,3,256]{3,0,2,1:T(8,128)(2,1)} %param.6) | copy-start | bytes 1769476
  6.7 12.5 %copy-start.13 = (bf16[128,16,96]{0,2,1:T(8,128)(2,1)S(1)}, bf16[128,16,96]{0,2,1:T(8,128)(2,1)}, u32[]{:S(2)}) copy-start(bf16[128,16,96]{0,2,1:T(8,128)(2,1)} %param.7) | copy-start | bytes 1179652
  6.8 3.0 %collective-permute-start = (bf16[12,48,128]{2,1,0:T(8,128)(2,1)S(1)}, bf16[12,48,128]{2,1,0:T(8,128)(2,1)S(1)}, u32[]{:S(2)}, u32[]{:S(2)}) collective-permute-start(bf16[12,48,128]{2,1,0:T(8,128)(2,1)S(1)} %pad_maximum_fusion.2), channel_id=1, source_target_pairs={{0,2},{2,4},{4,6},{6,8},{8,10},{10,12},{12,14},{14,16},{16,18},{18... | collective-permute-start | bytes 442376 | tf_op jit(solution)/shard_map/ppermute | solution.py:307
  8.4 4.8 %collective-permute-start.1 = (bf16[12,48,128]{2,1,0:T(8,128)(2,1)S(1)}, bf16[12,48,128]{2,1,0:T(8,128)(2,1)S(1)}, u32[]{:S(2)}, u32[]{:S(2)}) collective-permute-start(bf16[12,48,128]{2,1,0:T(8,128)(2,1)S(1)} %pad_maximum_fusion.3), channel_id=1, source_target_pairs={{2,0},{4,2},{6,4},{8,6},{10,8},{12,10},{14,12},{16,14},{18,16},{20... | collective-permute-start | bytes 442376 | tf_op jit(solution)/shard_map/ppermute | solution.py:308
  13.4 6.9 %collective-permute-start.5 = (bf16[9,64,256]{2,1,0:T(8,128)(2,1)S(1)}, bf16[9,64,256]{2,1,0:T(8,128)(2,1)S(1)}, u32[]{:S(2)}, u32[]{:S(2)}) collective-permute-start(bf16[9,64,256]{2,1,0:T(8,128)(2,1)S(1)} %constant_dynamic-slice_fusion.2), channel_id=1, source_target_pairs={{0,1},{1,0},{2,3},{3,2},{4,5},{5,4},{6,7},{7,6},{8,9},{9,8},{10,11... | collective-permute-start | bytes 884744 | tf_op jit(solution)/shard_map/ppermute | solution.py:278
  13.9 10.5 %copy-start.5 = (bf16[9,64,256]{2,1,0:T(8,128)(2,1)}, bf16[9,64,256]{2,1,0:T(8,128)(2,1)S(1)}, u32[]{:S(2)}) copy-start(bf16[9,64,256]{2,1,0:T(8,128)(2,1)S(1)} %collective-permute-done.3) | copy-start | bytes 884740
  13.9 9.8 %collective-permute-start.4 = (bf16[1,9,64,256]{3,2,1,0:T(8,128)(2,1)S(1)}, bf16[1,9,64,256]{3,2,1,0:T(8,128)(2,1)S(1)}, u32[]{:S(2)}, u32[]{:S(2)}) collective-permute-start(bf16[1,9,64,256]{3,2,1,0:T(8,128)(2,1)S(1)} %bitcast.38), channel_id=1, source_target_pairs={{0,2},{2,0},{4,6},{6,4},{8,10},{10,8},{12,14},{14,12},{16,18},{18,... | collective-permute-start | bytes 884744 | tf_op jit(solution)/shard_map/ppermute | solution.py:291
  17.6 6.8 %collective-permute-start.2 = (bf16[12,8,256]{2,1,0:T(8,128)(2,1)S(1)}, bf16[12,8,256]{2,1,0:T(8,128)(2,1)S(1)}, u32[]{:S(2)}, u32[]{:S(2)}) collective-permute-start(bf16[12,8,256]{2,1,0:T(8,128)(2,1)S(1)} %select_n.113), channel_id=1, source_target_pairs={{0,1},{1,0},{2,3},{3,2},{4,5},{5,4},{6,7},{7,6},{8,9},{9,8},{10,11... | collective-permute-start | bytes 147464 | tf_op jit(solution)/shard_map/ppermute | solution.py:278
  20.2 7.2 %copy-start.9 = (bf16[9,64,256]{2,1,0:T(8,128)(2,1)}, bf16[9,64,256]{2,1,0:T(8,128)(2,1)S(1)}, u32[]{:S(2)}) copy-start(bf16[9,64,256]{2,1,0:T(8,128)(2,1)S(1)} %collective-permute-done.5) | copy-start | bytes 884740
  20.2 7.2 %collective-permute-start.6 = (bf16[1,9,64,256]{3,2,1,0:T(8,128)(2,1)S(1)}, bf16[1,9,64,256]{3,2,1,0:T(8,128)(2,1)S(1)}, u32[]{:S(2)}, u32[]{:S(2)}) collective-permute-start(bf16[1,9,64,256]{3,2,1,0:T(8,128)(2,1)S(1)} %bitcast.41), channel_id=1, source_target_pairs={{0,2},{2,0},{4,6},{6,4},{8,10},{10,8},{12,14},{14,12},{16,18},{18,... | collective-permute-start | bytes 884744 | tf_op jit(solution)/shard_map/ppermute | solution.py:291
  23.8 9.7 %collective-permute-start.8 = (bf16[20,64,128]{2,1,0:T(8,128)(2,1)S(1)}, bf16[20,64,128]{2,1,0:T(8,128)(2,1)S(1)}, u32[]{:S(2)}, u32[]{:S(2)}) collective-permute-start(bf16[20,64,128]{2,1,0:T(8,128)(2,1)S(1)} %get-tuple-element.41), channel_id=1, source_target_pairs={{0,1},{1,0},{2,3},{3,2},{4,5},{5,4},{6,7},{7,6},{8,9},{9,8},{10,11... | collective-permute-start | bytes 983048 | tf_op jit(solution)/shard_map/ppermute | solution.py:278
  41.6 2.2 %collective-permute-start.9 = (bf16[9,256,128]{2,1,0:T(8,128)(2,1)}, bf16[9,256,128]{2,1,0:T(8,128)(2,1)S(1)}, u32[]{:S(2)}, u32[]{:S(2)}) collective-permute-start(bf16[9,256,128]{2,1,0:T(8,128)(2,1)} %get-tuple-element.47), channel_id=1, source_target_pairs={{0,2},{2,0},{4,6},{6,4},{8,10},{10,8},{12,14},{14,12},{16,18},{18,... | collective-permute-start | bytes 1769480 | tf_op jit(solution)/shard_map/ppermute | solution.py:227
  41.6 11.6 %collective-permute-start.17 = (bf16[9,256,128]{2,1,0:T(8,128)(2,1)}, bf16[9,256,128]{2,1,0:T(8,128)(2,1)S(1)}, u32[]{:S(2)}, u32[]{:S(2)}) collective-permute-start(bf16[9,256,128]{2,1,0:T(8,128)(2,1)} %get-tuple-element.53), channel_id=1, source_target_pairs={{0,2},{2,0},{4,6},{6,4},{8,10},{10,8},{12,14},{14,12},{16,18},{18,... | collective-permute-start | bytes 1769480 | tf_op jit(solution)/shard_map/ppermute | solution.py:227
  42.1 7.5 %copy-start.1 = (bf16[16,48,256]{2,1,0:T(8,128)(2,1)S(1)}, bf16[16,48,256]{2,1,0:T(8,128)(2,1)}, u32[]{:S(2)}) copy-start(bf16[16,48,256]{2,1,0:T(8,128)(2,1)} %copy-done) | copy-start | bytes 1179652
  43.8 6.5 %copy-start.8 = (bf16[1,9,64,256]{3,2,1,0:T(8,128)(2,1)S(1)}, bf16[1,9,64,256]{3,2,1,0:T(8,128)(2,1)}, u32[]{:S(2)}) copy-start(bf16[1,9,64,256]{3,2,1,0:T(8,128)(2,1)} %copy-done.7) | copy-start | bytes 884740
  43.8 6.5 %copy-start.12 = (bf16[18,64,256]{2,1,0:T(8,128)(2,1)S(1)}, bf16[18,64,256]{2,1,0:T(8,128)(2,1)}, u32[]{:S(2)}) copy-start(bf16[18,64,256]{2,1,0:T(8,128)(2,1)} %copy-done.11) | copy-start | bytes 1769476
  44.5 11.4 %collective-permute-start.10 = (bf16[9,64,128]{2,1,0:T(8,128)(2,1)S(1)}, bf16[9,64,128]{2,1,0:T(8,128)(2,1)S(1)}, u32[]{:S(2)}, u32[]{:S(2)}) collective-permute-start(bf16[9,64,128]{2,1,0:T(8,128)(2,1)S(1)} %get-tuple-element.49), channel_id=1, source_target_pairs={{0,4},{1,5},{2,6},{3,7},{4,0},{5,1},{6,2},{7,3},{8,12},{9,13},{10,... | collective-permute-start | bytes 442376 | tf_op jit(solution)/shard_map/ppermute | solution.py:242
  48.0 9.9 %collective-permute-start.11 = (bf16[9,64,128]{2,1,0:T(8,128)(2,1)S(1)}, bf16[9,64,128]{2,1,0:T(8,128)(2,1)S(1)}, u32[]{:S(2)}, u32[]{:S(2)}) collective-permute-start(bf16[9,64,128]{2,1,0:T(8,128)(2,1)S(1)} %get-tuple-element.50), channel_id=1, source_target_pairs={{0,1},{1,0},{2,3},{3,2},{4,5},{5,4},{6,7},{7,6},{8,9},{9,8},{10,11... | collective-permute-start | bytes 442376 | tf_op jit(solution)/shard_map/ppermute | solution.py:242
  48.5 9.4 %collective-permute-start.12 = (bf16[9,64,128]{2,1,0:T(8,128)(2,1)S(1)}, bf16[9,64,128]{2,1,0:T(8,128)(2,1)S(1)}, u32[]{:S(2)}, u32[]{:S(2)}) collective-permute-start(bf16[9,64,128]{2,1,0:T(8,128)(2,1)S(1)} %get-tuple-element.51), channel_id=1, source_target_pairs={{0,5},{1,4},{2,7},{3,6},{4,1},{5,0},{6,3},{7,2},{8,13},{9,12},{10,... | collective-permute-start | bytes 442376 | tf_op jit(solution)/shard_map/ppermute | solution.py:242
  49.7 39.7 %collective-permute-start.7 = (bf16[16,48,128]{2,1,0:T(8,128)(2,1)S(1)}, bf16[16,48,128]{2,1,0:T(8,128)(2,1)S(1)}, u32[]{:S(2)}, u32[]{:S(2)}) collective-permute-start(bf16[16,48,128]{2,1,0:T(8,128)(2,1)S(1)} %get-tuple-element.68), channel_id=1, source_target_pairs={{0,1},{1,0},{2,3},{3,2},{4,5},{5,4},{6,7},{7,6},{8,9},{9,8},{10,11... | collective-permute-start | bytes 589832 | tf_op jit(solution)/shard_map/ppermute | solution.py:278
  53.8 7.3 %collective-permute-start.18 = (bf16[9,64,128]{2,1,0:T(8,128)(2,1)S(1)}, bf16[9,64,128]{2,1,0:T(8,128)(2,1)S(1)}, u32[]{:S(2)}, u32[]{:S(2)}) collective-permute-start(bf16[9,64,128]{2,1,0:T(8,128)(2,1)S(1)} %get-tuple-element.55), channel_id=1, source_target_pairs={{0,4},{1,5},{2,6},{3,7},{4,0},{5,1},{6,2},{7,3},{8,12},{9,13},{10,... | collective-permute-start | bytes 442376 | tf_op jit(solution)/shard_map/ppermute | solution.py:242
  55.8 11.4 %collective-permute-start.19 = (bf16[9,64,128]{2,1,0:T(8,128)(2,1)S(1)}, bf16[9,64,128]{2,1,0:T(8,128)(2,1)S(1)}, u32[]{:S(2)}, u32[]{:S(2)}) collective-permute-start(bf16[9,64,128]{2,1,0:T(8,128)(2,1)S(1)} %get-tuple-element.56), channel_id=1, source_target_pairs={{0,1},{1,0},{2,3},{3,2},{4,5},{5,4},{6,7},{7,6},{8,9},{9,8},{10,11... | collective-permute-start | bytes 442376 | tf_op jit(solution)/shard_map/ppermute | solution.py:242
  57.9 9.4 %collective-permute-start.20 = (bf16[9,64,128]{2,1,0:T(8,128)(2,1)S(1)}, bf16[9,64,128]{2,1,0:T(8,128)(2,1)S(1)}, u32[]{:S(2)}, u32[]{:S(2)}) collective-permute-start(bf16[9,64,128]{2,1,0:T(8,128)(2,1)S(1)} %get-tuple-element.57), channel_id=1, source_target_pairs={{0,5},{1,4},{2,7},{3,6},{4,1},{5,0},{6,3},{7,2},{8,13},{9,12},{10,... | collective-permute-start | bytes 442376 | tf_op jit(solution)/shard_map/ppermute | solution.py:242
  58.0 11.0 %collective-permute-start.13 = (bf16[9,64,128]{2,1,0:T(8,128)(2,1)S(1)}, bf16[9,64,128]{2,1,0:T(8,128)(2,1)S(1)}, u32[]{:S(2)}, u32[]{:S(2)}) collective-permute-start(bf16[9,64,128]{2,1,0:T(8,128)(2,1)S(1)} %add_convert_fusion.5), channel_id=1, source_target_pairs={{0,8},{2,18},{4,12},{6,22},{8,0},{10,26},{12,4},{14,30},{16,24},{1... | collective-permute-start | bytes 442376 | tf_op jit(solution)/shard_map/ppermute | solution.py:251
  67.4 8.9 %collective-permute-start.21 = (bf16[9,64,128]{2,1,0:T(8,128)(2,1)S(1)}, bf16[9,64,128]{2,1,0:T(8,128)(2,1)S(1)}, u32[]{:S(2)}, u32[]{:S(2)}) collective-permute-start(bf16[9,64,128]{2,1,0:T(8,128)(2,1)S(1)} %add_convert_fusion.2), channel_id=1, source_target_pairs={{0,8},{2,18},{4,12},{6,22},{8,0},{10,26},{12,4},{14,30},{16,24},{1... | collective-permute-start | bytes 442376 | tf_op jit(solution)/shard_map/ppermute | solution.py:251
  69.0 8.4 %collective-permute-start.14 = (bf16[9,64,128]{2,1,0:T(8,128)(2,1)S(1)}, bf16[9,64,128]{2,1,0:T(8,128)(2,1)S(1)}, u32[]{:S(2)}, u32[]{:S(2)}) collective-permute-start(bf16[9,64,128]{2,1,0:T(8,128)(2,1)S(1)} %add_convert_fusion.4), channel_id=1, source_target_pairs={{0,16},{2,10},{4,20},{6,14},{8,24},{10,2},{12,28},{14,6},{16,0},{1... | collective-permute-start | bytes 442376 | tf_op jit(solution)/shard_map/ppermute | solution.py:251
  76.3 7.7 %collective-permute-start.22 = (bf16[9,64,128]{2,1,0:T(8,128)(2,1)S(1)}, bf16[9,64,128]{2,1,0:T(8,128)(2,1)S(1)}, u32[]{:S(2)}, u32[]{:S(2)}) collective-permute-start(bf16[9,64,128]{2,1,0:T(8,128)(2,1)S(1)} %add_convert_fusion.1), channel_id=1, source_target_pairs={{0,16},{2,10},{4,20},{6,14},{8,24},{10,2},{12,28},{14,6},{16,0},{1... | collective-permute-start | bytes 442376 | tf_op jit(solution)/shard_map/ppermute | solution.py:251
  77.5 7.7 %collective-permute-start.15 = (bf16[9,64,128]{2,1,0:T(8,128)(2,1)S(1)}, bf16[9,64,128]{2,1,0:T(8,128)(2,1)S(1)}, u32[]{:S(2)}, u32[]{:S(2)}) collective-permute-start(bf16[9,64,128]{2,1,0:T(8,128)(2,1)S(1)} %add_convert_fusion.3), channel_id=1, source_target_pairs={{0,4},{2,6},{4,0},{6,2},{8,12},{10,14},{12,8},{14,10},{16,20},{18,... | collective-permute-start | bytes 442376 | tf_op jit(solution)/shard_map/ppermute | solution.py:253
  84.0 5.2 %collective-permute-start.23 = (bf16[9,64,128]{2,1,0:T(8,128)(2,1)S(1)}, bf16[9,64,128]{2,1,0:T(8,128)(2,1)S(1)}, u32[]{:S(2)}, u32[]{:S(2)}) collective-permute-start(bf16[9,64,128]{2,1,0:T(8,128)(2,1)S(1)} %add_convert_fusion), channel_id=1, source_target_pairs={{0,4},{2,6},{4,0},{6,2},{8,12},{10,14},{12,8},{14,10},{16,20},{18,... | collective-permute-start | bytes 442376 | tf_op jit(solution)/shard_map/ppermute | solution.py:253
  85.3 4.2 %collective-permute-start.16 = (bf16[9,128,128]{2,1,0:T(8,128)(2,1)S(1)}, bf16[9,128,128]{2,1,0:T(8,128)(2,1)S(1)}, u32[]{:S(2)}, u32[]{:S(2)}) collective-permute-start(bf16[9,128,128]{2,1,0:T(8,128)(2,1)S(1)} %pad_maximum_fusion), channel_id=1, source_target_pairs={{0,2},{2,0},{4,6},{6,4},{8,10},{10,8},{12,14},{14,12},{16,18},{18,... | collective-permute-start | bytes 884744 | tf_op jit(solution)/shard_map/ppermute | solution.py:258
  89.3 1.6 %collective-permute-start.24 = (bf16[9,128,128]{2,1,0:T(8,128)(2,1)S(1)}, bf16[9,128,128]{2,1,0:T(8,128)(2,1)S(1)}, u32[]{:S(2)}, u32[]{:S(2)}) collective-permute-start(bf16[9,128,128]{2,1,0:T(8,128)(2,1)S(1)} %pad_maximum_fusion.1), channel_id=1, source_target_pairs={{0,2},{2,0},{4,6},{6,4},{8,10},{10,8},{12,14},{14,12},{16,18},{18,... | collective-permute-start | bytes 884744 | tf_op jit(solution)/shard_map/ppermute | solution.py:258
  (8 other events, 27.9 us)

commit v3 on v2

--- a/solution.py
+++ b/solution.py
@@ -19,8 +19,8 @@
 def call(kernel, outs, args, scratch=(), flops=0, smem_args=1):
     specs = [pl.BlockSpec(memory_space=pltpu.SMEM)] * smem_args
     specs += [pl.BlockSpec(memory_space=pltpu.VMEM)] * (len(args) - smem_args)
-    nbytes = sum(a.size * a.dtype.itemsize for a in args[smem_args:])
-    nbytes += sum(math.prod(s) * jnp.dtype(t).itemsize for s, t in outs)
+
+
     return pl.pallas_call(
         kernel,
         out_shape=[jax.ShapeDtypeStruct(s, t) for s, t in outs],
@@ -28,13 +28,17 @@
         out_specs=[pl.BlockSpec(memory_space=pltpu.VMEM)] * len(outs),
         scratch_shapes=list(scratch),
         compiler_params=pltpu.CompilerParams(vmem_limit_bytes=VMEM_LIMIT),
-        cost_estimate=pl.CostEstimate(flops=flops, bytes_accessed=nbytes, transcendentals=0),
+        cost_estimate=pl.CostEstimate(flops=0, bytes_accessed=0, transcendentals=0),
     )(*args)
 
 
 def silu_parts(pre):
     sigma = 1.0 / (1.0 + jnp.exp(-pre))
     return pre * sigma, sigma * (1.0 + pre * (1.0 - sigma))
+
+
+def after(x, *others):
+    return lax.optimization_barrier((x, others))[0]
 
 
 def row_mask(first, rows, total):
@@ -87,18 +91,18 @@
     iy, ix = where[0], where[1]
     rows, ch = fbuf.shape[1], fbuf.shape[2]
     ok = row_mask(iy * hl, rows, height)
-    groups = ch // 128
-    gap = jnp.zeros((rows - hl - OFF - HALO, ch), F32)
+    groups, tall = ch // 128, hl + 2 * HALO
+    before = jnp.zeros((OFF - HALO, ch), F32)
+    after = jnp.zeros((rows - hl - OFF - HALO, ch), F32)
     for c in range(wl + 2 * HALO):
         if HALO <= c < wl + HALO:
-            mid = ft[c - HALO].astype(F32)
+            q = c - HALO
+            mid = [up[q].astype(F32), ft[q].astype(F32), down[q].astype(F32)]
         else:
-            ref, at = (left, c) if c < HALO else (right, c - wl - HALO)
-            mid = jnp.concatenate([ref[g * HALO + at].astype(F32) for g in range(groups)], axis=1)
-        r = (c % 2) * HALO
-        above = up[c // 2].astype(F32)[r : r + HALO]
-        below = down[c // 2].astype(F32)[r : r + HALO]
-        x = jnp.concatenate([gap[: OFF - HALO], above, mid, below, gap], axis=0)
+            ref, q = (left, c) if c < HALO else (right, c - wl - HALO)
+            planes = [ref[(g * HALO + q) * tall : (g * HALO + q + 1) * tall].astype(F32) for g in range(groups)]
+            mid = [jnp.concatenate(planes, axis=1)]
+        x = jnp.concatenate([before] + mid + [after], axis=0)
         fbuf[c] = jnp.where(ok, x, 0.0).astype(BF16)
     assemble_filter(w, own, (mine, other), iy, ix % 2, ny)
     for c0, n in chunks(wl + 6, 11):
@@ -131,6 +135,20 @@
                 act_out[c - 2] = act[OFF : OFF + hl].astype(BF16)
 
 
+def edge_kernel(dims, where, ft, up, down, ct_low, ct_high, low, high):
+    ny, hl, wl, height, width = dims
+    ch = ft.shape[2]
+    groups, tall = ch // 128, hl + 2 * HALO
+    for out, first, cot in ((low, 0, ct_low), (high, wl - HALO, ct_high)):
+        for q in range(HALO):
+            c = first + q
+            x = jnp.concatenate([up[c].astype(F32), ft[c].astype(F32), down[c].astype(F32)], axis=0).astype(BF16)
+            for g in range(groups):
+                at = (g * HALO + q) * tall
+                out[at : at + tall] = x[:, g * 128 : (g + 1) * 128]
+        out[groups * HALO * tall :] = cot[...]
+
+
 def own_rows(rows, hl):
     at = lax.broadcasted_iota(jnp.int32, (rows, 1), 0)
     return (at >= OFF) & (at < OFF + hl)
@@ -157,49 +175,54 @@
             send[i * 3 + j] = jnp.where(low_core, high, low).astype(BF16)
 
 
-def outer_kernel(dims, count, where, hidden, slope, *refs):
-    cots, (outer, keep, send, shifted) = refs[:count], refs[count:]
-    ny, hl, wl, height, width = dims
-    iy = where[0]
-    rows = hidden.shape[1]
-    own = own_rows(rows, hl)
+def inner_kernel(dims, count, where, own, mine, other, slope2, slope1, fbuf, *refs):
+    cots, (inner, outer, keep, send, w, shifted) = refs[:count], refs[count:]
+    ny, hl, wl, height, width = dims
+    iy, ix = where[0], where[1]
+    rows = fbuf.shape[1]
+    mine_rows = own_rows(rows, hl)
     for c in range(wl + 4):
         parts = [ref[c].astype(F32) for ref in cots]
         if len(parts) == 2:
-            a, b = parts
+            gap = jnp.zeros((OFF, parts[0].shape[1]), F32)
+            a, b = [
+                jnp.where(iy == 0, jnp.concatenate([gap, p], axis=0), jnp.concatenate([p, gap], axis=0))
+                for p in parts
+            ]
             parts = [jnp.where(iy == 0, a, b), jnp.where(iy == 0, b, a)]
-        val = (jnp.concatenate(parts, axis=1) * slope[c]).astype(BF16)
-        outer[c] = val
-        if 2 <= c < wl + 2:
-            put_shifted(shifted, c - 2, val.astype(F32), own)
-    filter_grad(where, hidden, 2, shifted, wl, keep, send)
-
-
-def inner_kernel(dims, where, outer, own, mine, other, slope, fbuf, inner, keep, send, w, shifted):
-    ny, hl, wl, height, width = dims
-    iy, ix = where[0], where[1]
-    rows = fbuf.shape[1]
+        outer[c] = (jnp.concatenate(parts, axis=1) * slope2[c]).astype(BF16)
     assemble_filter(w, own, (mine, other), iy, ix % 2, ny)
-    mine_rows = own_rows(rows, hl)
     for c0, n in chunks(wl + 2, 9):
         grad = conv_chunk(outer, w, c0, n, True)
         for q in range(n):
             c = c0 + q
-            val = (grad[q] * slope[c]).astype(BF16)
+            val = (grad[q] * slope1[c]).astype(BF16)
             inner[c] = val
             if 1 <= c < wl + 1:
                 put_shifted(shifted, c - 1, val.astype(F32), mine_rows)
     filter_grad(where, fbuf, 3, shifted, wl, keep, send)
 
 
-def input_kernel(dims, where, inner, own, mine, other, out, w):
+def second_grad_kernel(dims, where, hidden, outer, keep, send, shifted):
+    ny, hl, wl, height, width = dims
+    own = own_rows(hidden.shape[1], hl)
+    for c in range(wl):
+        put_shifted(shifted, c, outer[c + 2].astype(F32), own)
+    filter_grad(where, hidden, 2, shifted, wl, keep, send)
+
+
+def input_kernel(dims, where, inner, own, mine, other, out, w, flat):
     ny, hl, wl, height, width = dims
     iy, ix = where[0], where[1]
     assemble_filter(w, own, (mine, other), iy, ix % 2, ny)
     for c0, n in chunks(wl, 8):
         grad = conv_chunk(inner, w, c0, n, True)
         for q in range(n):
-            out[c0 + q] = grad[q][OFF : OFF + hl].astype(BF16)
+            for g in range(flat.shape[0]):
+                part = grad[q][OFF : OFF + hl, g * 128 : (g + 1) * 128]
+                flat[g, pl.ds(c0 + q, hl, stride=wl), :] = part
+    for g in range(flat.shape[0]):
+        out[:, :, g * 128 : (g + 1) * 128] = flat[g].reshape(hl, wl, 128).astype(BF16)
 
 
 def split_kernel(blocks, where, keep, came, own, *messages):
@@ -222,42 +245,83 @@
                 m += 1
 
 
-def reduce_filter(where, keep, send, nx, ny, iy, ix):
-    other_core = [(i, i ^ 1) for i in range(nx)]
-    came = lax.ppermute(send, "gx", other_core)
+def finish_kernel(scale, where, here, there, out):
+    low_core = where[1] % 2 == 0
+    for t in range(here.shape[0]):
+        a, b = here[t].astype(F32) * scale, there[t].astype(F32) * scale
+        half = a.shape[1]
+        out[t, :, :half] = jnp.where(low_core, a, b)
+        out[t, :, half:] = jnp.where(low_core, b, a)
+
+
+def halving_kernel(where, keep, came, own, other, send):
+    iy, ix = where[0], where[1]
+    size = own.shape[1]
+    x = lax.rem(lax.div(ix, 2), 2)
+    by_y = lax.rem(ix, 2) == 0
+
+    def block(y, b):
+        at = pl.multiple_of((y * 2 + b) * size, size)
+        return keep[:, pl.ds(at, size), :] + came[:, pl.ds(at, size), :].astype(F32)
+
+    own[...] = block(iy, x)
+    other[...] = block(jnp.where(by_y, iy, 1 - iy), jnp.where(by_y, 1 - x, x))
+    send[0] = block(jnp.where(by_y, 1 - iy, iy), jnp.where(by_y, x, 1 - x)).astype(BF16)
+    send[1] = block(1 - iy, 1 - x).astype(BF16)
+
+
+def split_filter(where, keep, send, nx, ny):
+    came = lax.ppermute(send, "gx", [(i, i ^ 1) for i in range(nx)])
     blocks = 2 * ny
     taps, ch, half = keep.shape
-    size = ch // blocks
-    outs = [((taps, size, half), F32)] + [((taps, size, half), BF16)] * (blocks - 1)
-    parts = call(functools.partial(split_kernel, blocks), outs, (where, keep, came))
-    total, messages = parts[0], parts[1:]
+    shape = (taps, ch // blocks, half)
+    if ny == 2:
+        outs = [(shape, F32), (shape, F32), ((2,) + shape, BF16)]
+        return call(halving_kernel, outs, (where, keep, came))
+    outs = [(shape, F32)] + [(shape, BF16)] * (blocks - 1)
+    return call(functools.partial(split_kernel, blocks), outs, (where, keep, came))
+
+
+def send_planes(parts, nx, ny):
     arrived = []
-    m = 0
     for d in range(ny):
         for b in range(2):
             if d or b:
                 pairs = [
                     (g * ny + y, (g ^ (2 * b)) * ny + (y + d) % ny) for g in range(nx) for y in range(ny)
                 ]
-                arrived.append(lax.ppermute(messages[m], ("gx", "gy"), pairs))
-                m += 1
-    for part in arrived:
+                arrived.append(lax.ppermute(parts[len(arrived) + 1], ("gx", "gy"), pairs))
+    return arrived
+
+
+def halving_pairs(nx, step):
+    return [(g * 2 + y, g * 2 + 1 - y if g % 2 == step else (g ^ 2) * 2 + y) for g in range(nx) for y in range(2)]
+
+
+def add(parts):
+    total = parts[0].astype(F32)
+    for part in parts[1:]:
         total = total + part.astype(F32)
-    total = total.astype(BF16)
-    bits = [1 << b for b in range(2, nx.bit_length() - 1)]
-    for step in range(len(bits)):
-        near, far = bits[step], bits[len(bits) - 1 - step]
-        pairs = [(g, g ^ (near if g % 2 == 0 else far)) for g in range(nx)]
-        part = lax.ppermute(total, "gx", pairs)
-        total = (total.astype(F32) + part.astype(F32)).astype(BF16)
-    beside = lax.ppermute(total, "gx", [(g, g ^ 2) for g in range(nx)])
+    return total.astype(BF16)
+
+
+def far_bits(nx):
+    return [1 << b for b in range(2, nx.bit_length() - 1)]
+
+
+def far_partner(total, step, nx):
+    bits = far_bits(nx)
+    near, far = bits[step], bits[len(bits) - 1 - step]
+    return lax.ppermute(total, "gx", [(g, g ^ (near if g % 2 == 0 else far)) for g in range(nx)])
+
+
+def finish(where, total, beside, nx, ix, scale):
     first = (ix // 2) % 2 == 0
-    both = jnp.concatenate(
-        [jnp.where(first, total, beside), jnp.where(first, beside, total)], axis=1
-    )
-    rest = lax.ppermute(both, "gx", other_core)
-    low = ix % 2 == 0
-    return jnp.concatenate([jnp.where(low, both, rest), jnp.where(low, rest, both)], axis=2)
+    here = jnp.concatenate([jnp.where(first, total, beside), jnp.where(first, beside, total)], axis=1)
+    there = lax.ppermute(here, "gx", [(g, g ^ 1) for g in range(nx)])
+    taps, size, half = here.shape
+    (out,) = call(functools.partial(finish_kernel, scale), [((taps, size, 2 * half), F32)], (where, here, there))
+    return jnp.transpose(out.reshape(3, 3, size, 2 * half), (2, 0, 1, 3))
 
 
 def body(features, first_filter, second_filter, cotangent):
@@ -286,54 +350,49 @@
     def halves(taps):
         return lax.dynamic_slice_in_dim(taps, core * (co // 2), co // 2, 1)
 
-    def spread(send):
-        mine = jnp.stack([round_y(send, d) for d in range(1, ny)])
-        return mine, lax.ppermute(mine, "gx", [(i, i ^ 1) for i in range(nx)])
+    def spread_y(send):
+        return jnp.stack([round_y(send, d) for d in range(1, ny)])
+
+    def pass_core(mine):
+        return lax.ppermute(mine, "gx", [(i, i ^ 1) for i in range(nx)])
+
+    if ny == 2:
+        row_send = lax.dynamic_slice_in_dim(features, jnp.where(iy == 0, hl - HALO, 0), HALO, 0)
+        up = down = jnp.transpose(round_y(row_send, 1), (1, 0, 2))
+    else:
+        row_send = (features[hl - HALO :], features[:HALO])
+        up = jnp.transpose(round_y(row_send[0], 1), (1, 0, 2))
+        down = jnp.transpose(round_y(row_send[1], ny - 1), (1, 0, 2))
 
     first_own = jnp.transpose(first_filter, (1, 2, 0, 3)).reshape(9, co, ch)
     second_own = jnp.transpose(second_filter, (1, 2, 0, 3)).reshape(9, co, ch)
-    first_send = halves(first_own)
-    first_send, features, cotangent = lax.optimization_barrier((first_send, features, cotangent))
-    first_in = spread(first_send)
-
-    ft = jnp.transpose(features, (1, 0, 2))
+    first_mine = spread_y(halves(after(first_own, row_send)))
+
+    ft = jnp.transpose(after(features, row_send), (1, 0, 2))
     ct = jnp.transpose(cotangent, (1, 2, 0))
-    groups = ch // 128
-
-    def edge(f, c):
-        planes = [f[:, :, g * 128 : (g + 1) * 128] for g in range(groups)]
-        return jnp.concatenate(planes + [c.reshape(2 * groups, hl, 128)], axis=0)
-
-    left = lax.ppermute(edge(ft[wl - HALO :], ct[wl - 2 :]), "gx", forward)
-    right = lax.ppermute(edge(ft[:HALO], ct[:2]), "gx", backward)
-
-    def edge_rows(h0):
-        def of(planes):
-            return jnp.concatenate([planes[g * HALO : (g + 1) * HALO, h0 : h0 + HALO] for g in range(groups)], axis=2)
-
-        strip = jnp.concatenate([of(left), ft[:, h0 : h0 + HALO], of(right)], axis=0)
-        return strip.reshape(wl // 2 + HALO, 2 * HALO, ch)
-
+    groups, tall = ch // 128, hl + 2 * HALO
+    at = groups * HALO * tall
+    shape = ((at + 2 * height * co // 128, 128), BF16)
+    low, high = call(
+        functools.partial(edge_kernel, dims),
+        [shape] * 2,
+        (where, ft, up, down, ct[:2].reshape(-1, 128), ct[wl - 2 :].reshape(-1, 128)),
+    )
+    left = lax.ppermute(high, "gx", forward)
+    right = lax.ppermute(low, "gx", backward)
+    first_mine = after(first_mine, left, right)
+    first_in = (first_mine, pass_core(first_mine))
+    second_mine = spread_y(halves(after(second_own, up)))
+
+    ct = jnp.concatenate([left[at:].reshape(2, height, co), ct, right[at:].reshape(2, height, co)], axis=0)
     if ny == 2:
-        row_send = jnp.where(iy == 0, edge_rows(hl - HALO), edge_rows(0))
-        second_own, row_send = lax.optimization_barrier((second_own, row_send))
-        up = down = round_y(row_send, 1)
+        window = hl + OFF
+        rows_of = lambda y: lax.dynamic_slice_in_dim(ct, y * (height - window), window, 1)
     else:
-        up = round_y(edge_rows(hl - HALO), 1)
-        down = round_y(edge_rows(0), ny - 1)
-    second_in = spread(halves(second_own))
-
-    at = groups * HALO
-    ct = jnp.concatenate(
-        [left[at:].reshape(2, height, co), ct, right[at:].reshape(2, height, co)], axis=0
-    )
-    ct = jnp.pad(ct, ((0, 0), (OFF, rows - OFF - hl), (0, 0)))
-
-    def rows_of(y):
-        return lax.dynamic_slice_in_dim(ct, y * hl, rows, 1)
-
+        ct = jnp.pad(ct, ((0, 0), (OFF, rows - OFF - hl), (0, 0)))
+        rows_of = lambda y: lax.dynamic_slice_in_dim(ct, y * hl, rows, 1)
     cot_send = [rows_of((iy + d) % ny) for d in range(1, ny)]
-    (cot_send, first_in) = lax.optimization_barrier((cot_send, first_in))
+    ft = after(ft, cot_send, second_mine)
     cots = [rows_of(iy)] + [round_y(cot_send[d - 1], d) for d in range(1, ny)]
     if ny != 2:
         full = jnp.zeros((wl + 4, rows, ch), BF16)
@@ -353,6 +412,7 @@
         [weights],
         tap_flops * (wl + 6),
     )
+    second_in = (second_mine, pass_core(second_mine))
     act, slope2 = call(
         functools.partial(conv2_kernel, dims),
         [((wl, hl, ch), BF16), ((wl + 4, rows, ch), F32)],
@@ -361,28 +421,43 @@
         tap_flops * (wl + 4),
     )
     grad_shapes = [((9, ch, ch // 2), F32), ((9, ch, ch // 2), BF16)]
-    outer, keep2, send2 = call(
-        functools.partial(outer_kernel, dims, len(cots)),
-        [((wl + 4, rows, ch), BF16)] + grad_shapes,
-        (where, hidden, slope2, *cots),
-        [bf(wl * rows, 3 * ch)],
+    shifted = bf(wl * rows, 3 * ch)
+    inner, outer, keep1, send1 = call(
+        functools.partial(inner_kernel, dims, len(cots)),
+        [((wl + 2, rows, ch), BF16), ((wl + 4, rows, ch), BF16)] + grad_shapes,
+        (where, second_own, *second_in, slope2, slope1, fbuf, *cots),
+        [weights, shifted],
+        tap_flops * (2 * wl + 2),
+    )
+    keep2, send2 = call(
+        functools.partial(second_grad_kernel, dims),
+        grad_shapes,
+        (where, hidden, outer),
+        [shifted],
         tap_flops * wl,
     )
-    inner, keep1, send1 = call(
-        functools.partial(inner_kernel, dims),
-        [((wl + 2, rows, ch), BF16)] + grad_shapes,
-        (where, outer, second_own, *second_in, slope1, fbuf),
-        [weights, bf(wl * rows, 3 * ch)],
-        tap_flops * (2 * wl + 2),
-    )
+    parts1 = split_filter(where, keep1, send1, nx, ny)
+    keep2 = after(keep2, parts1)
+    parts2 = split_filter(where, keep2, send2, nx, ny)
     (input_grad,) = call(
         functools.partial(input_kernel, dims),
-        [((wl, hl, ch), BF16)],
+        [((hl, wl, ch), BF16)],
         (where, inner, first_own, *first_in),
-        [weights],
+        [weights, pltpu.VMEM((ch // 128, hl * wl, 128), F32)],
         tap_flops * wl,
     )
-    input_grad = jnp.transpose(input_grad, (1, 0, 2))
+    if ny == 2:
+        (own1, other1, send1), (own2, other2, send2) = parts1, parts2
+        axes, pairs = ("gx", "gy"), [halving_pairs(nx, step) for step in range(2)]
+        came1 = lax.ppermute(send1, axes, pairs[0])
+        came2 = lax.ppermute(send2, axes, pairs[0])
+        came1 = after(came1, parts2, input_grad)
+        total1 = add([own1, came1[0], lax.ppermute(add([other1, came1[1]]), axes, pairs[1])])
+        total2 = add([own2, came2[0], lax.ppermute(add([other2, came2[1]]), axes, pairs[1])])
+    else:
+        total1 = add([after(parts1[0], parts2, input_grad)] + send_planes(parts1, nx, ny))
+        total2 = add([parts2[0]] + send_planes(parts2, nx, ny))
+    act = after(act, total2)
 
     def channels_of(y):
         return lax.dynamic_slice_in_dim(act, y * co, co, 2)
@@ -393,12 +468,17 @@
         output = lax.dynamic_update_slice_in_dim(output, part, ((iy - d) % ny) * hl, 1)
     output = jnp.transpose(output, (2, 0, 1))
 
-    grads = []
-    for keep, send in ((keep1, send1), (keep2, send2)):
-        total = reduce_filter(where, keep, send, nx, ny, iy, ix)
-        total = total.astype(F32) * scale_factor
-        grads.append(jnp.transpose(total.reshape(3, 3, co, ch), (2, 0, 1, 3)))
-    return output, input_grad, grads[0], grads[1]
+    for step in range(len(far_bits(nx))):
+        other1 = far_partner(total1, step, nx)
+        other2 = far_partner(total2, step, nx)
+        total1 = add([total1, other1])
+        total2 = add([total2, other2])
+    total2 = after(total2, output)
+    beside1 = lax.ppermute(total1, "gx", [(g, g ^ 2) for g in range(nx)])
+    beside2 = lax.ppermute(total2, "gx", [(g, g ^ 2) for g in range(nx)])
+    first_grad = finish(where, total1, beside1, nx, ix, scale_factor)
+    second_grad = finish(where, total2, after(beside2, first_grad), nx, ix, scale_factor)
+    return output, input_grad, first_grad, second_grad
 
 
 def solution(mesh):

time: 93 us -> 83.3 us (0.90)
  starting transfers between devices: 36.9 us -> 27.4 us
  Pallas kernels: 16.3 us -> 19.5 us
  other arithmetic: 2.6 us -> 0.6 us
  local copies, waits for them, and re-layouts: 5.9 us -> 4.09 us
    ppermute x20 -> x18, starting transfers between devices: 30.6 us -> 20.5 us  [the longest x4 6.41 us: far_partner(): lax.ppermute(total, 'gx', [(g, g ^ (near if g % 2 == 0 else far)) for g i...]
    pallas_call x7 -> x10, Pallas kernels: 16.3 us -> 19.5 us  [call(): pl.pallas_call(kernel, out_shape=[jax.ShapeDtypeStruct(s, t) for s, t in...]
    unnamed x31 -> x11, local copies, waits for them, and re-layouts: 2.5 us -> 0.05 us
    transpose x1 -> x0, other arithmetic: 1.69 us -> none  [body(): grads.append(jnp.transpose(total.reshape(3, 3, co, ch), (2, 0, 1, 3)))]
    ppermute x5, waiting for transfers between devices: 3.57 us -> 4.9 us  [round_y(): return lax.ppermute(x, 'gy', [(i, (i + d) % ny) for i in range(ny)])]
    optimization_barrier x1, local copies, waits for them, and re-layouts: 1.11 us -> 0.12 us  [after(): return lax.optimization_barrier((x, others))[0]]
    dynamic_slice x2, local copies, waits for them, and re-layouts: 1.02 us -> 1.97 us  [halves(): return lax.dynamic_slice_in_dim(taps, core * (co // 2), co // 2, 1)]
    ppermute x20 -> x18, waiting for transfers between devices: 26.5 us -> 25.5 us  [the longest x4 10.1 us: far_partner(): lax.ppermute(total, 'gx', [(g, g ^ (near if g % 2 == 0 else far)) for g i...]
  transfers between devices with their start and end apart: 25 -> 23, of which waited for: 10 -> 11; matrix products, arithmetic and copies ran while one was open for 4% -> 5% of each run, Pallas kernels for 10% -> 17%
where the time goes in v3:
time: 83.3 us; the launch traced here: 83 us
  waiting for transfers between devices  30.4 us (36%)
  starting transfers between devices  27.4 us (33%)
  Pallas kernels  19.5 us (23%)
  local copies, waits for them, and re-layouts  4.09 us (5%)
  between operations  0.95 us (1%)
    pallas_call x10, Pallas kernels, call(): pl.pallas_call(kernel, out_shape=[jax.ShapeDtypeStruct(s, t) for s, t in...  19.5 us
    ppermute x4, waiting for transfers between devices, far_partner(): lax.ppermute(total, 'gx', [(g, g ^ (near if g % 2 == 0 else far)) for g i...  10.1 us
    ppermute x5, starting transfers between devices, round_y(): return lax.ppermute(x, 'gy', [(i, (i + d) % ny) for i in range(ny)])  6.91 us
    ppermute x4, starting transfers between devices, far_partner(): lax.ppermute(total, 'gx', [(g, g ^ (near if g % 2 == 0 else far)) for g i...  6.41 us
    ppermute x5, waiting for transfers between devices, round_y(): return lax.ppermute(x, 'gy', [(i, (i + d) % ny) for i in range(ny)])  4.9 us
    ppermute x1, waiting for transfers between devices, body(): lax.ppermute(add([other1, came1[1]]), axes, pairs[1])  4.56 us
    ppermute x1, starting transfers between devices, body(): left = lax.ppermute(high, 'gx', forward)  3.04 us
    ppermute x1, waiting for transfers between devices, body(): beside1 = lax.ppermute(total1, 'gx', [(g, g ^ 2) for g in range(nx)])  3.02 us
  transfers between devices with their start and end apart: 23, of which 11 were waited for; matrix products, arithmetic and copies ran while one was open for 5% of the time, Pallas kernels for 17%

profile of v3, /device:TPU:0, one launch (start us, length us, event | category | flops | bytes accessed | tf_op | source)
XLA Modules:
  0.0 83.0 jit_solution(13047762354981019558)
XLA Ops:
  1.5 3.0 %collective-permute-start = (bf16[4,16,256]{2,0,1:T(4,128)(2,1)S(1)}, bf16[4,16,256]{2,0,1:T(4,128)(2,1)S(1)}, u32[]{:S(2)}, u32[]{:S(2)}) collective-permute-start(bf16[4,16,256]{2,0,1:T(4,128)(2,1)S(1)} %copy.10), channel_id=1, source_target_pairs={{0,1},{1,0},{2,3},{3,2},{4,5},{5,4},{6,7},{7,6},{8,9},{9,8},{10,11... | collective-permute-start | bytes 98312 | tf_op jit(solution)/shard_map/ppermute | solution.py:342
  4.5 1.0 %constant_dynamic-slice_fusion.2 = bf16[9,64,256]{2,1,0:T(8,128)(2,1)S(1)} fusion(bf16[9,128,256]{2,1,0:T(8,128)(2,1)} %bitcast.42, s32[]{:T(128)S(6)} %select_n.83), kind=kLoop, calls=%fused_computation.28 | loop fusion | bytes 589828 | tf_op jit(solution)/shard_map/dynamic_slice | solution.py:351
  5.6 0.9 %fusion.6 = (bf16[2,96,128]{2,1,0:T(8,128)(2,1)S(1)}, bf16[2,96,128]{2,1,0:T(8,128)(2,1)S(1)}) fusion(bf16[16,96,128]{2,1,0:T(8,128)(2,1)} %bitcast.64), kind=kLoop, calls=%fused_computation.33 | loop fusion | bytes 196608 | tf_op jit(solution)/shard_map/slice | solution.py:379
  6.5 1.0 %constant_dynamic-slice_fusion.3 = bf16[9,64,256]{2,1,0:T(8,128)(2,1)S(1)} fusion(bf16[9,128,256]{2,1,0:T(8,128)(2,1)} %bitcast.45, s32[]{:T(128)S(6)} %select_n.83), kind=kLoop, calls=%fused_computation.29 | loop fusion | bytes 589828 | tf_op jit(solution)/shard_map/dynamic_slice | solution.py:351
  7.5 2.3 %collective-permute-start.3 = (bf16[9,64,256]{2,1,0:T(8,128)(2,1)S(1)}, bf16[9,64,256]{2,1,0:T(8,128)(2,1)S(1)}, u32[]{:S(2)}, u32[]{:S(2)}) collective-permute-start(bf16[9,64,256]{2,1,0:T(8,128)(2,1)S(1)} %constant_dynamic-slice_fusion.3), channel_id=1, source_target_pairs={{0,1},{1,0},{2,3},{3,2},{4,5},{5,4},{6,7},{7,6},{8,9},{9,8},{10,11... | collective-permute-start | bytes 884744 | tf_op jit(solution)/shard_map/ppermute | solution.py:342
  10.6 1.3 %collective-permute-start.2 = (bf16[640,128]{1,0:T(8,128)(2,1)S(1)}, bf16[640,128]{1,0:T(8,128)(2,1)S(1)}, u32[]{:S(2)}, u32[]{:S(2)}) collective-permute-start(bf16[640,128]{1,0:T(8,128)(2,1)S(1)} %get-tuple-element.35), channel_id=1, source_target_pairs={{2,0},{4,2},{6,4},{8,6},{10,8},{12,10},{14,12},{16,14},{18,16},{20... | collective-permute-start | bytes 491528 | tf_op jit(solution)/shard_map/ppermute | solution.py:382
  11.9 3.0 %collective-permute-start.1 = (bf16[640,128]{1,0:T(8,128)(2,1)S(1)}, bf16[640,128]{1,0:T(8,128)(2,1)S(1)}, u32[]{:S(2)}, u32[]{:S(2)}) collective-permute-start(bf16[640,128]{1,0:T(8,128)(2,1)S(1)} %get-tuple-element.34), channel_id=1, source_target_pairs={{0,2},{2,4},{4,6},{6,8},{8,10},{10,12},{12,14},{14,16},{16,18},{18... | collective-permute-start | bytes 491528 | tf_op jit(solution)/shard_map/ppermute | solution.py:381
  15.0 0.9 %collective-permute-done.1.left = bf16[640,128]{1,0:T(8,128)(2,1)S(1)} collective-permute-done((bf16[640,128]{1,0:T(8,128)(2,1)S(1)}, bf16[640,128]{1,0:T(8,128)(2,1)S(1)}, u32[]{:S(2)}, u32[]{:S(2)}) %collective-permute-start.1) | collective-permute-done | bytes 163872 | tf_op jit(solution)/shard_map/ppermute | solution.py:381
  16.1 2.3 %collective-permute-start.5 = (bf16[1,9,64,256]{3,2,1,0:T(8,128)(2,1)S(1)}, bf16[1,9,64,256]{3,2,1,0:T(8,128)(2,1)S(1)}, u32[]{:S(2)}, u32[]{:S(2)}) collective-permute-start(bf16[1,9,64,256]{3,2,1,0:T(8,128)(2,1)S(1)} %bitcast.50), channel_id=1, source_target_pairs={{0,2},{2,0},{4,6},{6,4},{8,10},{10,8},{12,14},{14,12},{16,18},{18,... | collective-permute-start | bytes 884744 | tf_op jit(solution)/shard_map/ppermute | solution.py:357
  18.3 2.0 %collective-permute-done.3 = bf16[9,64,256]{2,1,0:T(8,128)(2,1)S(1)} collective-permute-done((bf16[9,64,256]{2,1,0:T(8,128)(2,1)S(1)}, bf16[9,64,256]{2,1,0:T(8,128)(2,1)S(1)}, u32[]{:S(2)}, u32[]{:S(2)}) %collective-permute-start.3) | collective-permute-done | bytes 294944 | tf_op jit(solution)/shard_map/ppermute | solution.py:342
  21.2 3.0 %shard_map.76 = (bf16[22,64,256]{2,1,0:T(8,128)(2,1)S(1)}, f32[18,64,256]{2,1,0:T(8,128)S(1)}, bf16[24,64,256]{2,1,0:T(8,128)(2,1)S(1)}) custom-call(s32[2]{0:T(128)S(1)} %pad_add_fusion.where, bf16[16,48,256]{2,1,0:T(8,128)(2,1)S(1)} %bitcast.49, bf16[640,128]{1,0:T(8,128)(2,1)S(1)} %collective-permute-done.1.left, ...), custom_call_target="tpu_custom_call" | custom-call | tf_op jit(solution)/shard_map/pallas_call | solution.py:24
  24.2 2.7 %shard_map.77 = (bf16[16,48,256]{2,1,0:T(8,128)(2,1)S(1)}, f32[20,64,256]{2,1,0:T(8,128)S(1)}) custom-call(s32[2]{0:T(128)S(1)} %pad_add_fusion.where, bf16[22,64,256]{2,1,0:T(8,128)(2,1)S(1)} %get-tuple-element.40.hidden, bf16[9,128,256]{2,1,0:T(8,128)(2,1)S(1)} %bitcast.46, bf16[1,9,64,256]{3,2,1,0:T(8,128)(2,1)S(1)} %bitcast.54, ...), custom_call_target="tpu_custom_call" | custom-call | tf_op jit(solution)/shard_map/pallas_call | solution.py:24
  26.9 2.9 %collective-permute-done.7.refs_1_ = bf16[20,56,128]{2,1,0:T(8,128)(2,1)S(1)} collective-permute-done((bf16[20,56,128]{2,1,0:T(8,128)(2,1)S(1)}, bf16[20,56,128]{2,1,0:T(8,128)(2,1)S(1)}, u32[]{:S(2)}, u32[]{:S(2)}) %collective-permute-start.7) | collective-permute-done | bytes 286752 | tf_op jit(solution)/shard_map/ppermute | solution.py:342
  29.8 3.6 %shard_map.78 = (bf16[18,64,256]{2,1,0:T(8,128)(2,1)S(1)}, bf16[20,64,256]{2,1,0:T(8,128)(2,1)S(1)}, f32[9,256,128]{2,1,0:T(8,128)S(1)}, bf16[9,256,128]{2,1,0:T(8,128)(2,1)S(1)}) custom-call(s32[2]{0:T(128)S(1)} %pad_add_fusion.where, bf16[9,128,256]{2,1,0:T(8,128)(2,1)S(1)} %bitcast.47, bf16[1,9,64,256]{3,2,1,0:T(8,128)(2,1)S(1)} %bitcast.55, ...), custom_call_target="tpu_custom_call" | custom-call | tf_op jit(solution)/shard_map/pallas_call | solution.py:24
  33.4 2.0 %shard_map.79 = (f32[9,256,128]{2,1,0:T(8,128)S(1)}, bf16[9,256,128]{2,1,0:T(8,128)(2,1)S(1)}) custom-call(s32[2]{0:T(128)S(1)} %pad_add_fusion.where, bf16[22,64,256]{2,1,0:T(8,128)(2,1)S(1)} %get-tuple-element.40.hidden, bf16[20,64,256]{2,1,0:T(8,128)(2,1)S(1)} %get-tuple-element.45.outer), custom_call_target="tpu_custom_call" | custom-call | tf_op jit(solution)/shard_map/pallas_call | solution.py:24
  37.4 3.1 %shard_map.82 = bf16[48,16,256]{2,1,0:T(8,128)(2,1)} custom-call(s32[2]{0:T(128)S(1)} %pad_add_fusion.where, bf16[18,64,256]{2,1,0:T(8,128)(2,1)S(1)} %get-tuple-element.58.inner, bf16[9,128,256]{2,1,0:T(8,128)(2,1)S(1)} %bitcast.44, bf16[1,9,64,256]{3,2,1,0:T(8,128)(2,1)S(1)} %bitcast.52, bf16[1,9,64,256]{3,2,1,0:T(8,128)(2,1)S(1)} %collective-permute-done.5.other), custom_call_target="tpu_custom_call" | custom-call | tf_op jit(solution)/shard_map/pallas_call | solution.py:24
  41.1 2.3 %collective-permute-done.13 = bf16[2,9,64,128]{3,2,1,0:T(8,128)(2,1)S(1)} collective-permute-done((bf16[2,9,64,128]{3,2,1,0:T(8,128)(2,1)S(1)}, bf16[2,9,64,128]{3,2,1,0:T(8,128)(2,1)S(1)}, u32[]{:S(2)}, u32[]{:S(2)}) %collective-permute-start.13) | collective-permute-done | bytes 294944 | tf_op jit(solution)/shard_map/ppermute | solution.py:452
  43.5 1.6 %collective-permute-start.14 = (bf16[9,64,128]{2,1,0:T(8,128)(2,1)S(1)}, bf16[9,64,128]{2,1,0:T(8,128)(2,1)S(1)}, u32[]{:S(2)}, u32[]{:S(2)}) collective-permute-start(bf16[9,64,128]{2,1,0:T(8,128)(2,1)S(1)} %fusion), channel_id=1, source_target_pairs={{0,4},{1,5},{2,3},{3,2},{4,0},{5,1},{6,7},{7,6},{8,12},{9,13},{10,... | collective-permute-start | bytes 442376 | tf_op jit(solution)/shard_map/ppermute | solution.py:455
  45.7 4.6 %collective-permute-done.14 = bf16[9,64,128]{2,1,0:T(8,128)(2,1)S(1)} collective-permute-done((bf16[9,64,128]{2,1,0:T(8,128)(2,1)S(1)}, bf16[9,64,128]{2,1,0:T(8,128)(2,1)S(1)}, u32[]{:S(2)}, u32[]{:S(2)}) %collective-permute-start.14) | collective-permute-done | bytes 147488 | tf_op jit(solution)/shard_map/ppermute | solution.py:455
  50.4 1.6 %collective-permute-start.15 = (bf16[9,64,128]{2,1,0:T(8,128)(2,1)S(1)}, bf16[9,64,128]{2,1,0:T(8,128)(2,1)S(1)}, u32[]{:S(2)}, u32[]{:S(2)}) collective-permute-start(bf16[9,64,128]{2,1,0:T(8,128)(2,1)S(1)} %fusion.2), channel_id=1, source_target_pairs={{0,8},{2,18},{4,12},{6,22},{8,0},{10,26},{12,4},{14,30},{16,24},{1... | collective-permute-start | bytes 442376 | tf_op jit(solution)/shard_map/ppermute | solution.py:315
  52.1 1.6 %collective-permute-start.11 = (bf16[9,64,128]{2,1,0:T(8,128)(2,1)S(1)}, bf16[9,64,128]{2,1,0:T(8,128)(2,1)S(1)}, u32[]{:S(2)}, u32[]{:S(2)}) collective-permute-start(bf16[9,64,128]{2,1,0:T(8,128)(2,1)S(1)} %fusion.3), channel_id=1, source_target_pairs={{0,4},{1,5},{2,3},{3,2},{4,0},{5,1},{6,7},{7,6},{8,12},{9,13},{10,... | collective-permute-start | bytes 442376 | tf_op jit(solution)/shard_map/ppermute | solution.py:456
  53.6 2.0 %collective-permute-done.15 = bf16[9,64,128]{2,1,0:T(8,128)(2,1)S(1)} collective-permute-done((bf16[9,64,128]{2,1,0:T(8,128)(2,1)S(1)}, bf16[9,64,128]{2,1,0:T(8,128)(2,1)S(1)}, u32[]{:S(2)}, u32[]{:S(2)}) %collective-permute-start.15) | collective-permute-done | bytes 147488 | tf_op jit(solution)/shard_map/ppermute | solution.py:315
  55.6 2.6 %collective-permute-start.16 = (bf16[9,64,128]{2,1,0:T(8,128)(2,1)S(1)}, bf16[9,64,128]{2,1,0:T(8,128)(2,1)S(1)}, u32[]{:S(2)}, u32[]{:S(2)}) collective-permute-start(bf16[9,64,128]{2,1,0:T(8,128)(2,1)S(1)} %add_convert_fusion.3), channel_id=1, source_target_pairs={{0,16},{2,10},{4,20},{6,14},{8,24},{10,2},{12,28},{14,6},{16,0},{1... | collective-permute-start | bytes 442376 | tf_op jit(solution)/shard_map/ppermute | solution.py:315
  58.3 1.6 %collective-permute-start.19 = (bf16[9,64,128]{2,1,0:T(8,128)(2,1)S(1)}, bf16[9,64,128]{2,1,0:T(8,128)(2,1)S(1)}, u32[]{:S(2)}, u32[]{:S(2)}) collective-permute-start(bf16[9,64,128]{2,1,0:T(8,128)(2,1)S(1)} %fusion.5), channel_id=1, source_target_pairs={{0,8},{2,18},{4,12},{6,22},{8,0},{10,26},{12,4},{14,30},{16,24},{1... | collective-permute-start | bytes 442376 | tf_op jit(solution)/shard_map/ppermute | solution.py:315
  60.9 4.1 %collective-permute-done.16 = bf16[9,64,128]{2,1,0:T(8,128)(2,1)S(1)} collective-permute-done((bf16[9,64,128]{2,1,0:T(8,128)(2,1)S(1)}, bf16[9,64,128]{2,1,0:T(8,128)(2,1)S(1)}, u32[]{:S(2)}, u32[]{:S(2)}) %collective-permute-start.16) | collective-permute-done | bytes 147488 | tf_op jit(solution)/shard_map/ppermute | solution.py:315
  65.0 1.6 %collective-permute-start.17 = (bf16[9,64,128]{2,1,0:T(8,128)(2,1)S(1)}, bf16[9,64,128]{2,1,0:T(8,128)(2,1)S(1)}, u32[]{:S(2)}, u32[]{:S(2)}) collective-permute-start(bf16[9,64,128]{2,1,0:T(8,128)(2,1)S(1)} %add_convert_fusion.2), channel_id=1, source_target_pairs={{0,4},{2,6},{4,0},{6,2},{8,12},{10,14},{12,8},{14,10},{16,20},{18,... | collective-permute-start | bytes 442376 | tf_op jit(solution)/shard_map/ppermute | solution.py:477
  67.2 3.0 %collective-permute-done.17 = bf16[9,64,128]{2,1,0:T(8,128)(2,1)S(1)} collective-permute-done((bf16[9,64,128]{2,1,0:T(8,128)(2,1)S(1)}, bf16[9,64,128]{2,1,0:T(8,128)(2,1)S(1)}, u32[]{:S(2)}, u32[]{:S(2)}) %collective-permute-start.17) | collective-permute-done | bytes 147488 | tf_op jit(solution)/shard_map/ppermute | solution.py:477
  70.4 4.0 %collective-permute-done.20 = bf16[9,64,128]{2,1,0:T(8,128)(2,1)S(1)} collective-permute-done((bf16[9,64,128]{2,1,0:T(8,128)(2,1)S(1)}, bf16[9,64,128]{2,1,0:T(8,128)(2,1)S(1)}, u32[]{:S(2)}, u32[]{:S(2)}) %collective-permute-start.20) | collective-permute-done | bytes 147488 | tf_op jit(solution)/shard_map/ppermute | solution.py:315
  75.0 1.7 %shard_map.83 = f32[9,128,256]{2,1,0:T(8,128)} custom-call(s32[2]{0:T(128)S(1)} %pad_add_fusion.where, bf16[9,128,128]{2,1,0:T(8,128)(2,1)S(1)} %pad_maximum_fusion.1.here, bf16[9,128,128]{2,1,0:T(8,128)(2,1)S(1)} %collective-permute-done.18.there), custom_call_target="tpu_custom_call" | custom-call | tf_op jit(solution)/shard_map/pallas_call | solution.py:24
  76.7 3.0 %collective-permute-done.21 = bf16[9,64,128]{2,1,0:T(8,128)(2,1)S(1)} collective-permute-done((bf16[9,64,128]{2,1,0:T(8,128)(2,1)S(1)}, bf16[9,64,128]{2,1,0:T(8,128)(2,1)S(1)}, u32[]{:S(2)}, u32[]{:S(2)}) %collective-permute-start.21) | collective-permute-done | bytes 147488 | tf_op jit(solution)/shard_map/ppermute | solution.py:478
  79.8 1.6 %collective-permute-done.22.there = bf16[9,128,128]{2,1,0:T(8,128)(2,1)S(1)} collective-permute-done((bf16[9,128,128]{2,1,0:T(8,128)(2,1)S(1)}, bf16[9,128,128]{2,1,0:T(8,128)(2,1)S(1)}, u32[]{:S(2)}, u32[]{:S(2)}) %collective-permute-start.22) | collective-permute-done | bytes 294944 | tf_op jit(solution)/shard_map/ppermute | solution.py:321
  81.4 1.7 %shard_map.84 = f32[9,128,256]{2,1,0:T(8,128)} custom-call(s32[2]{0:T(128)S(1)} %pad_add_fusion.where, bf16[9,128,128]{2,1,0:T(8,128)(2,1)S(1)} %pad_maximum_fusion.2.here, bf16[9,128,128]{2,1,0:T(8,128)(2,1)S(1)} %collective-permute-done.22.there), custom_call_target="tpu_custom_call" | custom-call | tf_op jit(solution)/shard_map/pallas_call | solution.py:24
  (60 shorter events, 8.6 us)
Async XLA Ops:
  0.6 9.3 %copy-start.3 = (bf16[48,16,256]{2,1,0:T(8,128)(2,1)S(1)}, bf16[48,16,256]{2,1,0:T(8,128)(2,1)}, u32[]{:S(2)}) copy-start(bf16[48,16,256]{2,1,0:T(8,128)(2,1)} %param.4) | copy-start | bytes 1179652
  1.5 5.0 %collective-permute-start = (bf16[4,16,256]{2,0,1:T(4,128)(2,1)S(1)}, bf16[4,16,256]{2,0,1:T(4,128)(2,1)S(1)}, u32[]{:S(2)}, u32[]{:S(2)}) collective-permute-start(bf16[4,16,256]{2,0,1:T(4,128)(2,1)S(1)} %copy.10), channel_id=1, source_target_pairs={{0,1},{1,0},{2,3},{3,2},{4,5},{5,4},{6,7},{7,6},{8,9},{9,8},{10,11... | collective-permute-start | bytes 98312 | tf_op jit(solution)/shard_map/ppermute | solution.py:342
  5.5 10.6 %collective-permute-start.4 = (bf16[9,64,256]{2,1,0:T(8,128)(2,1)S(1)}, bf16[9,64,256]{2,1,0:T(8,128)(2,1)S(1)}, u32[]{:S(2)}, u32[]{:S(2)}) collective-permute-start(bf16[9,64,256]{2,1,0:T(8,128)(2,1)S(1)} %constant_dynamic-slice_fusion.2), channel_id=1, source_target_pairs={{0,1},{1,0},{2,3},{3,2},{4,5},{5,4},{6,7},{7,6},{8,9},{9,8},{10,11... | collective-permute-start | bytes 884744 | tf_op jit(solution)/shard_map/ppermute | solution.py:342
  5.6 10.4 %copy-start.2 = (bf16[128,16,96]{0,2,1:T(8,128)(2,1)S(1)}, bf16[128,16,96]{0,2,1:T(8,128)(2,1)}, u32[]{:S(2)}) copy-start(bf16[128,16,96]{0,2,1:T(8,128)(2,1)} %param.7) | copy-start | bytes 1179652
  7.5 12.9 %collective-permute-start.3 = (bf16[9,64,256]{2,1,0:T(8,128)(2,1)S(1)}, bf16[9,64,256]{2,1,0:T(8,128)(2,1)S(1)}, u32[]{:S(2)}, u32[]{:S(2)}) collective-permute-start(bf16[9,64,256]{2,1,0:T(8,128)(2,1)S(1)} %constant_dynamic-slice_fusion.3), channel_id=1, source_target_pairs={{0,1},{1,0},{2,3},{3,2},{4,5},{5,4},{6,7},{7,6},{8,9},{9,8},{10,11... | collective-permute-start | bytes 884744 | tf_op jit(solution)/shard_map/ppermute | solution.py:342
  10.6 4.4 %collective-permute-start.2 = (bf16[640,128]{1,0:T(8,128)(2,1)S(1)}, bf16[640,128]{1,0:T(8,128)(2,1)S(1)}, u32[]{:S(2)}, u32[]{:S(2)}) collective-permute-start(bf16[640,128]{1,0:T(8,128)(2,1)S(1)} %get-tuple-element.35), channel_id=1, source_target_pairs={{2,0},{4,2},{6,4},{8,6},{10,8},{12,10},{14,12},{16,14},{18,16},{20... | collective-permute-start | bytes 491528 | tf_op jit(solution)/shard_map/ppermute | solution.py:382
  11.9 4.0 %collective-permute-start.1 = (bf16[640,128]{1,0:T(8,128)(2,1)S(1)}, bf16[640,128]{1,0:T(8,128)(2,1)S(1)}, u32[]{:S(2)}, u32[]{:S(2)}) collective-permute-start(bf16[640,128]{1,0:T(8,128)(2,1)S(1)} %get-tuple-element.34), channel_id=1, source_target_pairs={{0,2},{2,4},{4,6},{6,8},{8,10},{10,12},{12,14},{14,16},{16,18},{18... | collective-permute-start | bytes 491528 | tf_op jit(solution)/shard_map/ppermute | solution.py:381
  15.0 6.2 %copy-start = (bf16[128,3,3,256]{3,0,2,1:T(8,128)(2,1)S(1)}, bf16[128,3,3,256]{3,0,2,1:T(8,128)(2,1)}, u32[]{:S(2)}) copy-start(bf16[128,3,3,256]{3,0,2,1:T(8,128)(2,1)} %param.5) | copy-start | bytes 1769476
  16.1 5.1 %collective-permute-start.5 = (bf16[1,9,64,256]{3,2,1,0:T(8,128)(2,1)S(1)}, bf16[1,9,64,256]{3,2,1,0:T(8,128)(2,1)S(1)}, u32[]{:S(2)}, u32[]{:S(2)}) collective-permute-start(bf16[1,9,64,256]{3,2,1,0:T(8,128)(2,1)S(1)} %bitcast.50), channel_id=1, source_target_pairs={{0,2},{2,0},{4,6},{6,4},{8,10},{10,8},{12,14},{14,12},{16,18},{18,... | collective-permute-start | bytes 884744 | tf_op jit(solution)/shard_map/ppermute | solution.py:357
  20.4 3.8 %collective-permute-start.6 = (bf16[1,9,64,256]{3,2,1,0:T(8,128)(2,1)S(1)}, bf16[1,9,64,256]{3,2,1,0:T(8,128)(2,1)S(1)}, u32[]{:S(2)}, u32[]{:S(2)}) collective-permute-start(bf16[1,9,64,256]{3,2,1,0:T(8,128)(2,1)S(1)} %bitcast.53), channel_id=1, source_target_pairs={{0,2},{2,0},{4,6},{6,4},{8,10},{10,8},{12,14},{14,12},{16,18},{18,... | collective-permute-start | bytes 884744 | tf_op jit(solution)/shard_map/ppermute | solution.py:357
  20.4 3.7 %copy-start.1 = (bf16[128,3,3,256]{3,0,2,1:T(8,128)(2,1)S(1)}, bf16[128,3,3,256]{3,0,2,1:T(8,128)(2,1)}, u32[]{:S(2)}) copy-start(bf16[128,3,3,256]{3,0,2,1:T(8,128)(2,1)} %param.6) | copy-start | bytes 1769476
  20.4 9.3 %collective-permute-start.7 = (bf16[20,56,128]{2,1,0:T(8,128)(2,1)S(1)}, bf16[20,56,128]{2,1,0:T(8,128)(2,1)S(1)}, u32[]{:S(2)}, u32[]{:S(2)}) collective-permute-start(bf16[20,56,128]{2,1,0:T(8,128)(2,1)S(1)} %get-tuple-element.63), channel_id=1, source_target_pairs={{0,1},{1,0},{2,3},{3,2},{4,5},{5,4},{6,7},{7,6},{8,9},{9,8},{10,11... | collective-permute-start | bytes 860168 | tf_op jit(solution)/shard_map/ppermute | solution.py:342
  33.4 2.6 %collective-permute-start.8 = (bf16[9,256,128]{2,1,0:T(8,128)(2,1)S(1)}, bf16[9,256,128]{2,1,0:T(8,128)(2,1)S(1)}, u32[]{:S(2)}, u32[]{:S(2)}) collective-permute-start(bf16[9,256,128]{2,1,0:T(8,128)(2,1)S(1)} %get-tuple-element.48), channel_id=1, source_target_pairs={{0,2},{2,0},{4,6},{6,4},{8,10},{10,8},{12,14},{14,12},{16,18},{18,... | collective-permute-start | bytes 1769480 | tf_op jit(solution)/shard_map/ppermute | solution.py:274
  35.4 5.0 %collective-permute-start.9 = (bf16[9,256,128]{2,1,0:T(8,128)(2,1)S(1)}, bf16[9,256,128]{2,1,0:T(8,128)(2,1)S(1)}, u32[]{:S(2)}, u32[]{:S(2)}) collective-permute-start(bf16[9,256,128]{2,1,0:T(8,128)(2,1)S(1)} %get-tuple-element.53), channel_id=1, source_target_pairs={{0,2},{2,0},{4,6},{6,4},{8,10},{10,8},{12,14},{14,12},{16,18},{18,... | collective-permute-start | bytes 1769480 | tf_op jit(solution)/shard_map/ppermute | solution.py:274
  36.6 6.8 %collective-permute-start.13 = (bf16[2,9,64,128]{3,2,1,0:T(8,128)(2,1)S(1)}, bf16[2,9,64,128]{3,2,1,0:T(8,128)(2,1)S(1)}, u32[]{:S(2)}, u32[]{:S(2)}) collective-permute-start(bf16[2,9,64,128]{3,2,1,0:T(8,128)(2,1)S(1)} %get-tuple-element.51), channel_id=1, source_target_pairs={{0,1},{1,0},{2,6},{3,7},{4,5},{5,4},{6,2},{7,3},{8,9},{9,8},{10,14... | collective-permute-start | bytes 884744 | tf_op jit(solution)/shard_map/ppermute | solution.py:452
  43.5 6.8 %collective-permute-start.14 = (bf16[9,64,128]{2,1,0:T(8,128)(2,1)S(1)}, bf16[9,64,128]{2,1,0:T(8,128)(2,1)S(1)}, u32[]{:S(2)}, u32[]{:S(2)}) collective-permute-start(bf16[9,64,128]{2,1,0:T(8,128)(2,1)S(1)} %fusion), channel_id=1, source_target_pairs={{0,4},{1,5},{2,3},{3,2},{4,0},{5,1},{6,7},{7,6},{8,12},{9,13},{10,... | collective-permute-start | bytes 442376 | tf_op jit(solution)/shard_map/ppermute | solution.py:455
  45.0 7.0 %collective-permute-start.10 = (bf16[2,9,64,128]{3,2,1,0:T(8,128)(2,1)S(1)}, bf16[2,9,64,128]{3,2,1,0:T(8,128)(2,1)S(1)}, u32[]{:S(2)}, u32[]{:S(2)}) collective-permute-start(bf16[2,9,64,128]{3,2,1,0:T(8,128)(2,1)S(1)} %get-tuple-element.55), channel_id=1, source_target_pairs={{0,1},{1,0},{2,6},{3,7},{4,5},{5,4},{6,2},{7,3},{8,9},{9,8},{10,14... | collective-permute-start | bytes 884744 | tf_op jit(solution)/shard_map/ppermute | solution.py:453
  50.4 5.2 %collective-permute-start.15 = (bf16[9,64,128]{2,1,0:T(8,128)(2,1)S(1)}, bf16[9,64,128]{2,1,0:T(8,128)(2,1)S(1)}, u32[]{:S(2)}, u32[]{:S(2)}) collective-permute-start(bf16[9,64,128]{2,1,0:T(8,128)(2,1)S(1)} %fusion.2), channel_id=1, source_target_pairs={{0,8},{2,18},{4,12},{6,22},{8,0},{10,26},{12,4},{14,30},{16,24},{1... | collective-permute-start | bytes 442376 | tf_op jit(solution)/shard_map/ppermute | solution.py:315
  52.1 6.2 %collective-permute-start.11 = (bf16[9,64,128]{2,1,0:T(8,128)(2,1)S(1)}, bf16[9,64,128]{2,1,0:T(8,128)(2,1)S(1)}, u32[]{:S(2)}, u32[]{:S(2)}) collective-permute-start(bf16[9,64,128]{2,1,0:T(8,128)(2,1)S(1)} %fusion.3), channel_id=1, source_target_pairs={{0,4},{1,5},{2,3},{3,2},{4,0},{5,1},{6,7},{7,6},{8,12},{9,13},{10,... | collective-permute-start | bytes 442376 | tf_op jit(solution)/shard_map/ppermute | solution.py:456
  55.6 9.4 %collective-permute-start.16 = (bf16[9,64,128]{2,1,0:T(8,128)(2,1)S(1)}, bf16[9,64,128]{2,1,0:T(8,128)(2,1)S(1)}, u32[]{:S(2)}, u32[]{:S(2)}) collective-permute-start(bf16[9,64,128]{2,1,0:T(8,128)(2,1)S(1)} %add_convert_fusion.3), channel_id=1, source_target_pairs={{0,16},{2,10},{4,20},{6,14},{8,24},{10,2},{12,28},{14,6},{16,0},{1... | collective-permute-start | bytes 442376 | tf_op jit(solution)/shard_map/ppermute | solution.py:315
  58.3 8.3 %collective-permute-start.19 = (bf16[9,64,128]{2,1,0:T(8,128)(2,1)S(1)}, bf16[9,64,128]{2,1,0:T(8,128)(2,1)S(1)}, u32[]{:S(2)}, u32[]{:S(2)}) collective-permute-start(bf16[9,64,128]{2,1,0:T(8,128)(2,1)S(1)} %fusion.5), channel_id=1, source_target_pairs={{0,8},{2,18},{4,12},{6,22},{8,0},{10,26},{12,4},{14,30},{16,24},{1... | collective-permute-start | bytes 442376 | tf_op jit(solution)/shard_map/ppermute | solution.py:315
  60.2 7.0 %collective-permute-start.12 = (bf16[16,48,128]{2,1,0:T(8,128)(2,1)S(1)}, bf16[16,48,128]{2,1,0:T(8,128)(2,1)S(1)}, u32[]{:S(2)}, u32[]{:S(2)}) collective-permute-start(bf16[16,48,128]{2,1,0:T(8,128)(2,1)S(1)} %get-tuple-element.64), channel_id=1, source_target_pairs={{0,1},{1,0},{2,3},{3,2},{4,5},{5,4},{6,7},{7,6},{8,9},{9,8},{10,11... | collective-permute-start | bytes 589832 | tf_op jit(solution)/shard_map/ppermute | solution.py:342
  65.0 5.2 %collective-permute-start.17 = (bf16[9,64,128]{2,1,0:T(8,128)(2,1)S(1)}, bf16[9,64,128]{2,1,0:T(8,128)(2,1)S(1)}, u32[]{:S(2)}, u32[]{:S(2)}) collective-permute-start(bf16[9,64,128]{2,1,0:T(8,128)(2,1)S(1)} %add_convert_fusion.2), channel_id=1, source_target_pairs={{0,4},{2,6},{4,0},{6,2},{8,12},{10,14},{12,8},{14,10},{16,20},{18,... | collective-permute-start | bytes 442376 | tf_op jit(solution)/shard_map/ppermute | solution.py:477
  66.7 7.7 %collective-permute-start.20 = (bf16[9,64,128]{2,1,0:T(8,128)(2,1)S(1)}, bf16[9,64,128]{2,1,0:T(8,128)(2,1)S(1)}, u32[]{:S(2)}, u32[]{:S(2)}) collective-permute-start(bf16[9,64,128]{2,1,0:T(8,128)(2,1)S(1)} %add_convert_fusion.1), channel_id=1, source_target_pairs={{0,16},{2,10},{4,20},{6,14},{8,24},{10,2},{12,28},{14,6},{16,0},{1... | collective-permute-start | bytes 442376 | tf_op jit(solution)/shard_map/ppermute | solution.py:315
  67.2 9.4 %copy-start.4 = (bf16[16,96,128]{2,1,0:T(8,128)(2,1)}, bf16[16,96,128]{2,1,0:T(8,128)(2,1)S(1)}, u32[]{:S(2)}) copy-start(bf16[16,96,128]{2,1,0:T(8,128)(2,1)S(1)} %constant_dynamic-update-slice_fusion) | copy-start | bytes 1179652
  70.3 4.7 %collective-permute-start.18 = (bf16[9,128,128]{2,1,0:T(8,128)(2,1)S(1)}, bf16[9,128,128]{2,1,0:T(8,128)(2,1)S(1)}, u32[]{:S(2)}, u32[]{:S(2)}) collective-permute-start(bf16[9,128,128]{2,1,0:T(8,128)(2,1)S(1)} %pad_maximum_fusion.1.here), channel_id=1, source_target_pairs={{0,2},{2,0},{4,6},{6,4},{8,10},{10,8},{12,14},{14,12},{16,18},{18,... | collective-permute-start | bytes 884744 | tf_op jit(solution)/shard_map/ppermute | solution.py:321
  74.4 5.2 %collective-permute-start.21 = (bf16[9,64,128]{2,1,0:T(8,128)(2,1)S(1)}, bf16[9,64,128]{2,1,0:T(8,128)(2,1)S(1)}, u32[]{:S(2)}, u32[]{:S(2)}) collective-permute-start(bf16[9,64,128]{2,1,0:T(8,128)(2,1)S(1)} %add_convert_fusion), channel_id=1, source_target_pairs={{0,4},{2,6},{4,0},{6,2},{8,12},{10,14},{12,8},{14,10},{16,20},{18,... | collective-permute-start | bytes 442376 | tf_op jit(solution)/shard_map/ppermute | solution.py:478
  79.7 1.6 %collective-permute-start.22 = (bf16[9,128,128]{2,1,0:T(8,128)(2,1)S(1)}, bf16[9,128,128]{2,1,0:T(8,128)(2,1)S(1)}, u32[]{:S(2)}, u32[]{:S(2)}) collective-permute-start(bf16[9,128,128]{2,1,0:T(8,128)(2,1)S(1)} %pad_maximum_fusion.2.here), channel_id=1, source_target_pairs={{0,2},{2,0},{4,6},{6,4},{8,10},{10,8},{12,14},{14,12},{16,18},{18,... | collective-permute-start | bytes 884744 | tf_op jit(solution)/shard_map/ppermute | solution.py:321

commit v4 on v3

--- a/solution.py
+++ b/solution.py
@@ -16,19 +16,21 @@
 TN = (((0,), (0,)), ((), ()))
 
 
-def call(kernel, outs, args, scratch=(), flops=0, smem_args=1):
-    specs = [pl.BlockSpec(memory_space=pltpu.SMEM)] * smem_args
-    specs += [pl.BlockSpec(memory_space=pltpu.VMEM)] * (len(args) - smem_args)
-
-
+def call(kernel, outs, args, scratch=(), smem_args=1, raw_args=(), raw_outs=(), aliases=None):
+    def spec(space):
+        return pl.BlockSpec(memory_space=space)
+
+    in_specs = [spec(pltpu.SMEM)] * smem_args
+    in_specs += [spec(pltpu.HBM if i in raw_args else pltpu.VMEM) for i in range(smem_args, len(args))]
+    args = [pltpu.with_memory_space_constraint(a, pltpu.HBM) if i in raw_args else a for i, a in enumerate(args)]
     return pl.pallas_call(
         kernel,
         out_shape=[jax.ShapeDtypeStruct(s, t) for s, t in outs],
-        in_specs=specs,
-        out_specs=[pl.BlockSpec(memory_space=pltpu.VMEM)] * len(outs),
+        in_specs=in_specs,
+        out_specs=[spec(pltpu.HBM if i in raw_outs else pltpu.VMEM) for i in range(len(outs))],
         scratch_shapes=list(scratch),
+        input_output_aliases=aliases or {},
         compiler_params=pltpu.CompilerParams(vmem_limit_bytes=VMEM_LIMIT),
-        cost_estimate=pl.CostEstimate(flops=0, bytes_accessed=0, transcendentals=0),
     )(*args)
 
 
@@ -73,17 +75,18 @@
     return out
 
 
-def assemble_filter(w, own, pieces, iy, core, ny):
+def assemble_filter(w, own, pieces, iy, ix, ny):
     co = own.shape[1]
-    half = co // 2
     w[:, pl.ds(pl.multiple_of(iy * co, co), co), :] = own[...]
+    core, x = lax.rem(ix, 2), lax.rem(lax.div(ix, 2), 2)
+    count, size = pieces[0].shape[1], pieces[0].shape[3]
     for d in range(1, ny):
         src = lax.rem(iy - d + ny, ny)
-        mine, other = pieces
-        at = pl.multiple_of(src * co + core * half, half)
-        w[:, pl.ds(at, half), :] = mine[d - 1]
-        at = pl.multiple_of(src * co + (1 - core) * half, half)
-        w[:, pl.ds(at, half), :] = other[d - 1]
+        for p in range(count):
+            part = 0 if count == 1 else (x if p == 0 else 1 - x)
+            for ref, half in ((pieces[0], core), (pieces[1], 1 - core)):
+                at = pl.multiple_of(src * co + half * (co // 2) + part * size, size)
+                w[:, pl.ds(at, size), :] = ref[d - 1, p]
 
 
 def conv1_kernel(dims, where, ft, left, right, up, down, own, mine, other, hidden, slope, fbuf, w):
@@ -104,7 +107,7 @@
             mid = [jnp.concatenate(planes, axis=1)]
         x = jnp.concatenate([before] + mid + [after], axis=0)
         fbuf[c] = jnp.where(ok, x, 0.0).astype(BF16)
-    assemble_filter(w, own, (mine, other), iy, ix % 2, ny)
+    assemble_filter(w, own, (mine, other), iy, ix, ny)
     for c0, n in chunks(wl + 6, 11):
         pre = conv_chunk(fbuf, w, c0, n, False)
         for q in range(n):
@@ -122,7 +125,7 @@
     iy, ix = where[0], where[1]
     rows = hidden.shape[1]
     ok = row_mask(iy * hl, rows, height)
-    assemble_filter(w, own, (mine, other), iy, ix % 2, ny)
+    assemble_filter(w, own, (mine, other), iy, ix, ny)
     for c0, n in chunks(wl + 4, 10):
         pre = conv_chunk(hidden, w, c0, n, False)
         for q in range(n):
@@ -133,6 +136,23 @@
             slope[c] = jnp.where(inside, grad, 0.0)
             if 2 <= c < wl + 2:
                 act_out[c - 2] = act[OFF : OFF + hl].astype(BF16)
+
+
+def cut_kernel(rows_at, where, features, first, second, cot, edge, send1, send2, low, high, sem):
+    iy, ix = where[0], where[1]
+    core = lax.rem(ix, 2)
+    wl, size = features.shape[1], send1.shape[1]
+    at = pl.multiple_of(core * size, size)
+    pairs = [(first.at[:, pl.ds(at, size), :], send1), (second.at[:, pl.ds(at, size), :], send2)]
+    pairs += [(cot.at[0:2], low), (cot.at[wl - 2 : wl], high)]
+    for n, h0 in enumerate(rows_at):
+        h0 = jnp.where(iy == 0, h0[0], h0[1])
+        pairs.append((features.at[pl.ds(h0, HALO)], edge.at[n]))
+    copies = [pltpu.make_async_copy(src, dst, sem.at[n]) for n, (src, dst) in enumerate(pairs)]
+    for copy in copies:
+        copy.start()
+    for copy in copies:
+        copy.wait()
 
 
 def edge_kernel(dims, where, ft, up, down, ct_low, ct_high, low, high):
@@ -146,7 +166,7 @@
             for g in range(groups):
                 at = (g * HALO + q) * tall
                 out[at : at + tall] = x[:, g * 128 : (g + 1) * 128]
-        out[groups * HALO * tall :] = cot[...]
+        out[groups * HALO * tall :] = cot[...].reshape(-1, 128)
 
 
 def own_rows(rows, hl):
@@ -191,7 +211,7 @@
             ]
             parts = [jnp.where(iy == 0, a, b), jnp.where(iy == 0, b, a)]
         outer[c] = (jnp.concatenate(parts, axis=1) * slope2[c]).astype(BF16)
-    assemble_filter(w, own, (mine, other), iy, ix % 2, ny)
+    assemble_filter(w, own, (mine, other), iy, ix, ny)
     for c0, n in chunks(wl + 2, 9):
         grad = conv_chunk(outer, w, c0, n, True)
         for q in range(n):
@@ -214,7 +234,7 @@
 def input_kernel(dims, where, inner, own, mine, other, out, w, flat):
     ny, hl, wl, height, width = dims
     iy, ix = where[0], where[1]
-    assemble_filter(w, own, (mine, other), iy, ix % 2, ny)
+    assemble_filter(w, own, (mine, other), iy, ix, ny)
     for c0, n in chunks(wl, 8):
         grad = conv_chunk(inner, w, c0, n, True)
         for q in range(n):
@@ -246,10 +266,10 @@
 
 
 def finish_kernel(scale, where, here, there, out):
-    low_core = where[1] % 2 == 0
+    low_core = lax.rem(where[1], 2) == 0
+    half = here.shape[2]
     for t in range(here.shape[0]):
         a, b = here[t].astype(F32) * scale, there[t].astype(F32) * scale
-        half = a.shape[1]
         out[t, :, :half] = jnp.where(low_core, a, b)
         out[t, :, half:] = jnp.where(low_core, b, a)
 
@@ -266,17 +286,22 @@
 
     own[...] = block(iy, x)
     other[...] = block(jnp.where(by_y, iy, 1 - iy), jnp.where(by_y, 1 - x, x))
-    send[0] = block(jnp.where(by_y, 1 - iy, iy), jnp.where(by_y, x, 1 - x)).astype(BF16)
-    send[1] = block(1 - iy, 1 - x).astype(BF16)
-
-
-def split_filter(where, keep, send, nx, ny):
-    came = lax.ppermute(send, "gx", [(i, i ^ 1) for i in range(nx)])
+    send[:, :size, :] = block(jnp.where(by_y, 1 - iy, iy), jnp.where(by_y, x, 1 - x)).astype(BF16)
+    send[:, size:, :] = block(1 - iy, 1 - x).astype(BF16)
+
+
+def fold_kernel(own, other, came, total, send):
+    size = own.shape[1]
+    total[...] = own[...] + came[:, :size, :].astype(F32)
+    send[...] = (other[...] + came[:, size:, :].astype(F32)).astype(BF16)
+
+
+def split_filter(where, keep, came, nx, ny):
     blocks = 2 * ny
     taps, ch, half = keep.shape
     shape = (taps, ch // blocks, half)
     if ny == 2:
-        outs = [(shape, F32), (shape, F32), ((2,) + shape, BF16)]
+        outs = [(shape, F32), (shape, F32), ((taps, ch // 2, half), BF16)]
         return call(halving_kernel, outs, (where, keep, came))
     outs = [(shape, F32)] + [(shape, BF16)] * (blocks - 1)
     return call(functools.partial(split_kernel, blocks), outs, (where, keep, came))
@@ -320,8 +345,8 @@
     here = jnp.concatenate([jnp.where(first, total, beside), jnp.where(first, beside, total)], axis=1)
     there = lax.ppermute(here, "gx", [(g, g ^ 1) for g in range(nx)])
     taps, size, half = here.shape
-    (out,) = call(functools.partial(finish_kernel, scale), [((taps, size, 2 * half), F32)], (where, here, there))
-    return jnp.transpose(out.reshape(3, 3, size, 2 * half), (2, 0, 1, 3))
+    (result,) = call(functools.partial(finish_kernel, scale), [((taps, size, 2 * half), F32)], (where, here, there))
+    return jnp.transpose(result.reshape(3, 3, size, 2 * half), (2, 0, 1, 3))
 
 
 def body(features, first_filter, second_filter, cotangent):
@@ -347,42 +372,43 @@
         mine = jnp.stack([round_y(send, d) for d in range(1, ny)])
         return mine, lax.ppermute(mine, "gx", [(i, i ^ 1) for i in range(nx)])
 
-    def halves(taps):
-        return lax.dynamic_slice_in_dim(taps, core * (co // 2), co // 2, 1)
-
-    def spread_y(send):
-        return jnp.stack([round_y(send, d) for d in range(1, ny)])
-
     def pass_core(mine):
         return lax.ppermute(mine, "gx", [(i, i ^ 1) for i in range(nx)])
 
-    if ny == 2:
-        row_send = lax.dynamic_slice_in_dim(features, jnp.where(iy == 0, hl - HALO, 0), HALO, 0)
-        up = down = jnp.transpose(round_y(row_send, 1), (1, 0, 2))
-    else:
-        row_send = (features[hl - HALO :], features[:HALO])
-        up = jnp.transpose(round_y(row_send[0], 1), (1, 0, 2))
-        down = jnp.transpose(round_y(row_send[1], ny - 1), (1, 0, 2))
-
     first_own = jnp.transpose(first_filter, (1, 2, 0, 3)).reshape(9, co, ch)
     second_own = jnp.transpose(second_filter, (1, 2, 0, 3)).reshape(9, co, ch)
-    first_mine = spread_y(halves(after(first_own, row_send)))
-
-    ft = jnp.transpose(after(features, row_send), (1, 0, 2))
     ct = jnp.transpose(cotangent, (1, 2, 0))
     groups, tall = ch // 128, hl + 2 * HALO
+
+    half = co // 2
+    rows_at = [(hl - HALO, 0)] if ny == 2 else [(hl - HALO, hl - HALO), (0, 0)]
+    edge_send, first_send, second_send, ct_low, ct_high = call(
+        functools.partial(cut_kernel, rows_at),
+        [((len(rows_at), HALO, wl, ch), BF16)] + [((9, half, ch), BF16)] * 2 + [((2, height, co), BF16)] * 2,
+        (where, features, first_own, second_own, ct),
+        [pltpu.SemaphoreType.DMA((4 + len(rows_at),))],
+        raw_args=(1, 2, 3, 4),
+    )
+    up = jnp.transpose(round_y(edge_send[0], 1), (1, 0, 2))
+    down = up if ny == 2 else jnp.transpose(round_y(edge_send[1], ny - 1), (1, 0, 2))
+
+    def spread_y(send):
+        return jnp.stack([round_y(send, d) for d in range(1, ny)])[:, None]
+
+    first_mine = spread_y(first_send)
+
+    ft = jnp.transpose(after(features, edge_send), (1, 0, 2))
     at = groups * HALO * tall
     shape = ((at + 2 * height * co // 128, 128), BF16)
-    low, high = call(
-        functools.partial(edge_kernel, dims),
-        [shape] * 2,
-        (where, ft, up, down, ct[:2].reshape(-1, 128), ct[wl - 2 :].reshape(-1, 128)),
-    )
+    if co % 128:
+        ct_low, ct_high = ct_low.reshape(-1, 128), ct_high.reshape(-1, 128)
+    low, high = call(functools.partial(edge_kernel, dims), [shape] * 2, (where, ft, up, down, ct_low, ct_high))
     left = lax.ppermute(high, "gx", forward)
     right = lax.ppermute(low, "gx", backward)
     first_mine = after(first_mine, left, right)
     first_in = (first_mine, pass_core(first_mine))
-    second_mine = spread_y(halves(after(second_own, up)))
+    second_mine = spread_y(after(second_send, low))
+    second_in = (second_mine, pass_core(second_mine))
 
     ct = jnp.concatenate([left[at:].reshape(2, height, co), ct, right[at:].reshape(2, height, co)], axis=0)
     if ny == 2:
@@ -402,7 +428,6 @@
 
     bf = lambda *s: pltpu.VMEM(s, BF16)
     weights = bf(9, ch, ch)
-    tap_flops = 2 * 9 * ch * ch * rows
 
     fbuf_shape = ((wl + 8, rows, ch), BF16)
     hidden, slope1, fbuf = call(
@@ -410,15 +435,12 @@
         [((wl + 6, rows, ch), BF16), ((wl + 2, rows, ch), F32), fbuf_shape],
         (where, ft, left, right, up, down, first_own, *first_in),
         [weights],
-        tap_flops * (wl + 6),
-    )
-    second_in = (second_mine, pass_core(second_mine))
+    )
     act, slope2 = call(
         functools.partial(conv2_kernel, dims),
         [((wl, hl, ch), BF16), ((wl + 4, rows, ch), F32)],
         (where, hidden, second_own, *second_in),
         [weights],
-        tap_flops * (wl + 4),
     )
     grad_shapes = [((9, ch, ch // 2), F32), ((9, ch, ch // 2), BF16)]
     shifted = bf(wl * rows, 3 * ch)
@@ -427,24 +449,20 @@
         [((wl + 2, rows, ch), BF16), ((wl + 4, rows, ch), BF16)] + grad_shapes,
         (where, second_own, *second_in, slope2, slope1, fbuf, *cots),
         [weights, shifted],
-        tap_flops * (2 * wl + 2),
     )
     keep2, send2 = call(
         functools.partial(second_grad_kernel, dims),
         grad_shapes,
         (where, hidden, outer),
         [shifted],
-        tap_flops * wl,
-    )
-    parts1 = split_filter(where, keep1, send1, nx, ny)
-    keep2 = after(keep2, parts1)
-    parts2 = split_filter(where, keep2, send2, nx, ny)
+    )
+    parts1 = split_filter(where, keep1, pass_core(send1), nx, ny)
+    parts2 = split_filter(where, after(keep2, parts1), pass_core(send2), nx, ny)
     (input_grad,) = call(
         functools.partial(input_kernel, dims),
         [((hl, wl, ch), BF16)],
         (where, inner, first_own, *first_in),
         [weights, pltpu.VMEM((ch // 128, hl * wl, 128), F32)],
-        tap_flops * wl,
     )
     if ny == 2:
         (own1, other1, send1), (own2, other2, send2) = parts1, parts2
@@ -452,8 +470,11 @@
         came1 = lax.ppermute(send1, axes, pairs[0])
         came2 = lax.ppermute(send2, axes, pairs[0])
         came1 = after(came1, parts2, input_grad)
-        total1 = add([own1, came1[0], lax.ppermute(add([other1, came1[1]]), axes, pairs[1])])
-        total2 = add([own2, came2[0], lax.ppermute(add([other2, came2[1]]), axes, pairs[1])])
+        shape = own1.shape
+        own1, pass1 = call(fold_kernel, [(shape, F32), (shape, BF16)], (own1, other1, came1), smem_args=0)
+        own2, pass2 = call(fold_kernel, [(shape, F32), (shape, BF16)], (own2, other2, came2), smem_args=0)
+        total1 = add([own1, lax.ppermute(pass1, axes, pairs[1])])
+        total2 = add([own2, lax.ppermute(pass2, axes, pairs[1])])
     else:
         total1 = add([after(parts1[0], parts2, input_grad)] + send_planes(parts1, nx, ny))
         total2 = add([parts2[0]] + send_planes(parts2, nx, ny))
@@ -477,7 +498,7 @@
     beside1 = lax.ppermute(total1, "gx", [(g, g ^ 2) for g in range(nx)])
     beside2 = lax.ppermute(total2, "gx", [(g, g ^ 2) for g in range(nx)])
     first_grad = finish(where, total1, beside1, nx, ix, scale_factor)
-    second_grad = finish(where, total2, after(beside2, first_grad), nx, ix, scale_factor)
+    second_grad = finish(where, total2, beside2, nx, ix, scale_factor)
     return output, input_grad, first_grad, second_grad
 
 

time: 83.3 us -> 77.1 us (0.926)
  waiting for transfers between devices: 30.4 us -> 18.3 us
  starting transfers between devices: 27.4 us -> 34.9 us
  local copies, waits for them, and re-layouts: 4.09 us -> 0.42 us
  Pallas kernels: 19.5 us -> 21.3 us
    ppermute x4, waiting for transfers between devices: 10.1 us -> 2.91 us  [far_partner(): lax.ppermute(total, 'gx', [(g, g ^ (near if g % 2 == 0 else far)) for g i...]
    ppermute x4 -> x2, waiting for transfers between devices: 4.57 us -> 1.44 us  [the longest x1 1.44 us: body(): total2 = add([own2, lax.ppermute(pass2, axes, pairs[1])])]
    ppermute x4, starting transfers between devices: 6.41 us -> 9.33 us  [far_partner(): lax.ppermute(total, 'gx', [(g, g ^ (near if g % 2 == 0 else far)) for g i...]
    dynamic_slice x3 -> x0, local copies, waits for them, and re-layouts: 2.79 us -> none  [the longest x2 1.97 us: halves(): return lax.dynamic_slice_in_dim(taps, core * (co // 2), co // 2, 1)]
    ppermute x1, waiting for transfers between devices: 3.02 us -> 0.5 us  [body(): beside1 = lax.ppermute(total1, 'gx', [(g, g ^ 2) for g in range(nx)])]
    ppermute x1, waiting for transfers between devices: 0.01 us -> 1.85 us  [body(): came2 = lax.ppermute(send2, axes, pairs[0])]
    pallas_call x10 -> x13, Pallas kernels: 19.5 us -> 21.3 us  [call(): pl.pallas_call(kernel, out_shape=[jax.ShapeDtypeStruct(s, t) for s, t in...]
    ppermute x2, waiting for transfers between devices: 1.57 us -> 0.01 us  [finish(): there = lax.ppermute(here, 'gx', [(g, g ^ 1) for g in range(nx)])]
  transfers between devices with their start and end apart: 23 -> 23, of which waited for: 11 -> 13; matrix products, arithmetic and copies ran while one was open for 5% -> 1% of each run, Pallas kernels for 17% -> 19%
where the time goes in v4:
time: 77.1 us; the launch traced here: 76.3 us
  starting transfers between devices  34.9 us (45%)
  Pallas kernels  21.3 us (28%)
  waiting for transfers between devices  18.3 us (24%)
  between operations  0.96 us (1%)
    pallas_call x13, Pallas kernels, call(): pl.pallas_call(kernel, out_shape=[jax.ShapeDtypeStruct(s, t) for s, t in...  21.3 us
    ppermute x4, starting transfers between devices, far_partner(): lax.ppermute(total, 'gx', [(g, g ^ (near if g % 2 == 0 else far)) for g i...  9.33 us
    ppermute x5, starting transfers between devices, round_y(): return lax.ppermute(x, 'gy', [(i, (i + d) % ny) for i in range(ny)])  7.39 us
    ppermute x5, waiting for transfers between devices, round_y(): return lax.ppermute(x, 'gy', [(i, (i + d) % ny) for i in range(ny)])  6.3 us
    ppermute x1, waiting for transfers between devices, body(): beside2 = lax.ppermute(total2, 'gx', [(g, g ^ 2) for g in range(nx)])  3.41 us
    ppermute x1, starting transfers between devices, body(): beside1 = lax.ppermute(total1, 'gx', [(g, g ^ 2) for g in range(nx)])  3.1 us
    ppermute x4, starting transfers between devices, pass_core(): return lax.ppermute(mine, 'gx', [(i, i ^ 1) for i in range(nx)])  3.04 us
    ppermute x1, starting transfers between devices, body(): left = lax.ppermute(high, 'gx', forward)  3.04 us
  transfers between devices with their start and end apart: 23, of which 13 were waited for; matrix products, arithmetic and copies ran while one was open for 1% of the time, Pallas kernels for 19%

profile of v4, /device:TPU:0, one launch (start us, length us, event | category | flops | bytes accessed | tf_op | source)
XLA Modules:
  0.0 76.3 jit_solution(12474522359970079580)
XLA Ops:
  0.7 1.6 %shard_map.75 = (bf16[1,4,16,256]{3,2,1,0:T(8,128)(2,1)S(1)}, bf16[9,64,256]{2,1,0:T(8,128)(2,1)S(1)}, bf16[9,64,256]{2,1,0:T(8,128)(2,1)S(1)}, bf16[2,96,128]{2,1,0:T(8,128)(2,1)S(1)}, bf16[2,96,128]{2,1,0:T(8,128)(2,1)S(1)}) custom-call(s32[2]{0:T(128)S(1)} %pad_add_fusion.where, bf16[48,16,256]{2,1,0:T(8,128)(2,1)} %features.1, ...), custom_call_target="tpu_custom_call" | custom-call | tf_op jit(solution)/shard_map/pallas_call | solution.py:26
  2.4 3.0 %collective-permute-start = (bf16[4,16,256]{2,0,1:T(4,128)(2,1)S(1)}, bf16[4,16,256]{2,0,1:T(4,128)(2,1)S(1)}, u32[]{:S(2)}, u32[]{:S(2)}) collective-permute-start(bf16[4,16,256]{2,0,1:T(4,128)(2,1)S(1)} %bitcast.52), channel_id=1, source_target_pairs={{0,1},{1,0},{2,3},{3,2},{4,5},{5,4},{6,7},{7,6},{8,9},{9,8},{10,11... | collective-permute-start | bytes 98312 | tf_op jit(solution)/shard_map/ppermute | solution.py:367
  5.7 1.7 %collective-permute-done = bf16[4,16,256]{2,0,1:T(4,128)(2,1)S(1)} collective-permute-done((bf16[4,16,256]{2,0,1:T(4,128)(2,1)S(1)}, bf16[4,16,256]{2,0,1:T(4,128)(2,1)S(1)}, u32[]{:S(2)}, u32[]{:S(2)}) %collective-permute-start) | collective-permute-done | bytes 32800 | tf_op jit(solution)/shard_map/ppermute | solution.py:367
  7.9 2.4 %collective-permute-start.3 = (bf16[9,64,256]{2,1,0:T(8,128)(2,1)S(1)}, bf16[9,64,256]{2,1,0:T(8,128)(2,1)S(1)}, u32[]{:S(2)}, u32[]{:S(2)}) collective-permute-start(bf16[9,64,256]{2,1,0:T(8,128)(2,1)S(1)} %get-tuple-element.47), channel_id=1, source_target_pairs={{0,1},{1,0},{2,3},{3,2},{4,5},{5,4},{6,7},{7,6},{8,9},{9,8},{10,11... | collective-permute-start | bytes 884744 | tf_op jit(solution)/shard_map/ppermute | solution.py:367
  10.4 1.3 %collective-permute-start.2 = (bf16[640,128]{1,0:T(8,128)(2,1)S(1)}, bf16[640,128]{1,0:T(8,128)(2,1)S(1)}, u32[]{:S(2)}, u32[]{:S(2)}) collective-permute-start(bf16[640,128]{1,0:T(8,128)(2,1)S(1)} %get-tuple-element.45), channel_id=1, source_target_pairs={{2,0},{4,2},{6,4},{8,6},{10,8},{12,10},{14,12},{16,14},{18,16},{20... | collective-permute-start | bytes 491528 | tf_op jit(solution)/shard_map/ppermute | solution.py:407
  11.7 3.0 %collective-permute-start.1 = (bf16[640,128]{1,0:T(8,128)(2,1)S(1)}, bf16[640,128]{1,0:T(8,128)(2,1)S(1)}, u32[]{:S(2)}, u32[]{:S(2)}) collective-permute-start(bf16[640,128]{1,0:T(8,128)(2,1)S(1)} %get-tuple-element.44), channel_id=1, source_target_pairs={{0,2},{2,4},{4,6},{6,8},{8,10},{10,12},{12,14},{14,16},{16,18},{18... | collective-permute-start | bytes 491528 | tf_op jit(solution)/shard_map/ppermute | solution.py:406
  14.8 0.9 %collective-permute-done.1.left = bf16[640,128]{1,0:T(8,128)(2,1)S(1)} collective-permute-done((bf16[640,128]{1,0:T(8,128)(2,1)S(1)}, bf16[640,128]{1,0:T(8,128)(2,1)S(1)}, u32[]{:S(2)}, u32[]{:S(2)}) %collective-permute-start.1) | collective-permute-done | bytes 163872 | tf_op jit(solution)/shard_map/ppermute | solution.py:406
  15.8 2.4 %collective-permute-start.5 = (bf16[1,1,9,64,256]{4,3,2,1,0:T(8,128)(2,1)S(1)}, bf16[1,1,9,64,256]{4,3,2,1,0:T(8,128)(2,1)S(1)}, u32[]{:S(2)}, u32[]{:S(2)}) collective-permute-start(bf16[1,1,9,64,256]{4,3,2,1,0:T(8,128)(2,1)S(1)} %bitcast.35), channel_id=1, source_target_pairs={{0,2},{2,0},{4,6},{6,4},{8,10},{10,8},{12,14},{14,12},{16,18},{18,... | collective-permute-start | bytes 884744 | tf_op jit(solution)/shard_map/ppermute | solution.py:376
  18.2 2.0 %collective-permute-done.3 = bf16[9,64,256]{2,1,0:T(8,128)(2,1)S(1)} collective-permute-done((bf16[9,64,256]{2,1,0:T(8,128)(2,1)S(1)}, bf16[9,64,256]{2,1,0:T(8,128)(2,1)S(1)}, u32[]{:S(2)}, u32[]{:S(2)}) %collective-permute-start.3) | collective-permute-done | bytes 294944 | tf_op jit(solution)/shard_map/ppermute | solution.py:367
  20.3 1.0 %collective-permute-start.7 = (bf16[20,56,128]{2,1,0:T(8,128)(2,1)S(1)}, bf16[20,56,128]{2,1,0:T(8,128)(2,1)S(1)}, u32[]{:S(2)}, u32[]{:S(2)}) collective-permute-start(bf16[20,56,128]{2,1,0:T(8,128)(2,1)S(1)} %get-tuple-element.77), channel_id=1, source_target_pairs={{0,1},{1,0},{2,3},{3,2},{4,5},{5,4},{6,7},{7,6},{8,9},{9,8},{10,11... | collective-permute-start | bytes 860168 | tf_op jit(solution)/shard_map/ppermute | solution.py:367
  21.4 2.9 %shard_map.77 = (bf16[22,64,256]{2,1,0:T(8,128)(2,1)S(1)}, f32[18,64,256]{2,1,0:T(8,128)S(1)}, bf16[24,64,256]{2,1,0:T(8,128)(2,1)S(1)}) custom-call(s32[2]{0:T(128)S(1)} %pad_add_fusion.where, bf16[16,48,256]{2,1,0:T(8,128)(2,1)S(1)} %bitcast.34, bf16[640,128]{1,0:T(8,128)(2,1)S(1)} %collective-permute-done.1.left, ...), custom_call_target="tpu_custom_call" | custom-call | tf_op jit(solution)/shard_map/pallas_call | solution.py:26
  24.4 2.7 %shard_map.78 = (bf16[16,48,256]{2,1,0:T(8,128)(2,1)S(1)}, f32[20,64,256]{2,1,0:T(8,128)S(1)}) custom-call(s32[2]{0:T(128)S(1)} %pad_add_fusion.where, bf16[22,64,256]{2,1,0:T(8,128)(2,1)S(1)} %get-tuple-element.51.hidden, bf16[9,128,256]{2,1,0:T(8,128)(2,1)S(1)} %bitcast.31, bf16[1,1,9,64,256]{4,3,2,1,0:T(8,128)(2,1)S(1)} %bitcast.39, ...), custom_call_target="tpu_custom_call" | custom-call | tf_op jit(solution)/shard_map/pallas_call | solution.py:26
  27.0 2.6 %collective-permute-done.7.refs_1_ = bf16[20,56,128]{2,1,0:T(8,128)(2,1)S(1)} collective-permute-done((bf16[20,56,128]{2,1,0:T(8,128)(2,1)S(1)}, bf16[20,56,128]{2,1,0:T(8,128)(2,1)S(1)}, u32[]{:S(2)}, u32[]{:S(2)}) %collective-permute-start.7) | collective-permute-done | bytes 286752 | tf_op jit(solution)/shard_map/ppermute | solution.py:367
  29.6 3.6 %shard_map.79 = (bf16[18,64,256]{2,1,0:T(8,128)(2,1)S(1)}, bf16[20,64,256]{2,1,0:T(8,128)(2,1)S(1)}, f32[9,256,128]{2,1,0:T(8,128)S(1)}, bf16[9,256,128]{2,1,0:T(8,128)(2,1)S(1)}) custom-call(s32[2]{0:T(128)S(1)} %pad_add_fusion.where, bf16[9,128,256]{2,1,0:T(8,128)(2,1)S(1)} %bitcast.32, bf16[1,1,9,64,256]{4,3,2,1,0:T(8,128)(2,1)S(1)} %bitcast.40, ...), custom_call_target="tpu_custom_call" | custom-call | tf_op jit(solution)/shard_map/pallas_call | solution.py:26
  33.3 2.0 %shard_map.80 = (f32[9,256,128]{2,1,0:T(8,128)S(1)}, bf16[9,256,128]{2,1,0:T(8,128)(2,1)S(1)}) custom-call(s32[2]{0:T(128)S(1)} %pad_add_fusion.where, bf16[22,64,256]{2,1,0:T(8,128)(2,1)S(1)} %get-tuple-element.51.hidden, bf16[20,64,256]{2,1,0:T(8,128)(2,1)S(1)} %get-tuple-element.56.outer), custom_call_target="tpu_custom_call" | custom-call | tf_op jit(solution)/shard_map/pallas_call | solution.py:26
  36.5 1.0 %collective-permute-start.13 = (bf16[9,128,128]{2,1,0:T(8,128)(2,1)S(1)}, bf16[9,128,128]{2,1,0:T(8,128)(2,1)S(1)}, u32[]{:S(2)}, u32[]{:S(2)}) collective-permute-start(bf16[9,128,128]{2,1,0:T(8,128)(2,1)S(1)} %get-tuple-element.62), channel_id=1, source_target_pairs={{0,1},{1,0},{2,6},{3,7},{4,5},{5,4},{6,2},{7,3},{8,9},{9,8},{10,14... | collective-permute-start | bytes 884744 | tf_op jit(solution)/shard_map/ppermute | solution.py:470
  38.2 1.1 %collective-permute-start.10 = (bf16[9,128,128]{2,1,0:T(8,128)(2,1)S(1)}, bf16[9,128,128]{2,1,0:T(8,128)(2,1)S(1)}, u32[]{:S(2)}, u32[]{:S(2)}) collective-permute-start(bf16[9,128,128]{2,1,0:T(8,128)(2,1)S(1)} %get-tuple-element.67), channel_id=1, source_target_pairs={{0,1},{1,0},{2,6},{3,7},{4,5},{5,4},{6,2},{7,3},{8,9},{9,8},{10,14... | collective-permute-start | bytes 884744 | tf_op jit(solution)/shard_map/ppermute | solution.py:471
  39.3 3.1 %shard_map.84 = bf16[48,16,256]{2,1,0:T(8,128)(2,1)} custom-call(s32[2]{0:T(128)S(1)} %pad_add_fusion.where, bf16[18,64,256]{2,1,0:T(8,128)(2,1)S(1)} %get-tuple-element.71.inner, bf16[9,128,256]{2,1,0:T(8,128)(2,1)S(1)} %bitcast.29, bf16[1,1,9,64,256]{4,3,2,1,0:T(8,128)(2,1)S(1)} %bitcast.37, bf16[1,1,9,64,256]{4,3,2,1,0:T(8,128)(2,1)S(1)} %collective-permute-done.5.other), custom_call_target="tpu_custom_call" | custom-call | tf_op jit(solution)/shard_map/pallas_call | solution.py:26
  43.4 1.8 %collective-permute-start.14 = (bf16[9,64,128]{2,1,0:T(8,128)(2,1)S(1)}, bf16[9,64,128]{2,1,0:T(8,128)(2,1)S(1)}, u32[]{:S(2)}, u32[]{:S(2)}) collective-permute-start(bf16[9,64,128]{2,1,0:T(8,128)(2,1)S(1)} %get-tuple-element.74), channel_id=1, source_target_pairs={{0,4},{1,5},{2,3},{3,2},{4,0},{5,1},{6,7},{7,6},{8,12},{9,13},{10,... | collective-permute-start | bytes 442376 | tf_op jit(solution)/shard_map/ppermute | solution.py:476
  45.2 1.9 %collective-permute-done.10.came = bf16[9,128,128]{2,1,0:T(8,128)(2,1)S(1)} collective-permute-done((bf16[9,128,128]{2,1,0:T(8,128)(2,1)S(1)}, bf16[9,128,128]{2,1,0:T(8,128)(2,1)S(1)}, u32[]{:S(2)}, u32[]{:S(2)}) %collective-permute-start.10) | collective-permute-done | bytes 294944 | tf_op jit(solution)/shard_map/ppermute | solution.py:471
  47.1 2.5 %collective-permute-start.11 = (bf16[9,64,128]{2,1,0:T(8,128)(2,1)S(1)}, bf16[9,64,128]{2,1,0:T(8,128)(2,1)S(1)}, u32[]{:S(2)}, u32[]{:S(2)}) collective-permute-start(bf16[9,64,128]{2,1,0:T(8,128)(2,1)S(1)} %get-tuple-element.69), channel_id=1, source_target_pairs={{0,4},{1,5},{2,3},{3,2},{4,0},{5,1},{6,7},{7,6},{8,12},{9,13},{10,... | collective-permute-start | bytes 442376 | tf_op jit(solution)/shard_map/ppermute | solution.py:477
  49.6 1.6 %collective-permute-start.15 = (bf16[9,64,128]{2,1,0:T(8,128)(2,1)S(1)}, bf16[9,64,128]{2,1,0:T(8,128)(2,1)S(1)}, u32[]{:S(2)}, u32[]{:S(2)}) collective-permute-start(bf16[9,64,128]{2,1,0:T(8,128)(2,1)S(1)} %add_convert_fusion.4), channel_id=1, source_target_pairs={{0,8},{2,18},{4,12},{6,22},{8,0},{10,26},{12,4},{14,30},{16,24},{1... | collective-permute-start | bytes 442376 | tf_op jit(solution)/shard_map/ppermute | solution.py:340
  51.2 1.4 %collective-permute-done.11 = bf16[9,64,128]{2,1,0:T(8,128)(2,1)S(1)} collective-permute-done((bf16[9,64,128]{2,1,0:T(8,128)(2,1)S(1)}, bf16[9,64,128]{2,1,0:T(8,128)(2,1)S(1)}, u32[]{:S(2)}, u32[]{:S(2)}) %collective-permute-start.11) | collective-permute-done | bytes 147488 | tf_op jit(solution)/shard_map/ppermute | solution.py:477
  52.7 1.8 %collective-permute-start.19 = (bf16[9,64,128]{2,1,0:T(8,128)(2,1)S(1)}, bf16[9,64,128]{2,1,0:T(8,128)(2,1)S(1)}, u32[]{:S(2)}, u32[]{:S(2)}) collective-permute-start(bf16[9,64,128]{2,1,0:T(8,128)(2,1)S(1)} %add_convert_fusion.5), channel_id=1, source_target_pairs={{0,8},{2,18},{4,12},{6,22},{8,0},{10,26},{12,4},{14,30},{16,24},{1... | collective-permute-start | bytes 442376 | tf_op jit(solution)/shard_map/ppermute | solution.py:340
  55.5 3.3 %collective-permute-start.16 = (bf16[9,64,128]{2,1,0:T(8,128)(2,1)S(1)}, bf16[9,64,128]{2,1,0:T(8,128)(2,1)S(1)}, u32[]{:S(2)}, u32[]{:S(2)}) collective-permute-start(bf16[9,64,128]{2,1,0:T(8,128)(2,1)S(1)} %add_convert_fusion.3), channel_id=1, source_target_pairs={{0,16},{2,10},{4,20},{6,14},{8,24},{10,2},{12,28},{14,6},{16,0},{1... | collective-permute-start | bytes 442376 | tf_op jit(solution)/shard_map/ppermute | solution.py:340
  59.5 2.6 %collective-permute-start.20 = (bf16[9,64,128]{2,1,0:T(8,128)(2,1)S(1)}, bf16[9,64,128]{2,1,0:T(8,128)(2,1)S(1)}, u32[]{:S(2)}, u32[]{:S(2)}) collective-permute-start(bf16[9,64,128]{2,1,0:T(8,128)(2,1)S(1)} %add_convert_fusion.1), channel_id=1, source_target_pairs={{0,16},{2,10},{4,20},{6,14},{8,24},{10,2},{12,28},{14,6},{16,0},{1... | collective-permute-start | bytes 442376 | tf_op jit(solution)/shard_map/ppermute | solution.py:340
  62.6 3.1 %collective-permute-start.17 = (bf16[9,64,128]{2,1,0:T(8,128)(2,1)S(1)}, bf16[9,64,128]{2,1,0:T(8,128)(2,1)S(1)}, u32[]{:S(2)}, u32[]{:S(2)}) collective-permute-start(bf16[9,64,128]{2,1,0:T(8,128)(2,1)S(1)} %add_convert_fusion.2), channel_id=1, source_target_pairs={{0,4},{2,6},{4,0},{6,2},{8,12},{10,14},{12,8},{14,10},{16,20},{18,... | collective-permute-start | bytes 442376 | tf_op jit(solution)/shard_map/ppermute | solution.py:498
  65.7 1.8 %collective-permute-done.20 = bf16[9,64,128]{2,1,0:T(8,128)(2,1)S(1)} collective-permute-done((bf16[9,64,128]{2,1,0:T(8,128)(2,1)S(1)}, bf16[9,64,128]{2,1,0:T(8,128)(2,1)S(1)}, u32[]{:S(2)}, u32[]{:S(2)}) %collective-permute-start.20) | collective-permute-done | bytes 147488 | tf_op jit(solution)/shard_map/ppermute | solution.py:340
  67.6 1.2 %collective-permute-start.21 = (bf16[9,64,128]{2,1,0:T(8,128)(2,1)S(1)}, bf16[9,64,128]{2,1,0:T(8,128)(2,1)S(1)}, u32[]{:S(2)}, u32[]{:S(2)}) collective-permute-start(bf16[9,64,128]{2,1,0:T(8,128)(2,1)S(1)} %add_convert_fusion), channel_id=1, source_target_pairs={{0,4},{2,6},{4,0},{6,2},{8,12},{10,14},{12,8},{14,10},{16,20},{18,... | collective-permute-start | bytes 442376 | tf_op jit(solution)/shard_map/ppermute | solution.py:499
  69.4 3.4 %collective-permute-done.21 = bf16[9,64,128]{2,1,0:T(8,128)(2,1)S(1)} collective-permute-done((bf16[9,64,128]{2,1,0:T(8,128)(2,1)S(1)}, bf16[9,64,128]{2,1,0:T(8,128)(2,1)S(1)}, u32[]{:S(2)}, u32[]{:S(2)}) %collective-permute-start.21) | collective-permute-done | bytes 147488 | tf_op jit(solution)/shard_map/ppermute | solution.py:499
  73.0 1.7 %shard_map.86 = f32[9,128,256]{2,1,0:T(8,128)} custom-call(s32[2]{0:T(128)S(1)} %pad_add_fusion.where, bf16[9,128,128]{2,1,0:T(8,128)(2,1)S(1)} %pad_maximum_fusion.1.here, bf16[9,128,128]{2,1,0:T(8,128)(2,1)S(1)} %collective-permute-done.18.there), custom_call_target="tpu_custom_call" | custom-call | tf_op jit(solution)/shard_map/pallas_call | solution.py:26
  74.6 1.7 %shard_map.87 = f32[9,128,256]{2,1,0:T(8,128)} custom-call(s32[2]{0:T(128)S(1)} %pad_add_fusion.where, bf16[9,128,128]{2,1,0:T(8,128)(2,1)S(1)} %pad_maximum_fusion.2.here, bf16[9,128,128]{2,1,0:T(8,128)(2,1)S(1)} %collective-permute-done.22.there), custom_call_target="tpu_custom_call" | custom-call | tf_op jit(solution)/shard_map/pallas_call | solution.py:26
  (57 shorter events, 7.0 us)
Async XLA Ops:
  0.6 4.9 %copy-start.2 = (bf16[48,16,256]{2,1,0:T(8,128)(2,1)S(1)}, bf16[48,16,256]{2,1,0:T(8,128)(2,1)}, u32[]{:S(2)}) copy-start(bf16[48,16,256]{2,1,0:T(8,128)(2,1)} %features.1) | copy-start | bytes 1179652
  2.4 13.4 %copy-start.3 = (bf16[128,16,96]{0,2,1:T(8,128)(2,1)S(1)}, bf16[128,16,96]{0,2,1:T(8,128)(2,1)}, u32[]{:S(2)}) copy-start(bf16[128,16,96]{0,2,1:T(8,128)(2,1)} %param.7) | copy-start | bytes 1179652
  2.4 4.9 %collective-permute-start = (bf16[4,16,256]{2,0,1:T(4,128)(2,1)S(1)}, bf16[4,16,256]{2,0,1:T(4,128)(2,1)S(1)}, u32[]{:S(2)}, u32[]{:S(2)}) collective-permute-start(bf16[4,16,256]{2,0,1:T(4,128)(2,1)S(1)} %bitcast.52), channel_id=1, source_target_pairs={{0,1},{1,0},{2,3},{3,2},{4,5},{5,4},{6,7},{7,6},{8,9},{9,8},{10,11... | collective-permute-start | bytes 98312 | tf_op jit(solution)/shard_map/ppermute | solution.py:367
  5.4 10.4 %collective-permute-start.4 = (bf16[9,64,256]{2,1,0:T(8,128)(2,1)S(1)}, bf16[9,64,256]{2,1,0:T(8,128)(2,1)S(1)}, u32[]{:S(2)}, u32[]{:S(2)}) collective-permute-start(bf16[9,64,256]{2,1,0:T(8,128)(2,1)S(1)} %get-tuple-element.49), channel_id=1, source_target_pairs={{0,1},{1,0},{2,3},{3,2},{4,5},{5,4},{6,7},{7,6},{8,9},{9,8},{10,11... | collective-permute-start | bytes 884744 | tf_op jit(solution)/shard_map/ppermute | solution.py:367
  7.9 12.3 %collective-permute-start.3 = (bf16[9,64,256]{2,1,0:T(8,128)(2,1)S(1)}, bf16[9,64,256]{2,1,0:T(8,128)(2,1)S(1)}, u32[]{:S(2)}, u32[]{:S(2)}) collective-permute-start(bf16[9,64,256]{2,1,0:T(8,128)(2,1)S(1)} %get-tuple-element.47), channel_id=1, source_target_pairs={{0,1},{1,0},{2,3},{3,2},{4,5},{5,4},{6,7},{7,6},{8,9},{9,8},{10,11... | collective-permute-start | bytes 884744 | tf_op jit(solution)/shard_map/ppermute | solution.py:367
  10.4 4.4 %collective-permute-start.2 = (bf16[640,128]{1,0:T(8,128)(2,1)S(1)}, bf16[640,128]{1,0:T(8,128)(2,1)S(1)}, u32[]{:S(2)}, u32[]{:S(2)}) collective-permute-start(bf16[640,128]{1,0:T(8,128)(2,1)S(1)} %get-tuple-element.45), channel_id=1, source_target_pairs={{2,0},{4,2},{6,4},{8,6},{10,8},{12,10},{14,12},{16,14},{18,16},{20... | collective-permute-start | bytes 491528 | tf_op jit(solution)/shard_map/ppermute | solution.py:407
  11.7 4.0 %collective-permute-start.1 = (bf16[640,128]{1,0:T(8,128)(2,1)S(1)}, bf16[640,128]{1,0:T(8,128)(2,1)S(1)}, u32[]{:S(2)}, u32[]{:S(2)}) collective-permute-start(bf16[640,128]{1,0:T(8,128)(2,1)S(1)} %get-tuple-element.44), channel_id=1, source_target_pairs={{0,2},{2,4},{4,6},{6,8},{8,10},{10,12},{12,14},{14,16},{16,18},{18... | collective-permute-start | bytes 491528 | tf_op jit(solution)/shard_map/ppermute | solution.py:406
  14.7 6.6 %copy-start = (bf16[128,3,3,256]{3,0,2,1:T(8,128)(2,1)S(1)}, bf16[128,3,3,256]{3,0,2,1:T(8,128)(2,1)}, u32[]{:S(2)}) copy-start(bf16[128,3,3,256]{3,0,2,1:T(8,128)(2,1)} %param.5) | copy-start | bytes 1769476
  15.8 5.6 %collective-permute-start.5 = (bf16[1,1,9,64,256]{4,3,2,1,0:T(8,128)(2,1)S(1)}, bf16[1,1,9,64,256]{4,3,2,1,0:T(8,128)(2,1)S(1)}, u32[]{:S(2)}, u32[]{:S(2)}) collective-permute-start(bf16[1,1,9,64,256]{4,3,2,1,0:T(8,128)(2,1)S(1)} %bitcast.35), channel_id=1, source_target_pairs={{0,2},{2,0},{4,6},{6,4},{8,10},{10,8},{12,14},{14,12},{16,18},{18,... | collective-permute-start | bytes 884744 | tf_op jit(solution)/shard_map/ppermute | solution.py:376
  20.2 4.1 %collective-permute-start.6 = (bf16[1,1,9,64,256]{4,3,2,1,0:T(8,128)(2,1)S(1)}, bf16[1,1,9,64,256]{4,3,2,1,0:T(8,128)(2,1)S(1)}, u32[]{:S(2)}, u32[]{:S(2)}) collective-permute-start(bf16[1,1,9,64,256]{4,3,2,1,0:T(8,128)(2,1)S(1)} %bitcast.38), channel_id=1, source_target_pairs={{0,2},{2,0},{4,6},{6,4},{8,10},{10,8},{12,14},{14,12},{16,18},{18,... | collective-permute-start | bytes 884744 | tf_op jit(solution)/shard_map/ppermute | solution.py:376
  20.3 4.0 %copy-start.1 = (bf16[128,3,3,256]{3,0,2,1:T(8,128)(2,1)S(1)}, bf16[128,3,3,256]{3,0,2,1:T(8,128)(2,1)}, u32[]{:S(2)}) copy-start(bf16[128,3,3,256]{3,0,2,1:T(8,128)(2,1)} %param.6) | copy-start | bytes 1769476
  20.3 9.3 %collective-permute-start.7 = (bf16[20,56,128]{2,1,0:T(8,128)(2,1)S(1)}, bf16[20,56,128]{2,1,0:T(8,128)(2,1)S(1)}, u32[]{:S(2)}, u32[]{:S(2)}) collective-permute-start(bf16[20,56,128]{2,1,0:T(8,128)(2,1)S(1)} %get-tuple-element.77), channel_id=1, source_target_pairs={{0,1},{1,0},{2,3},{3,2},{4,5},{5,4},{6,7},{7,6},{8,9},{9,8},{10,11... | collective-permute-start | bytes 860168 | tf_op jit(solution)/shard_map/ppermute | solution.py:367
  33.2 2.6 %collective-permute-start.8 = (bf16[9,256,128]{2,1,0:T(8,128)(2,1)S(1)}, bf16[9,256,128]{2,1,0:T(8,128)(2,1)S(1)}, u32[]{:S(2)}, u32[]{:S(2)}) collective-permute-start(bf16[9,256,128]{2,1,0:T(8,128)(2,1)S(1)} %get-tuple-element.59), channel_id=1, source_target_pairs={{0,2},{2,0},{4,6},{6,4},{8,10},{10,8},{12,14},{14,12},{16,18},{18,... | collective-permute-start | bytes 1769480 | tf_op jit(solution)/shard_map/ppermute | solution.py:376
  35.3 2.3 %collective-permute-start.9 = (bf16[9,256,128]{2,1,0:T(8,128)(2,1)S(1)}, bf16[9,256,128]{2,1,0:T(8,128)(2,1)S(1)}, u32[]{:S(2)}, u32[]{:S(2)}) collective-permute-start(bf16[9,256,128]{2,1,0:T(8,128)(2,1)S(1)} %get-tuple-element.64), channel_id=1, source_target_pairs={{0,2},{2,0},{4,6},{6,4},{8,10},{10,8},{12,14},{14,12},{16,18},{18,... | collective-permute-start | bytes 1769480 | tf_op jit(solution)/shard_map/ppermute | solution.py:376
  36.5 6.8 %collective-permute-start.13 = (bf16[9,128,128]{2,1,0:T(8,128)(2,1)S(1)}, bf16[9,128,128]{2,1,0:T(8,128)(2,1)S(1)}, u32[]{:S(2)}, u32[]{:S(2)}) collective-permute-start(bf16[9,128,128]{2,1,0:T(8,128)(2,1)S(1)} %get-tuple-element.62), channel_id=1, source_target_pairs={{0,1},{1,0},{2,6},{3,7},{4,5},{5,4},{6,2},{7,3},{8,9},{9,8},{10,14... | collective-permute-start | bytes 884744 | tf_op jit(solution)/shard_map/ppermute | solution.py:470
  38.2 8.8 %collective-permute-start.10 = (bf16[9,128,128]{2,1,0:T(8,128)(2,1)S(1)}, bf16[9,128,128]{2,1,0:T(8,128)(2,1)S(1)}, u32[]{:S(2)}, u32[]{:S(2)}) collective-permute-start(bf16[9,128,128]{2,1,0:T(8,128)(2,1)S(1)} %get-tuple-element.67), channel_id=1, source_target_pairs={{0,1},{1,0},{2,6},{3,7},{4,5},{5,4},{6,2},{7,3},{8,9},{9,8},{10,14... | collective-permute-start | bytes 884744 | tf_op jit(solution)/shard_map/ppermute | solution.py:471
  43.4 6.2 %collective-permute-start.14 = (bf16[9,64,128]{2,1,0:T(8,128)(2,1)S(1)}, bf16[9,64,128]{2,1,0:T(8,128)(2,1)S(1)}, u32[]{:S(2)}, u32[]{:S(2)}) collective-permute-start(bf16[9,64,128]{2,1,0:T(8,128)(2,1)S(1)} %get-tuple-element.74), channel_id=1, source_target_pairs={{0,4},{1,5},{2,3},{3,2},{4,0},{5,1},{6,7},{7,6},{8,12},{9,13},{10,... | collective-permute-start | bytes 442376 | tf_op jit(solution)/shard_map/ppermute | solution.py:476
  47.1 5.6 %collective-permute-start.11 = (bf16[9,64,128]{2,1,0:T(8,128)(2,1)S(1)}, bf16[9,64,128]{2,1,0:T(8,128)(2,1)S(1)}, u32[]{:S(2)}, u32[]{:S(2)}) collective-permute-start(bf16[9,64,128]{2,1,0:T(8,128)(2,1)S(1)} %get-tuple-element.69), channel_id=1, source_target_pairs={{0,4},{1,5},{2,3},{3,2},{4,0},{5,1},{6,7},{7,6},{8,12},{9,13},{10,... | collective-permute-start | bytes 442376 | tf_op jit(solution)/shard_map/ppermute | solution.py:477
  49.6 5.9 %collective-permute-start.15 = (bf16[9,64,128]{2,1,0:T(8,128)(2,1)S(1)}, bf16[9,64,128]{2,1,0:T(8,128)(2,1)S(1)}, u32[]{:S(2)}, u32[]{:S(2)}) collective-permute-start(bf16[9,64,128]{2,1,0:T(8,128)(2,1)S(1)} %add_convert_fusion.4), channel_id=1, source_target_pairs={{0,8},{2,18},{4,12},{6,22},{8,0},{10,26},{12,4},{14,30},{16,24},{1... | collective-permute-start | bytes 442376 | tf_op jit(solution)/shard_map/ppermute | solution.py:340
  52.7 6.8 %collective-permute-start.19 = (bf16[9,64,128]{2,1,0:T(8,128)(2,1)S(1)}, bf16[9,64,128]{2,1,0:T(8,128)(2,1)S(1)}, u32[]{:S(2)}, u32[]{:S(2)}) collective-permute-start(bf16[9,64,128]{2,1,0:T(8,128)(2,1)S(1)} %add_convert_fusion.5), channel_id=1, source_target_pairs={{0,8},{2,18},{4,12},{6,22},{8,0},{10,26},{12,4},{14,30},{16,24},{1... | collective-permute-start | bytes 442376 | tf_op jit(solution)/shard_map/ppermute | solution.py:340
  54.6 7.5 %collective-permute-start.12 = (bf16[16,48,128]{2,1,0:T(8,128)(2,1)S(1)}, bf16[16,48,128]{2,1,0:T(8,128)(2,1)S(1)}, u32[]{:S(2)}, u32[]{:S(2)}) collective-permute-start(bf16[16,48,128]{2,1,0:T(8,128)(2,1)S(1)} %get-tuple-element.78), channel_id=1, source_target_pairs={{0,1},{1,0},{2,3},{3,2},{4,5},{5,4},{6,7},{7,6},{8,9},{9,8},{10,11... | collective-permute-start | bytes 589832 | tf_op jit(solution)/shard_map/ppermute | solution.py:367
  55.5 7.0 %collective-permute-start.16 = (bf16[9,64,128]{2,1,0:T(8,128)(2,1)S(1)}, bf16[9,64,128]{2,1,0:T(8,128)(2,1)S(1)}, u32[]{:S(2)}, u32[]{:S(2)}) collective-permute-start(bf16[9,64,128]{2,1,0:T(8,128)(2,1)S(1)} %add_convert_fusion.3), channel_id=1, source_target_pairs={{0,16},{2,10},{4,20},{6,14},{8,24},{10,2},{12,28},{14,6},{16,0},{1... | collective-permute-start | bytes 442376 | tf_op jit(solution)/shard_map/ppermute | solution.py:340
  59.5 8.0 %collective-permute-start.20 = (bf16[9,64,128]{2,1,0:T(8,128)(2,1)S(1)}, bf16[9,64,128]{2,1,0:T(8,128)(2,1)S(1)}, u32[]{:S(2)}, u32[]{:S(2)}) collective-permute-start(bf16[9,64,128]{2,1,0:T(8,128)(2,1)S(1)} %add_convert_fusion.1), channel_id=1, source_target_pairs={{0,16},{2,10},{4,20},{6,14},{8,24},{10,2},{12,28},{14,6},{16,0},{1... | collective-permute-start | bytes 442376 | tf_op jit(solution)/shard_map/ppermute | solution.py:340
  62.1 10.7 %copy-start.4 = (bf16[16,96,128]{2,1,0:T(8,128)(2,1)}, bf16[16,96,128]{2,1,0:T(8,128)(2,1)S(1)}, u32[]{:S(2)}) copy-start(bf16[16,96,128]{2,1,0:T(8,128)(2,1)S(1)} %constant_dynamic-update-slice_fusion) | copy-start | bytes 1179652
  62.6 6.7 %collective-permute-start.17 = (bf16[9,64,128]{2,1,0:T(8,128)(2,1)S(1)}, bf16[9,64,128]{2,1,0:T(8,128)(2,1)S(1)}, u32[]{:S(2)}, u32[]{:S(2)}) collective-permute-start(bf16[9,64,128]{2,1,0:T(8,128)(2,1)S(1)} %add_convert_fusion.2), channel_id=1, source_target_pairs={{0,4},{2,6},{4,0},{6,2},{8,12},{10,14},{12,8},{14,10},{16,20},{18,... | collective-permute-start | bytes 442376 | tf_op jit(solution)/shard_map/ppermute | solution.py:498
  67.6 5.2 %collective-permute-start.21 = (bf16[9,64,128]{2,1,0:T(8,128)(2,1)S(1)}, bf16[9,64,128]{2,1,0:T(8,128)(2,1)S(1)}, u32[]{:S(2)}, u32[]{:S(2)}) collective-permute-start(bf16[9,64,128]{2,1,0:T(8,128)(2,1)S(1)} %add_convert_fusion), channel_id=1, source_target_pairs={{0,4},{2,6},{4,0},{6,2},{8,12},{10,14},{12,8},{14,10},{16,20},{18,... | collective-permute-start | bytes 442376 | tf_op jit(solution)/shard_map/ppermute | solution.py:499
  69.3 3.6 %collective-permute-start.18 = (bf16[9,128,128]{2,1,0:T(8,128)(2,1)S(1)}, bf16[9,128,128]{2,1,0:T(8,128)(2,1)S(1)}, u32[]{:S(2)}, u32[]{:S(2)}) collective-permute-start(bf16[9,128,128]{2,1,0:T(8,128)(2,1)S(1)} %pad_maximum_fusion.1.here), channel_id=1, source_target_pairs={{0,2},{2,0},{4,6},{6,4},{8,10},{10,8},{12,14},{14,12},{16,18},{18,... | collective-permute-start | bytes 884744 | tf_op jit(solution)/shard_map/ppermute | solution.py:346
  72.9 1.8 %collective-permute-start.22 = (bf16[9,128,128]{2,1,0:T(8,128)(2,1)S(1)}, bf16[9,128,128]{2,1,0:T(8,128)(2,1)S(1)}, u32[]{:S(2)}, u32[]{:S(2)}) collective-permute-start(bf16[9,128,128]{2,1,0:T(8,128)(2,1)S(1)} %pad_maximum_fusion.2.here), channel_id=1, source_target_pairs={{0,2},{2,0},{4,6},{6,4},{8,10},{10,8},{12,14},{14,12},{16,18},{18,... | collective-permute-start | bytes 884744 | tf_op jit(solution)/shard_map/ppermute | solution.py:346

commit v5 on v4

--- a/solution.py
+++ b/solution.py
@@ -195,8 +195,8 @@
             send[i * 3 + j] = jnp.where(low_core, high, low).astype(BF16)
 
 
-def inner_kernel(dims, count, where, own, mine, other, slope2, slope1, fbuf, *refs):
-    cots, (inner, outer, keep, send, w, shifted) = refs[:count], refs[count:]
+def inner_kernel(dims, count, where, w, slope2, slope1, fbuf, *refs):
+    cots, (inner, outer, keep, send, shifted) = refs[:count], refs[count:]
     ny, hl, wl, height, width = dims
     iy, ix = where[0], where[1]
     rows = fbuf.shape[1]
@@ -211,7 +211,6 @@
             ]
             parts = [jnp.where(iy == 0, a, b), jnp.where(iy == 0, b, a)]
         outer[c] = (jnp.concatenate(parts, axis=1) * slope2[c]).astype(BF16)
-    assemble_filter(w, own, (mine, other), iy, ix, ny)
     for c0, n in chunks(wl + 2, 9):
         grad = conv_chunk(outer, w, c0, n, True)
         for q in range(n):
@@ -407,7 +406,7 @@
     right = lax.ppermute(low, "gx", backward)
     first_mine = after(first_mine, left, right)
     first_in = (first_mine, pass_core(first_mine))
-    second_mine = spread_y(after(second_send, low))
+    second_mine = spread_y(after(second_send, up))
     second_in = (second_mine, pass_core(second_mine))
 
     ct = jnp.concatenate([left[at:].reshape(2, height, co), ct, right[at:].reshape(2, height, co)], axis=0)
@@ -436,19 +435,18 @@
         (where, ft, left, right, up, down, first_own, *first_in),
         [weights],
     )
-    act, slope2 = call(
+    act, slope2, second_all = call(
         functools.partial(conv2_kernel, dims),
-        [((wl, hl, ch), BF16), ((wl + 4, rows, ch), F32)],
+        [((wl, hl, ch), BF16), ((wl + 4, rows, ch), F32), ((9, ch, ch), BF16)],
         (where, hidden, second_own, *second_in),
-        [weights],
     )
     grad_shapes = [((9, ch, ch // 2), F32), ((9, ch, ch // 2), BF16)]
     shifted = bf(wl * rows, 3 * ch)
     inner, outer, keep1, send1 = call(
         functools.partial(inner_kernel, dims, len(cots)),
         [((wl + 2, rows, ch), BF16), ((wl + 4, rows, ch), BF16)] + grad_shapes,
-        (where, second_own, *second_in, slope2, slope1, fbuf, *cots),
-        [weights, shifted],
+        (where, second_all, slope2, slope1, fbuf, *cots),
+        [shifted],
     )
     keep2, send2 = call(
         functools.partial(second_grad_kernel, dims),
@@ -478,7 +476,7 @@
     else:
         total1 = add([after(parts1[0], parts2, input_grad)] + send_planes(parts1, nx, ny))
         total2 = add([parts2[0]] + send_planes(parts2, nx, ny))
-    act = after(act, total2)
+    act = after(act, total1)
 
     def channels_of(y):
         return lax.dynamic_slice_in_dim(act, y * co, co, 2)

time: 77.1 us -> 76.8 us (level)
    ppermute x1, waiting for transfers between devices: 1.44 us -> 0.48 us  [body(): total2 = add([own2, lax.ppermute(pass2, axes, pairs[1])])]
where the time goes in v5:
time: 76.8 us; the launch traced here: 76 us
  starting transfers between devices  35.3 us (46%)
  Pallas kernels  21.2 us (28%)
  waiting for transfers between devices  17.7 us (23%)
  between operations  0.96 us (1%)
    pallas_call x13, Pallas kernels, call(): pl.pallas_call(kernel, out_shape=[jax.ShapeDtypeStruct(s, t) for s, t in...  21.2 us
    ppermute x4, starting transfers between devices, far_partner(): lax.ppermute(total, 'gx', [(g, g ^ (near if g % 2 == 0 else far)) for g i...  9.4 us
    ppermute x5, starting transfers between devices, round_y(): return lax.ppermute(x, 'gy', [(i, (i + d) % ny) for i in range(ny)])  7.34 us
    ppermute x5, waiting for transfers between devices, round_y(): return lax.ppermute(x, 'gy', [(i, (i + d) % ny) for i in range(ny)])  6.34 us
    ppermute x4, waiting for transfers between devices, far_partner(): lax.ppermute(total, 'gx', [(g, g ^ (near if g % 2 == 0 else far)) for g i...  3.64 us
    ppermute x1, waiting for transfers between devices, body(): beside2 = lax.ppermute(total2, 'gx', [(g, g ^ 2) for g in range(nx)])  3.46 us
    ppermute x1, starting transfers between devices, body(): beside1 = lax.ppermute(total1, 'gx', [(g, g ^ 2) for g in range(nx)])  3.08 us
    ppermute x4, starting transfers between devices, pass_core(): return lax.ppermute(mine, 'gx', [(i, i ^ 1) for i in range(nx)])  3.04 us
  transfers between devices with their start and end apart: 23, of which 13 were waited for; matrix products, arithmetic and copies ran while one was open for 1% of the time, Pallas kernels for 19%

profile of v5, /device:TPU:0, one launch (start us, length us, event | category | flops | bytes accessed | tf_op | source)
XLA Modules:
  0.0 76.0 jit_solution(3462400851643547182)
XLA Ops:
  0.7 1.6 %shard_map.75 = (bf16[1,4,16,256]{3,2,1,0:T(8,128)(2,1)S(1)}, bf16[9,64,256]{2,1,0:T(8,128)(2,1)S(1)}, bf16[9,64,256]{2,1,0:T(8,128)(2,1)S(1)}, bf16[2,96,128]{2,1,0:T(8,128)(2,1)S(1)}, bf16[2,96,128]{2,1,0:T(8,128)(2,1)S(1)}) custom-call(s32[2]{0:T(128)S(1)} %pad_add_fusion.where, bf16[48,16,256]{2,1,0:T(8,128)(2,1)} %features.1, ...), custom_call_target="tpu_custom_call" | custom-call | tf_op jit(solution)/shard_map/pallas_call | solution.py:26
  2.4 3.0 %collective-permute-start = (bf16[4,16,256]{2,0,1:T(4,128)(2,1)S(1)}, bf16[4,16,256]{2,0,1:T(4,128)(2,1)S(1)}, u32[]{:S(2)}, u32[]{:S(2)}) collective-permute-start(bf16[4,16,256]{2,0,1:T(4,128)(2,1)S(1)} %bitcast.50), channel_id=1, source_target_pairs={{0,1},{1,0},{2,3},{3,2},{4,5},{5,4},{6,7},{7,6},{8,9},{9,8},{10,11... | collective-permute-start | bytes 98312 | tf_op jit(solution)/shard_map/ppermute | solution.py:366
  5.5 1.8 %collective-permute-done = bf16[4,16,256]{2,0,1:T(4,128)(2,1)S(1)} collective-permute-done((bf16[4,16,256]{2,0,1:T(4,128)(2,1)S(1)}, bf16[4,16,256]{2,0,1:T(4,128)(2,1)S(1)}, u32[]{:S(2)}, u32[]{:S(2)}) %collective-permute-start) | collective-permute-done | bytes 32800 | tf_op jit(solution)/shard_map/ppermute | solution.py:366
  7.3 2.4 %collective-permute-start.3 = (bf16[9,64,256]{2,1,0:T(8,128)(2,1)S(1)}, bf16[9,64,256]{2,1,0:T(8,128)(2,1)S(1)}, u32[]{:S(2)}, u32[]{:S(2)}) collective-permute-start(bf16[9,64,256]{2,1,0:T(8,128)(2,1)S(1)} %get-tuple-element.48), channel_id=1, source_target_pairs={{0,1},{1,0},{2,3},{3,2},{4,5},{5,4},{6,7},{7,6},{8,9},{9,8},{10,11... | collective-permute-start | bytes 884744 | tf_op jit(solution)/shard_map/ppermute | solution.py:366
  10.5 1.3 %collective-permute-start.2 = (bf16[640,128]{1,0:T(8,128)(2,1)S(1)}, bf16[640,128]{1,0:T(8,128)(2,1)S(1)}, u32[]{:S(2)}, u32[]{:S(2)}) collective-permute-start(bf16[640,128]{1,0:T(8,128)(2,1)S(1)} %get-tuple-element.46), channel_id=1, source_target_pairs={{2,0},{4,2},{6,4},{8,6},{10,8},{12,10},{14,12},{16,14},{18,16},{20... | collective-permute-start | bytes 491528 | tf_op jit(solution)/shard_map/ppermute | solution.py:406
  11.8 3.0 %collective-permute-start.1 = (bf16[640,128]{1,0:T(8,128)(2,1)S(1)}, bf16[640,128]{1,0:T(8,128)(2,1)S(1)}, u32[]{:S(2)}, u32[]{:S(2)}) collective-permute-start(bf16[640,128]{1,0:T(8,128)(2,1)S(1)} %get-tuple-element.45), channel_id=1, source_target_pairs={{0,2},{2,4},{4,6},{6,8},{8,10},{10,12},{12,14},{14,16},{16,18},{18... | collective-permute-start | bytes 491528 | tf_op jit(solution)/shard_map/ppermute | solution.py:405
  14.9 0.9 %collective-permute-done.1.left = bf16[640,128]{1,0:T(8,128)(2,1)S(1)} collective-permute-done((bf16[640,128]{1,0:T(8,128)(2,1)S(1)}, bf16[640,128]{1,0:T(8,128)(2,1)S(1)}, u32[]{:S(2)}, u32[]{:S(2)}) %collective-permute-start.1) | collective-permute-done | bytes 163872 | tf_op jit(solution)/shard_map/ppermute | solution.py:405
  15.9 2.4 %collective-permute-start.5 = (bf16[1,1,9,64,256]{4,3,2,1,0:T(8,128)(2,1)S(1)}, bf16[1,1,9,64,256]{4,3,2,1,0:T(8,128)(2,1)S(1)}, u32[]{:S(2)}, u32[]{:S(2)}) collective-permute-start(bf16[1,1,9,64,256]{4,3,2,1,0:T(8,128)(2,1)S(1)} %bitcast.34), channel_id=1, source_target_pairs={{0,2},{2,0},{4,6},{6,4},{8,10},{10,8},{12,14},{14,12},{16,18},{18,... | collective-permute-start | bytes 884744 | tf_op jit(solution)/shard_map/ppermute | solution.py:375
  18.3 1.9 %collective-permute-done.3 = bf16[9,64,256]{2,1,0:T(8,128)(2,1)S(1)} collective-permute-done((bf16[9,64,256]{2,1,0:T(8,128)(2,1)S(1)}, bf16[9,64,256]{2,1,0:T(8,128)(2,1)S(1)}, u32[]{:S(2)}, u32[]{:S(2)}) %collective-permute-start.3) | collective-permute-done | bytes 294944 | tf_op jit(solution)/shard_map/ppermute | solution.py:366
  20.3 1.0 %collective-permute-start.7 = (bf16[20,56,128]{2,1,0:T(8,128)(2,1)S(1)}, bf16[20,56,128]{2,1,0:T(8,128)(2,1)S(1)}, u32[]{:S(2)}, u32[]{:S(2)}) collective-permute-start(bf16[20,56,128]{2,1,0:T(8,128)(2,1)S(1)} %get-tuple-element.79), channel_id=1, source_target_pairs={{0,1},{1,0},{2,3},{3,2},{4,5},{5,4},{6,7},{7,6},{8,9},{9,8},{10,11... | collective-permute-start | bytes 860168 | tf_op jit(solution)/shard_map/ppermute | solution.py:366
  21.4 2.9 %shard_map.77 = (bf16[22,64,256]{2,1,0:T(8,128)(2,1)S(1)}, f32[18,64,256]{2,1,0:T(8,128)S(1)}, bf16[24,64,256]{2,1,0:T(8,128)(2,1)S(1)}) custom-call(s32[2]{0:T(128)S(1)} %pad_add_fusion.where, bf16[16,48,256]{2,1,0:T(8,128)(2,1)S(1)} %bitcast.31, bf16[640,128]{1,0:T(8,128)(2,1)S(1)} %collective-permute-done.1.left, ...), custom_call_target="tpu_custom_call" | custom-call | tf_op jit(solution)/shard_map/pallas_call | solution.py:26
  24.4 2.7 %shard_map.78 = (bf16[16,48,256]{2,1,0:T(8,128)(2,1)S(1)}, f32[20,64,256]{2,1,0:T(8,128)S(1)}, bf16[9,256,256]{2,1,0:T(8,128)(2,1)S(1)}) custom-call(s32[2]{0:T(128)S(1)} %pad_add_fusion.where, bf16[22,64,256]{2,1,0:T(8,128)(2,1)S(1)} %get-tuple-element.52.hidden, bf16[9,128,256]{2,1,0:T(8,128)(2,1)S(1)} %bitcast.33, ...), custom_call_target="tpu_custom_call" | custom-call | tf_op jit(solution)/shard_map/pallas_call | solution.py:26
  27.0 2.6 %collective-permute-done.7.refs_1_ = bf16[20,56,128]{2,1,0:T(8,128)(2,1)S(1)} collective-permute-done((bf16[20,56,128]{2,1,0:T(8,128)(2,1)S(1)}, bf16[20,56,128]{2,1,0:T(8,128)(2,1)S(1)}, u32[]{:S(2)}, u32[]{:S(2)}) %collective-permute-start.7) | collective-permute-done | bytes 286752 | tf_op jit(solution)/shard_map/ppermute | solution.py:366
  29.6 3.5 %shard_map.79 = (bf16[18,64,256]{2,1,0:T(8,128)(2,1)S(1)}, bf16[20,64,256]{2,1,0:T(8,128)(2,1)S(1)}, f32[9,256,128]{2,1,0:T(8,128)S(1)}, bf16[9,256,128]{2,1,0:T(8,128)(2,1)S(1)}) custom-call(s32[2]{0:T(128)S(1)} %pad_add_fusion.where, bf16[9,256,256]{2,1,0:T(8,128)(2,1)S(1)} %get-tuple-element.54.w, f32[20,64,256]{2,1,0:T(8,128)S(1)} %get-tuple-element.55.slope2, ...), custom_call_target="tpu_custom_call" | custom-call | tf_op jit(solution)/shard_map/pallas_call | solution.py:26
  33.2 2.0 %shard_map.81 = (f32[9,256,128]{2,1,0:T(8,128)S(1)}, bf16[9,256,128]{2,1,0:T(8,128)(2,1)S(1)}) custom-call(s32[2]{0:T(128)S(1)} %pad_add_fusion.where, bf16[22,64,256]{2,1,0:T(8,128)(2,1)S(1)} %get-tuple-element.52.hidden, bf16[20,64,256]{2,1,0:T(8,128)(2,1)S(1)} %get-tuple-element.63.outer), custom_call_target="tpu_custom_call" | custom-call | tf_op jit(solution)/shard_map/pallas_call | solution.py:26
  36.4 1.0 %collective-permute-start.9 = (bf16[9,128,128]{2,1,0:T(8,128)(2,1)S(1)}, bf16[9,128,128]{2,1,0:T(8,128)(2,1)S(1)}, u32[]{:S(2)}, u32[]{:S(2)}) collective-permute-start(bf16[9,128,128]{2,1,0:T(8,128)(2,1)S(1)} %get-tuple-element.62), channel_id=1, source_target_pairs={{0,1},{1,0},{2,6},{3,7},{4,5},{5,4},{6,2},{7,3},{8,9},{9,8},{10,14... | collective-permute-start | bytes 884744 | tf_op jit(solution)/shard_map/ppermute | solution.py:468
  38.1 1.1 %collective-permute-start.17 = (bf16[9,128,128]{2,1,0:T(8,128)(2,1)S(1)}, bf16[9,128,128]{2,1,0:T(8,128)(2,1)S(1)}, u32[]{:S(2)}, u32[]{:S(2)}) collective-permute-start(bf16[9,128,128]{2,1,0:T(8,128)(2,1)S(1)} %get-tuple-element.69), channel_id=1, source_target_pairs={{0,1},{1,0},{2,6},{3,7},{4,5},{5,4},{6,2},{7,3},{8,9},{9,8},{10,14... | collective-permute-start | bytes 884744 | tf_op jit(solution)/shard_map/ppermute | solution.py:469
  39.2 3.1 %shard_map.83 = bf16[48,16,256]{2,1,0:T(8,128)(2,1)} custom-call(s32[2]{0:T(128)S(1)} %pad_add_fusion.where, bf16[18,64,256]{2,1,0:T(8,128)(2,1)S(1)} %get-tuple-element.70.inner, bf16[9,128,256]{2,1,0:T(8,128)(2,1)S(1)} %bitcast.29, bf16[1,1,9,64,256]{4,3,2,1,0:T(8,128)(2,1)S(1)} %bitcast.36, bf16[1,1,9,64,256]{4,3,2,1,0:T(8,128)(2,1)S(1)} %collective-permute-done.5.other), custom_call_target="tpu_custom_call" | custom-call | tf_op jit(solution)/shard_map/pallas_call | solution.py:26
  43.3 1.8 %collective-permute-start.11 = (bf16[9,64,128]{2,1,0:T(8,128)(2,1)S(1)}, bf16[9,64,128]{2,1,0:T(8,128)(2,1)S(1)}, u32[]{:S(2)}, u32[]{:S(2)}) collective-permute-start(bf16[9,64,128]{2,1,0:T(8,128)(2,1)S(1)} %get-tuple-element.73), channel_id=1, source_target_pairs={{0,4},{1,5},{2,3},{3,2},{4,0},{5,1},{6,7},{7,6},{8,12},{9,13},{10,... | collective-permute-start | bytes 442376 | tf_op jit(solution)/shard_map/ppermute | solution.py:474
  45.1 1.9 %collective-permute-done.17.came = bf16[9,128,128]{2,1,0:T(8,128)(2,1)S(1)} collective-permute-done((bf16[9,128,128]{2,1,0:T(8,128)(2,1)S(1)}, bf16[9,128,128]{2,1,0:T(8,128)(2,1)S(1)}, u32[]{:S(2)}, u32[]{:S(2)}) %collective-permute-start.17) | collective-permute-done | bytes 294944 | tf_op jit(solution)/shard_map/ppermute | solution.py:469
  47.0 2.5 %collective-permute-start.18 = (bf16[9,64,128]{2,1,0:T(8,128)(2,1)S(1)}, bf16[9,64,128]{2,1,0:T(8,128)(2,1)S(1)}, u32[]{:S(2)}, u32[]{:S(2)}) collective-permute-start(bf16[9,64,128]{2,1,0:T(8,128)(2,1)S(1)} %get-tuple-element.76), channel_id=1, source_target_pairs={{0,4},{1,5},{2,3},{3,2},{4,0},{5,1},{6,7},{7,6},{8,12},{9,13},{10,... | collective-permute-start | bytes 442376 | tf_op jit(solution)/shard_map/ppermute | solution.py:475
  49.5 1.6 %collective-permute-start.13 = (bf16[9,64,128]{2,1,0:T(8,128)(2,1)S(1)}, bf16[9,64,128]{2,1,0:T(8,128)(2,1)S(1)}, u32[]{:S(2)}, u32[]{:S(2)}) collective-permute-start(bf16[9,64,128]{2,1,0:T(8,128)(2,1)S(1)} %add_convert_fusion.5), channel_id=1, source_target_pairs={{0,8},{2,18},{4,12},{6,22},{8,0},{10,26},{12,4},{14,30},{16,24},{1... | collective-permute-start | bytes 442376 | tf_op jit(solution)/shard_map/ppermute | solution.py:339
  52.6 1.8 %collective-permute-start.19 = (bf16[9,64,128]{2,1,0:T(8,128)(2,1)S(1)}, bf16[9,64,128]{2,1,0:T(8,128)(2,1)S(1)}, u32[]{:S(2)}, u32[]{:S(2)}) collective-permute-start(bf16[9,64,128]{2,1,0:T(8,128)(2,1)S(1)} %add_convert_fusion.2), channel_id=1, source_target_pairs={{0,8},{2,18},{4,12},{6,22},{8,0},{10,26},{12,4},{14,30},{16,24},{1... | collective-permute-start | bytes 442376 | tf_op jit(solution)/shard_map/ppermute | solution.py:339
  54.4 1.0 %collective-permute-done.13 = bf16[9,64,128]{2,1,0:T(8,128)(2,1)S(1)} collective-permute-done((bf16[9,64,128]{2,1,0:T(8,128)(2,1)S(1)}, bf16[9,64,128]{2,1,0:T(8,128)(2,1)S(1)}, u32[]{:S(2)}, u32[]{:S(2)}) %collective-permute-start.13) | collective-permute-done | bytes 147488 | tf_op jit(solution)/shard_map/ppermute | solution.py:339
  55.4 2.7 %collective-permute-start.14 = (bf16[9,64,128]{2,1,0:T(8,128)(2,1)S(1)}, bf16[9,64,128]{2,1,0:T(8,128)(2,1)S(1)}, u32[]{:S(2)}, u32[]{:S(2)}) collective-permute-start(bf16[9,64,128]{2,1,0:T(8,128)(2,1)S(1)} %add_convert_fusion.4), channel_id=1, source_target_pairs={{0,16},{2,10},{4,20},{6,14},{8,24},{10,2},{12,28},{14,6},{16,0},{1... | collective-permute-start | bytes 442376 | tf_op jit(solution)/shard_map/ppermute | solution.py:339
  58.8 3.3 %collective-permute-start.20 = (bf16[9,64,128]{2,1,0:T(8,128)(2,1)S(1)}, bf16[9,64,128]{2,1,0:T(8,128)(2,1)S(1)}, u32[]{:S(2)}, u32[]{:S(2)}) collective-permute-start(bf16[9,64,128]{2,1,0:T(8,128)(2,1)S(1)} %add_convert_fusion.1), channel_id=1, source_target_pairs={{0,16},{2,10},{4,20},{6,14},{8,24},{10,2},{12,28},{14,6},{16,0},{1... | collective-permute-start | bytes 442376 | tf_op jit(solution)/shard_map/ppermute | solution.py:339
  62.3 3.1 %collective-permute-start.15 = (bf16[9,64,128]{2,1,0:T(8,128)(2,1)S(1)}, bf16[9,64,128]{2,1,0:T(8,128)(2,1)S(1)}, u32[]{:S(2)}, u32[]{:S(2)}) collective-permute-start(bf16[9,64,128]{2,1,0:T(8,128)(2,1)S(1)} %add_convert_fusion.3), channel_id=1, source_target_pairs={{0,4},{2,6},{4,0},{6,2},{8,12},{10,14},{12,8},{14,10},{16,20},{18,... | collective-permute-start | bytes 442376 | tf_op jit(solution)/shard_map/ppermute | solution.py:496
  65.4 1.9 %collective-permute-done.20 = bf16[9,64,128]{2,1,0:T(8,128)(2,1)S(1)} collective-permute-done((bf16[9,64,128]{2,1,0:T(8,128)(2,1)S(1)}, bf16[9,64,128]{2,1,0:T(8,128)(2,1)S(1)}, u32[]{:S(2)}, u32[]{:S(2)}) %collective-permute-start.20) | collective-permute-done | bytes 147488 | tf_op jit(solution)/shard_map/ppermute | solution.py:339
  67.3 1.5 %collective-permute-start.21 = (bf16[9,64,128]{2,1,0:T(8,128)(2,1)S(1)}, bf16[9,64,128]{2,1,0:T(8,128)(2,1)S(1)}, u32[]{:S(2)}, u32[]{:S(2)}) collective-permute-start(bf16[9,64,128]{2,1,0:T(8,128)(2,1)S(1)} %add_convert_fusion), channel_id=1, source_target_pairs={{0,4},{2,6},{4,0},{6,2},{8,12},{10,14},{12,8},{14,10},{16,20},{18,... | collective-permute-start | bytes 442376 | tf_op jit(solution)/shard_map/ppermute | solution.py:497
  69.1 3.5 %collective-permute-done.21 = bf16[9,64,128]{2,1,0:T(8,128)(2,1)S(1)} collective-permute-done((bf16[9,64,128]{2,1,0:T(8,128)(2,1)S(1)}, bf16[9,64,128]{2,1,0:T(8,128)(2,1)S(1)}, u32[]{:S(2)}, u32[]{:S(2)}) %collective-permute-start.21) | collective-permute-done | bytes 147488 | tf_op jit(solution)/shard_map/ppermute | solution.py:497
  72.7 1.7 %shard_map.85 = f32[9,128,256]{2,1,0:T(8,128)} custom-call(s32[2]{0:T(128)S(1)} %pad_add_fusion.where, bf16[9,128,128]{2,1,0:T(8,128)(2,1)S(1)} %pad_maximum_fusion.1.here, bf16[9,128,128]{2,1,0:T(8,128)(2,1)S(1)} %collective-permute-done.16.there), custom_call_target="tpu_custom_call" | custom-call | tf_op jit(solution)/shard_map/pallas_call | solution.py:26
  74.4 1.7 %shard_map.87 = f32[9,128,256]{2,1,0:T(8,128)} custom-call(s32[2]{0:T(128)S(1)} %pad_add_fusion.where, bf16[9,128,128]{2,1,0:T(8,128)(2,1)S(1)} %pad_maximum_fusion.2.here, bf16[9,128,128]{2,1,0:T(8,128)(2,1)S(1)} %collective-permute-done.22.there), custom_call_target="tpu_custom_call" | custom-call | tf_op jit(solution)/shard_map/pallas_call | solution.py:26
  (57 shorter events, 6.8 us)
Async XLA Ops:
  0.6 9.1 %copy-start.2 = (bf16[48,16,256]{2,1,0:T(8,128)(2,1)S(1)}, bf16[48,16,256]{2,1,0:T(8,128)(2,1)}, u32[]{:S(2)}) copy-start(bf16[48,16,256]{2,1,0:T(8,128)(2,1)} %features.1) | copy-start | bytes 1179652
  2.4 13.4 %copy-start.3 = (bf16[128,16,96]{0,2,1:T(8,128)(2,1)S(1)}, bf16[128,16,96]{0,2,1:T(8,128)(2,1)}, u32[]{:S(2)}) copy-start(bf16[128,16,96]{0,2,1:T(8,128)(2,1)} %param.7) | copy-start | bytes 1179652
  2.4 4.9 %collective-permute-start = (bf16[4,16,256]{2,0,1:T(4,128)(2,1)S(1)}, bf16[4,16,256]{2,0,1:T(4,128)(2,1)S(1)}, u32[]{:S(2)}, u32[]{:S(2)}) collective-permute-start(bf16[4,16,256]{2,0,1:T(4,128)(2,1)S(1)} %bitcast.50), channel_id=1, source_target_pairs={{0,1},{1,0},{2,3},{3,2},{4,5},{5,4},{6,7},{7,6},{8,9},{9,8},{10,11... | collective-permute-start | bytes 98312 | tf_op jit(solution)/shard_map/ppermute | solution.py:366
  5.4 10.4 %collective-permute-start.4 = (bf16[9,64,256]{2,1,0:T(8,128)(2,1)S(1)}, bf16[9,64,256]{2,1,0:T(8,128)(2,1)S(1)}, u32[]{:S(2)}, u32[]{:S(2)}) collective-permute-start(bf16[9,64,256]{2,1,0:T(8,128)(2,1)S(1)} %get-tuple-element.50), channel_id=1, source_target_pairs={{0,1},{1,0},{2,3},{3,2},{4,5},{5,4},{6,7},{7,6},{8,9},{9,8},{10,11... | collective-permute-start | bytes 884744 | tf_op jit(solution)/shard_map/ppermute | solution.py:366
  7.3 12.9 %collective-permute-start.3 = (bf16[9,64,256]{2,1,0:T(8,128)(2,1)S(1)}, bf16[9,64,256]{2,1,0:T(8,128)(2,1)S(1)}, u32[]{:S(2)}, u32[]{:S(2)}) collective-permute-start(bf16[9,64,256]{2,1,0:T(8,128)(2,1)S(1)} %get-tuple-element.48), channel_id=1, source_target_pairs={{0,1},{1,0},{2,3},{3,2},{4,5},{5,4},{6,7},{7,6},{8,9},{9,8},{10,11... | collective-permute-start | bytes 884744 | tf_op jit(solution)/shard_map/ppermute | solution.py:366
  10.5 4.4 %collective-permute-start.2 = (bf16[640,128]{1,0:T(8,128)(2,1)S(1)}, bf16[640,128]{1,0:T(8,128)(2,1)S(1)}, u32[]{:S(2)}, u32[]{:S(2)}) collective-permute-start(bf16[640,128]{1,0:T(8,128)(2,1)S(1)} %get-tuple-element.46), channel_id=1, source_target_pairs={{2,0},{4,2},{6,4},{8,6},{10,8},{12,10},{14,12},{16,14},{18,16},{20... | collective-permute-start | bytes 491528 | tf_op jit(solution)/shard_map/ppermute | solution.py:406
  11.8 4.0 %collective-permute-start.1 = (bf16[640,128]{1,0:T(8,128)(2,1)S(1)}, bf16[640,128]{1,0:T(8,128)(2,1)S(1)}, u32[]{:S(2)}, u32[]{:S(2)}) collective-permute-start(bf16[640,128]{1,0:T(8,128)(2,1)S(1)} %get-tuple-element.45), channel_id=1, source_target_pairs={{0,2},{2,4},{4,6},{6,8},{8,10},{10,12},{12,14},{14,16},{16,18},{18... | collective-permute-start | bytes 491528 | tf_op jit(solution)/shard_map/ppermute | solution.py:405
  14.8 6.6 %copy-start = (bf16[128,3,3,256]{3,0,2,1:T(8,128)(2,1)S(1)}, bf16[128,3,3,256]{3,0,2,1:T(8,128)(2,1)}, u32[]{:S(2)}) copy-start(bf16[128,3,3,256]{3,0,2,1:T(8,128)(2,1)} %param.5) | copy-start | bytes 1769476
  15.9 5.5 %collective-permute-start.5 = (bf16[1,1,9,64,256]{4,3,2,1,0:T(8,128)(2,1)S(1)}, bf16[1,1,9,64,256]{4,3,2,1,0:T(8,128)(2,1)S(1)}, u32[]{:S(2)}, u32[]{:S(2)}) collective-permute-start(bf16[1,1,9,64,256]{4,3,2,1,0:T(8,128)(2,1)S(1)} %bitcast.34), channel_id=1, source_target_pairs={{0,2},{2,0},{4,6},{6,4},{8,10},{10,8},{12,14},{14,12},{16,18},{18,... | collective-permute-start | bytes 884744 | tf_op jit(solution)/shard_map/ppermute | solution.py:375
  20.2 4.1 %collective-permute-start.6 = (bf16[1,1,9,64,256]{4,3,2,1,0:T(8,128)(2,1)S(1)}, bf16[1,1,9,64,256]{4,3,2,1,0:T(8,128)(2,1)S(1)}, u32[]{:S(2)}, u32[]{:S(2)}) collective-permute-start(bf16[1,1,9,64,256]{4,3,2,1,0:T(8,128)(2,1)S(1)} %bitcast.41), channel_id=1, source_target_pairs={{0,2},{2,0},{4,6},{6,4},{8,10},{10,8},{12,14},{14,12},{16,18},{18,... | collective-permute-start | bytes 884744 | tf_op jit(solution)/shard_map/ppermute | solution.py:375
  20.3 4.0 %copy-start.1 = (bf16[128,3,3,256]{3,0,2,1:T(8,128)(2,1)S(1)}, bf16[128,3,3,256]{3,0,2,1:T(8,128)(2,1)}, u32[]{:S(2)}) copy-start(bf16[128,3,3,256]{3,0,2,1:T(8,128)(2,1)} %param.6) | copy-start | bytes 1769476
  20.3 9.3 %collective-permute-start.7 = (bf16[20,56,128]{2,1,0:T(8,128)(2,1)S(1)}, bf16[20,56,128]{2,1,0:T(8,128)(2,1)S(1)}, u32[]{:S(2)}, u32[]{:S(2)}) collective-permute-start(bf16[20,56,128]{2,1,0:T(8,128)(2,1)S(1)} %get-tuple-element.79), channel_id=1, source_target_pairs={{0,1},{1,0},{2,3},{3,2},{4,5},{5,4},{6,7},{7,6},{8,9},{9,8},{10,11... | collective-permute-start | bytes 860168 | tf_op jit(solution)/shard_map/ppermute | solution.py:366
  33.1 2.6 %collective-permute-start.8 = (bf16[9,256,128]{2,1,0:T(8,128)(2,1)S(1)}, bf16[9,256,128]{2,1,0:T(8,128)(2,1)S(1)}, u32[]{:S(2)}, u32[]{:S(2)}) collective-permute-start(bf16[9,256,128]{2,1,0:T(8,128)(2,1)S(1)} %get-tuple-element.59), channel_id=1, source_target_pairs={{0,2},{2,0},{4,6},{6,4},{8,10},{10,8},{12,14},{14,12},{16,18},{18,... | collective-permute-start | bytes 1769480 | tf_op jit(solution)/shard_map/ppermute | solution.py:375
  35.2 2.3 %collective-permute-start.10 = (bf16[9,256,128]{2,1,0:T(8,128)(2,1)S(1)}, bf16[9,256,128]{2,1,0:T(8,128)(2,1)S(1)}, u32[]{:S(2)}, u32[]{:S(2)}) collective-permute-start(bf16[9,256,128]{2,1,0:T(8,128)(2,1)S(1)} %get-tuple-element.66), channel_id=1, source_target_pairs={{0,2},{2,0},{4,6},{6,4},{8,10},{10,8},{12,14},{14,12},{16,18},{18,... | collective-permute-start | bytes 1769480 | tf_op jit(solution)/shard_map/ppermute | solution.py:375
  36.4 6.8 %collective-permute-start.9 = (bf16[9,128,128]{2,1,0:T(8,128)(2,1)S(1)}, bf16[9,128,128]{2,1,0:T(8,128)(2,1)S(1)}, u32[]{:S(2)}, u32[]{:S(2)}) collective-permute-start(bf16[9,128,128]{2,1,0:T(8,128)(2,1)S(1)} %get-tuple-element.62), channel_id=1, source_target_pairs={{0,1},{1,0},{2,6},{3,7},{4,5},{5,4},{6,2},{7,3},{8,9},{9,8},{10,14... | collective-permute-start | bytes 884744 | tf_op jit(solution)/shard_map/ppermute | solution.py:468
  38.1 8.8 %collective-permute-start.17 = (bf16[9,128,128]{2,1,0:T(8,128)(2,1)S(1)}, bf16[9,128,128]{2,1,0:T(8,128)(2,1)S(1)}, u32[]{:S(2)}, u32[]{:S(2)}) collective-permute-start(bf16[9,128,128]{2,1,0:T(8,128)(2,1)S(1)} %get-tuple-element.69), channel_id=1, source_target_pairs={{0,1},{1,0},{2,6},{3,7},{4,5},{5,4},{6,2},{7,3},{8,9},{9,8},{10,14... | collective-permute-start | bytes 884744 | tf_op jit(solution)/shard_map/ppermute | solution.py:469
  43.3 6.2 %collective-permute-start.11 = (bf16[9,64,128]{2,1,0:T(8,128)(2,1)S(1)}, bf16[9,64,128]{2,1,0:T(8,128)(2,1)S(1)}, u32[]{:S(2)}, u32[]{:S(2)}) collective-permute-start(bf16[9,64,128]{2,1,0:T(8,128)(2,1)S(1)} %get-tuple-element.73), channel_id=1, source_target_pairs={{0,4},{1,5},{2,3},{3,2},{4,0},{5,1},{6,7},{7,6},{8,12},{9,13},{10,... | collective-permute-start | bytes 442376 | tf_op jit(solution)/shard_map/ppermute | solution.py:474
  47.0 5.6 %collective-permute-start.18 = (bf16[9,64,128]{2,1,0:T(8,128)(2,1)S(1)}, bf16[9,64,128]{2,1,0:T(8,128)(2,1)S(1)}, u32[]{:S(2)}, u32[]{:S(2)}) collective-permute-start(bf16[9,64,128]{2,1,0:T(8,128)(2,1)S(1)} %get-tuple-element.76), channel_id=1, source_target_pairs={{0,4},{1,5},{2,3},{3,2},{4,0},{5,1},{6,7},{7,6},{8,12},{9,13},{10,... | collective-permute-start | bytes 442376 | tf_op jit(solution)/shard_map/ppermute | solution.py:475
  49.5 5.9 %collective-permute-start.13 = (bf16[9,64,128]{2,1,0:T(8,128)(2,1)S(1)}, bf16[9,64,128]{2,1,0:T(8,128)(2,1)S(1)}, u32[]{:S(2)}, u32[]{:S(2)}) collective-permute-start(bf16[9,64,128]{2,1,0:T(8,128)(2,1)S(1)} %add_convert_fusion.5), channel_id=1, source_target_pairs={{0,8},{2,18},{4,12},{6,22},{8,0},{10,26},{12,4},{14,30},{16,24},{1... | collective-permute-start | bytes 442376 | tf_op jit(solution)/shard_map/ppermute | solution.py:339
  51.3 10.8 %collective-permute-start.12 = (bf16[16,48,128]{2,1,0:T(8,128)(2,1)S(1)}, bf16[16,48,128]{2,1,0:T(8,128)(2,1)S(1)}, u32[]{:S(2)}, u32[]{:S(2)}) collective-permute-start(bf16[16,48,128]{2,1,0:T(8,128)(2,1)S(1)} %get-tuple-element.80), channel_id=1, source_target_pairs={{0,1},{1,0},{2,3},{3,2},{4,5},{5,4},{6,7},{7,6},{8,9},{9,8},{10,11... | collective-permute-start | bytes 589832 | tf_op jit(solution)/shard_map/ppermute | solution.py:366
  52.6 6.2 %collective-permute-start.19 = (bf16[9,64,128]{2,1,0:T(8,128)(2,1)S(1)}, bf16[9,64,128]{2,1,0:T(8,128)(2,1)S(1)}, u32[]{:S(2)}, u32[]{:S(2)}) collective-permute-start(bf16[9,64,128]{2,1,0:T(8,128)(2,1)S(1)} %add_convert_fusion.2), channel_id=1, source_target_pairs={{0,8},{2,18},{4,12},{6,22},{8,0},{10,26},{12,4},{14,30},{16,24},{1... | collective-permute-start | bytes 442376 | tf_op jit(solution)/shard_map/ppermute | solution.py:339
  55.4 6.8 %collective-permute-start.14 = (bf16[9,64,128]{2,1,0:T(8,128)(2,1)S(1)}, bf16[9,64,128]{2,1,0:T(8,128)(2,1)S(1)}, u32[]{:S(2)}, u32[]{:S(2)}) collective-permute-start(bf16[9,64,128]{2,1,0:T(8,128)(2,1)S(1)} %add_convert_fusion.4), channel_id=1, source_target_pairs={{0,16},{2,10},{4,20},{6,14},{8,24},{10,2},{12,28},{14,6},{16,0},{1... | collective-permute-start | bytes 442376 | tf_op jit(solution)/shard_map/ppermute | solution.py:339
  58.8 8.4 %collective-permute-start.20 = (bf16[9,64,128]{2,1,0:T(8,128)(2,1)S(1)}, bf16[9,64,128]{2,1,0:T(8,128)(2,1)S(1)}, u32[]{:S(2)}, u32[]{:S(2)}) collective-permute-start(bf16[9,64,128]{2,1,0:T(8,128)(2,1)S(1)} %add_convert_fusion.1), channel_id=1, source_target_pairs={{0,16},{2,10},{4,20},{6,14},{8,24},{10,2},{12,28},{14,6},{16,0},{1... | collective-permute-start | bytes 442376 | tf_op jit(solution)/shard_map/ppermute | solution.py:339
  62.1 10.4 %copy-start.4 = (bf16[16,96,128]{2,1,0:T(8,128)(2,1)}, bf16[16,96,128]{2,1,0:T(8,128)(2,1)S(1)}, u32[]{:S(2)}) copy-start(bf16[16,96,128]{2,1,0:T(8,128)(2,1)S(1)} %constant_dynamic-update-slice_fusion) | copy-start | bytes 1179652
  62.3 6.7 %collective-permute-start.15 = (bf16[9,64,128]{2,1,0:T(8,128)(2,1)S(1)}, bf16[9,64,128]{2,1,0:T(8,128)(2,1)S(1)}, u32[]{:S(2)}, u32[]{:S(2)}) collective-permute-start(bf16[9,64,128]{2,1,0:T(8,128)(2,1)S(1)} %add_convert_fusion.3), channel_id=1, source_target_pairs={{0,4},{2,6},{4,0},{6,2},{8,12},{10,14},{12,8},{14,10},{16,20},{18,... | collective-permute-start | bytes 442376 | tf_op jit(solution)/shard_map/ppermute | solution.py:496
  67.3 5.2 %collective-permute-start.21 = (bf16[9,64,128]{2,1,0:T(8,128)(2,1)S(1)}, bf16[9,64,128]{2,1,0:T(8,128)(2,1)S(1)}, u32[]{:S(2)}, u32[]{:S(2)}) collective-permute-start(bf16[9,64,128]{2,1,0:T(8,128)(2,1)S(1)} %add_convert_fusion), channel_id=1, source_target_pairs={{0,4},{2,6},{4,0},{6,2},{8,12},{10,14},{12,8},{14,10},{16,20},{18,... | collective-permute-start | bytes 442376 | tf_op jit(solution)/shard_map/ppermute | solution.py:497
  69.0 3.7 %collective-permute-start.16 = (bf16[9,128,128]{2,1,0:T(8,128)(2,1)S(1)}, bf16[9,128,128]{2,1,0:T(8,128)(2,1)S(1)}, u32[]{:S(2)}, u32[]{:S(2)}) collective-permute-start(bf16[9,128,128]{2,1,0:T(8,128)(2,1)S(1)} %pad_maximum_fusion.1.here), channel_id=1, source_target_pairs={{0,2},{2,0},{4,6},{6,4},{8,10},{10,8},{12,14},{14,12},{16,18},{18,... | collective-permute-start | bytes 884744 | tf_op jit(solution)/shard_map/ppermute | solution.py:345
  72.6 1.8 %collective-permute-start.22 = (bf16[9,128,128]{2,1,0:T(8,128)(2,1)S(1)}, bf16[9,128,128]{2,1,0:T(8,128)(2,1)S(1)}, u32[]{:S(2)}, u32[]{:S(2)}) collective-permute-start(bf16[9,128,128]{2,1,0:T(8,128)(2,1)S(1)} %pad_maximum_fusion.2.here), channel_id=1, source_target_pairs={{0,2},{2,0},{4,6},{6,4},{8,10},{10,8},{12,14},{14,12},{16,18},{18,... | collective-permute-start | bytes 884744 | tf_op jit(solution)/shard_map/ppermute | solution.py:345

commit v6 on v5

--- a/solution.py
+++ b/solution.py
@@ -138,21 +138,29 @@
                 act_out[c - 2] = act[OFF : OFF + hl].astype(BF16)
 
 
-def cut_kernel(rows_at, where, features, first, second, cot, edge, send1, send2, low, high, sem):
-    iy, ix = where[0], where[1]
-    core = lax.rem(ix, 2)
-    wl, size = features.shape[1], send1.shape[1]
-    at = pl.multiple_of(core * size, size)
-    pairs = [(first.at[:, pl.ds(at, size), :], send1), (second.at[:, pl.ds(at, size), :], send2)]
-    pairs += [(cot.at[0:2], low), (cot.at[wl - 2 : wl], high)]
-    for n, h0 in enumerate(rows_at):
-        h0 = jnp.where(iy == 0, h0[0], h0[1])
-        pairs.append((features.at[pl.ds(h0, HALO)], edge.at[n]))
+def run_copies(pairs, sem):
     copies = [pltpu.make_async_copy(src, dst, sem.at[n]) for n, (src, dst) in enumerate(pairs)]
     for copy in copies:
         copy.start()
     for copy in copies:
         copy.wait()
+
+
+def cut_kernel(rows_at, where, features, first, edge, send, sem):
+    iy, ix = where[0], where[1]
+    size = send.shape[1]
+    at = pl.multiple_of(lax.rem(ix, 2) * size, size)
+    pairs = [(first.at[:, pl.ds(at, size), :], send)]
+    for n, h0 in enumerate(rows_at):
+        h0 = jnp.where(iy == 0, h0[0], h0[1])
+        pairs.append((features.at[pl.ds(h0, HALO)], edge.at[n]))
+    run_copies(pairs, sem)
+
+
+def cut_later_kernel(where, second, cot, send, low, high, sem):
+    size, wl = send.shape[1], cot.shape[0]
+    at = pl.multiple_of(lax.rem(where[1], 2) * size, size)
+    run_copies([(second.at[:, pl.ds(at, size), :], send), (cot.at[0:2], low), (cot.at[wl - 2 : wl], high)], sem)
 
 
 def edge_kernel(dims, where, ft, up, down, ct_low, ct_high, low, high):
@@ -381,12 +389,20 @@
 
     half = co // 2
     rows_at = [(hl - HALO, 0)] if ny == 2 else [(hl - HALO, hl - HALO), (0, 0)]
-    edge_send, first_send, second_send, ct_low, ct_high = call(
+    half_shape = ((9, half, ch), BF16)
+    edge_send, first_send = call(
         functools.partial(cut_kernel, rows_at),
-        [((len(rows_at), HALO, wl, ch), BF16)] + [((9, half, ch), BF16)] * 2 + [((2, height, co), BF16)] * 2,
-        (where, features, first_own, second_own, ct),
-        [pltpu.SemaphoreType.DMA((4 + len(rows_at),))],
-        raw_args=(1, 2, 3, 4),
+        [((len(rows_at), HALO, wl, ch), BF16), half_shape],
+        (where, features, first_own),
+        [pltpu.SemaphoreType.DMA((1 + len(rows_at),))],
+        raw_args=(1, 2),
+    )
+    second_send, ct_low, ct_high = call(
+        cut_later_kernel,
+        [half_shape] + [((2, height, co), BF16)] * 2,
+        (after(where, edge_send), second_own, ct),
+        [pltpu.SemaphoreType.DMA((3,))],
+        raw_args=(1, 2),
     )
     up = jnp.transpose(round_y(edge_send[0], 1), (1, 0, 2))
     down = up if ny == 2 else jnp.transpose(round_y(edge_send[1], ny - 1), (1, 0, 2))

time: 76.8 us -> 76.6 us (level)
  waiting for transfers between devices: 17.7 us -> 16.2 us
  Pallas kernels: 21.2 us -> 22.6 us
    ppermute x5, waiting for transfers between devices: 6.34 us -> 4.78 us  [round_y(): return lax.ppermute(x, 'gy', [(i, (i + d) % ny) for i in range(ny)])]
    pallas_call x13 -> x14, Pallas kernels: 21.2 us -> 22.6 us  [call(): pl.pallas_call(kernel, out_shape=[jax.ShapeDtypeStruct(s, t) for s, t in...]
  transfers between devices with their start and end apart: 23 -> 23, of which waited for: 13 -> 13; matrix products, arithmetic and copies ran while one was open for 1% -> 1% of each run, Pallas kernels for 19% -> 21%
where the time goes in v6:
time: 76.6 us; the launch traced here: 75.9 us
  starting transfers between devices  35.2 us (46%)
  Pallas kernels  22.6 us (30%)
  waiting for transfers between devices  16.2 us (21%)
  between operations  0.96 us (1%)
    pallas_call x14, Pallas kernels, call(): pl.pallas_call(kernel, out_shape=[jax.ShapeDtypeStruct(s, t) for s, t in...  22.6 us
    ppermute x4, starting transfers between devices, far_partner(): lax.ppermute(total, 'gx', [(g, g ^ (near if g % 2 == 0 else far)) for g i...  9.36 us
    ppermute x5, starting transfers between devices, round_y(): return lax.ppermute(x, 'gy', [(i, (i + d) % ny) for i in range(ny)])  7.34 us
    ppermute x5, waiting for transfers between devices, round_y(): return lax.ppermute(x, 'gy', [(i, (i + d) % ny) for i in range(ny)])  4.78 us
    ppermute x4, waiting for transfers between devices, far_partner(): lax.ppermute(total, 'gx', [(g, g ^ (near if g % 2 == 0 else far)) for g i...  3.71 us
    ppermute x1, waiting for transfers between devices, body(): beside2 = lax.ppermute(total2, 'gx', [(g, g ^ 2) for g in range(nx)])  3.45 us
    ppermute x1, starting transfers between devices, body(): beside1 = lax.ppermute(total1, 'gx', [(g, g ^ 2) for g in range(nx)])  3.06 us
    ppermute x4, starting transfers between devices, pass_core(): return lax.ppermute(mine, 'gx', [(i, i ^ 1) for i in range(nx)])  3.04 us
  transfers between devices with their start and end apart: 23, of which 13 were waited for; matrix products, arithmetic and copies ran while one was open for 1% of the time, Pallas kernels for 21%

profile of v6, /device:TPU:0, one launch (start us, length us, event | category | flops | bytes accessed | tf_op | source)
XLA Modules:
  0.0 75.9 jit_solution(2638846643708210048)
XLA Ops:
  0.7 1.5 %shard_map.75 = (bf16[1,4,16,256]{3,2,1,0:T(8,128)(2,1)S(1)}, bf16[9,64,256]{2,1,0:T(8,128)(2,1)S(1)}) custom-call(s32[2]{0:T(128)S(1)} %pad_add_fusion.where, bf16[48,16,256]{2,1,0:T(8,128)(2,1)} %features.1, bf16[9,128,256]{2,1,0:T(8,128)(2,1)} %bitcast.27), custom_call_target="tpu_custom_call" | custom-call | tf_op jit(solution)/shard_map/pallas_call | solution.py:26
  2.3 3.0 %collective-permute-start = (bf16[4,16,256]{2,0,1:T(4,128)(2,1)S(1)}, bf16[4,16,256]{2,0,1:T(4,128)(2,1)S(1)}, u32[]{:S(2)}, u32[]{:S(2)}) collective-permute-start(bf16[4,16,256]{2,0,1:T(4,128)(2,1)S(1)} %bitcast.50), channel_id=1, source_target_pairs={{0,1},{1,0},{2,3},{3,2},{4,5},{5,4},{6,7},{7,6},{8,9},{9,8},{10,11... | collective-permute-start | bytes 98312 | tf_op jit(solution)/shard_map/ppermute | solution.py:374
  5.4 1.5 %shard_map.76 = (bf16[9,64,256]{2,1,0:T(8,128)(2,1)S(1)}, bf16[2,96,128]{2,1,0:T(8,128)(2,1)S(1)}, bf16[2,96,128]{2,1,0:T(8,128)(2,1)S(1)}) custom-call(s32[2]{0:T(128)S(1)} %pad_add_fusion.where, bf16[9,128,256]{2,1,0:T(8,128)(2,1)} %bitcast.32, bf16[16,96,128]{2,1,0:T(8,128)(2,1)} %bitcast.43), custom_call_target="tpu_custom_call" | custom-call | tf_op jit(solution)/shard_map/pallas_call | solution.py:26
  7.2 2.4 %collective-permute-start.3 = (bf16[9,64,256]{2,1,0:T(8,128)(2,1)S(1)}, bf16[9,64,256]{2,1,0:T(8,128)(2,1)S(1)}, u32[]{:S(2)}, u32[]{:S(2)}) collective-permute-start(bf16[9,64,256]{2,1,0:T(8,128)(2,1)S(1)} %get-tuple-element.50), channel_id=1, source_target_pairs={{0,1},{1,0},{2,3},{3,2},{4,5},{5,4},{6,7},{7,6},{8,9},{9,8},{10,11... | collective-permute-start | bytes 884744 | tf_op jit(solution)/shard_map/ppermute | solution.py:374
  10.3 1.3 %collective-permute-start.2 = (bf16[640,128]{1,0:T(8,128)(2,1)S(1)}, bf16[640,128]{1,0:T(8,128)(2,1)S(1)}, u32[]{:S(2)}, u32[]{:S(2)}) collective-permute-start(bf16[640,128]{1,0:T(8,128)(2,1)S(1)} %get-tuple-element.48), channel_id=1, source_target_pairs={{2,0},{4,2},{6,4},{8,6},{10,8},{12,10},{14,12},{16,14},{18,16},{20... | collective-permute-start | bytes 491528 | tf_op jit(solution)/shard_map/ppermute | solution.py:422
  11.6 3.0 %collective-permute-start.1 = (bf16[640,128]{1,0:T(8,128)(2,1)S(1)}, bf16[640,128]{1,0:T(8,128)(2,1)S(1)}, u32[]{:S(2)}, u32[]{:S(2)}) collective-permute-start(bf16[640,128]{1,0:T(8,128)(2,1)S(1)} %get-tuple-element.47), channel_id=1, source_target_pairs={{0,2},{2,4},{4,6},{6,8},{8,10},{10,12},{12,14},{14,16},{16,18},{18... | collective-permute-start | bytes 491528 | tf_op jit(solution)/shard_map/ppermute | solution.py:421
  14.7 0.9 %collective-permute-done.1.left = bf16[640,128]{1,0:T(8,128)(2,1)S(1)} collective-permute-done((bf16[640,128]{1,0:T(8,128)(2,1)S(1)}, bf16[640,128]{1,0:T(8,128)(2,1)S(1)}, u32[]{:S(2)}, u32[]{:S(2)}) %collective-permute-start.1) | collective-permute-done | bytes 163872 | tf_op jit(solution)/shard_map/ppermute | solution.py:421
  15.8 2.4 %collective-permute-start.5 = (bf16[1,1,9,64,256]{4,3,2,1,0:T(8,128)(2,1)S(1)}, bf16[1,1,9,64,256]{4,3,2,1,0:T(8,128)(2,1)S(1)}, u32[]{:S(2)}, u32[]{:S(2)}) collective-permute-start(bf16[1,1,9,64,256]{4,3,2,1,0:T(8,128)(2,1)S(1)} %bitcast.34), channel_id=1, source_target_pairs={{0,2},{2,0},{4,6},{6,4},{8,10},{10,8},{12,14},{14,12},{16,18},{18,... | collective-permute-start | bytes 884744 | tf_op jit(solution)/shard_map/ppermute | solution.py:383
  18.2 1.9 %collective-permute-done.3 = bf16[9,64,256]{2,1,0:T(8,128)(2,1)S(1)} collective-permute-done((bf16[9,64,256]{2,1,0:T(8,128)(2,1)S(1)}, bf16[9,64,256]{2,1,0:T(8,128)(2,1)S(1)}, u32[]{:S(2)}, u32[]{:S(2)}) %collective-permute-start.3) | collective-permute-done | bytes 294944 | tf_op jit(solution)/shard_map/ppermute | solution.py:374
  20.2 1.0 %collective-permute-start.7 = (bf16[20,56,128]{2,1,0:T(8,128)(2,1)S(1)}, bf16[20,56,128]{2,1,0:T(8,128)(2,1)S(1)}, u32[]{:S(2)}, u32[]{:S(2)}) collective-permute-start(bf16[20,56,128]{2,1,0:T(8,128)(2,1)S(1)} %get-tuple-element.81), channel_id=1, source_target_pairs={{0,1},{1,0},{2,3},{3,2},{4,5},{5,4},{6,7},{7,6},{8,9},{9,8},{10,11... | collective-permute-start | bytes 860168 | tf_op jit(solution)/shard_map/ppermute | solution.py:374
  21.2 3.0 %shard_map.78 = (bf16[22,64,256]{2,1,0:T(8,128)(2,1)S(1)}, f32[18,64,256]{2,1,0:T(8,128)S(1)}, bf16[24,64,256]{2,1,0:T(8,128)(2,1)S(1)}) custom-call(s32[2]{0:T(128)S(1)} %pad_add_fusion.where, bf16[16,48,256]{2,1,0:T(8,128)(2,1)S(1)} %bitcast.31, bf16[640,128]{1,0:T(8,128)(2,1)S(1)} %collective-permute-done.1.left, ...), custom_call_target="tpu_custom_call" | custom-call | tf_op jit(solution)/shard_map/pallas_call | solution.py:26
  24.2 2.7 %shard_map.79 = (bf16[16,48,256]{2,1,0:T(8,128)(2,1)S(1)}, f32[20,64,256]{2,1,0:T(8,128)S(1)}, bf16[9,256,256]{2,1,0:T(8,128)(2,1)S(1)}) custom-call(s32[2]{0:T(128)S(1)} %pad_add_fusion.where, bf16[22,64,256]{2,1,0:T(8,128)(2,1)S(1)} %get-tuple-element.54.hidden, bf16[9,128,256]{2,1,0:T(8,128)(2,1)S(1)} %bitcast.33, ...), custom_call_target="tpu_custom_call" | custom-call | tf_op jit(solution)/shard_map/pallas_call | solution.py:26
  26.9 2.6 %collective-permute-done.7.refs_1_ = bf16[20,56,128]{2,1,0:T(8,128)(2,1)S(1)} collective-permute-done((bf16[20,56,128]{2,1,0:T(8,128)(2,1)S(1)}, bf16[20,56,128]{2,1,0:T(8,128)(2,1)S(1)}, u32[]{:S(2)}, u32[]{:S(2)}) %collective-permute-start.7) | collective-permute-done | bytes 286752 | tf_op jit(solution)/shard_map/ppermute | solution.py:374
  29.5 3.5 %shard_map.80 = (bf16[18,64,256]{2,1,0:T(8,128)(2,1)S(1)}, bf16[20,64,256]{2,1,0:T(8,128)(2,1)S(1)}, f32[9,256,128]{2,1,0:T(8,128)S(1)}, bf16[9,256,128]{2,1,0:T(8,128)(2,1)S(1)}) custom-call(s32[2]{0:T(128)S(1)} %pad_add_fusion.where, bf16[9,256,256]{2,1,0:T(8,128)(2,1)S(1)} %get-tuple-element.56.w, f32[20,64,256]{2,1,0:T(8,128)S(1)} %get-tuple-element.57.slope2, ...), custom_call_target="tpu_custom_call" | custom-call | tf_op jit(solution)/shard_map/pallas_call | solution.py:26
  33.1 2.0 %shard_map.82 = (f32[9,256,128]{2,1,0:T(8,128)S(1)}, bf16[9,256,128]{2,1,0:T(8,128)(2,1)S(1)}) custom-call(s32[2]{0:T(128)S(1)} %pad_add_fusion.where, bf16[22,64,256]{2,1,0:T(8,128)(2,1)S(1)} %get-tuple-element.54.hidden, bf16[20,64,256]{2,1,0:T(8,128)(2,1)S(1)} %get-tuple-element.65.outer), custom_call_target="tpu_custom_call" | custom-call | tf_op jit(solution)/shard_map/pallas_call | solution.py:26
  36.3 1.0 %collective-permute-start.9 = (bf16[9,128,128]{2,1,0:T(8,128)(2,1)S(1)}, bf16[9,128,128]{2,1,0:T(8,128)(2,1)S(1)}, u32[]{:S(2)}, u32[]{:S(2)}) collective-permute-start(bf16[9,128,128]{2,1,0:T(8,128)(2,1)S(1)} %get-tuple-element.64), channel_id=1, source_target_pairs={{0,1},{1,0},{2,6},{3,7},{4,5},{5,4},{6,2},{7,3},{8,9},{9,8},{10,14... | collective-permute-start | bytes 884744 | tf_op jit(solution)/shard_map/ppermute | solution.py:484
  38.0 1.1 %collective-permute-start.17 = (bf16[9,128,128]{2,1,0:T(8,128)(2,1)S(1)}, bf16[9,128,128]{2,1,0:T(8,128)(2,1)S(1)}, u32[]{:S(2)}, u32[]{:S(2)}) collective-permute-start(bf16[9,128,128]{2,1,0:T(8,128)(2,1)S(1)} %get-tuple-element.71), channel_id=1, source_target_pairs={{0,1},{1,0},{2,6},{3,7},{4,5},{5,4},{6,2},{7,3},{8,9},{9,8},{10,14... | collective-permute-start | bytes 884744 | tf_op jit(solution)/shard_map/ppermute | solution.py:485
  39.1 3.1 %shard_map.84 = bf16[48,16,256]{2,1,0:T(8,128)(2,1)} custom-call(s32[2]{0:T(128)S(1)} %pad_add_fusion.where, bf16[18,64,256]{2,1,0:T(8,128)(2,1)S(1)} %get-tuple-element.72.inner, bf16[9,128,256]{2,1,0:T(8,128)(2,1)S(1)} %bitcast.29, bf16[1,1,9,64,256]{4,3,2,1,0:T(8,128)(2,1)S(1)} %bitcast.36, bf16[1,1,9,64,256]{4,3,2,1,0:T(8,128)(2,1)S(1)} %collective-permute-done.5.other), custom_call_target="tpu_custom_call" | custom-call | tf_op jit(solution)/shard_map/pallas_call | solution.py:26
  43.1 1.8 %collective-permute-start.11 = (bf16[9,64,128]{2,1,0:T(8,128)(2,1)S(1)}, bf16[9,64,128]{2,1,0:T(8,128)(2,1)S(1)}, u32[]{:S(2)}, u32[]{:S(2)}) collective-permute-start(bf16[9,64,128]{2,1,0:T(8,128)(2,1)S(1)} %get-tuple-element.75), channel_id=1, source_target_pairs={{0,4},{1,5},{2,3},{3,2},{4,0},{5,1},{6,7},{7,6},{8,12},{9,13},{10,... | collective-permute-start | bytes 442376 | tf_op jit(solution)/shard_map/ppermute | solution.py:490
  44.9 1.8 %collective-permute-done.17.came = bf16[9,128,128]{2,1,0:T(8,128)(2,1)S(1)} collective-permute-done((bf16[9,128,128]{2,1,0:T(8,128)(2,1)S(1)}, bf16[9,128,128]{2,1,0:T(8,128)(2,1)S(1)}, u32[]{:S(2)}, u32[]{:S(2)}) %collective-permute-start.17) | collective-permute-done | bytes 294944 | tf_op jit(solution)/shard_map/ppermute | solution.py:485
  46.8 2.5 %collective-permute-start.18 = (bf16[9,64,128]{2,1,0:T(8,128)(2,1)S(1)}, bf16[9,64,128]{2,1,0:T(8,128)(2,1)S(1)}, u32[]{:S(2)}, u32[]{:S(2)}) collective-permute-start(bf16[9,64,128]{2,1,0:T(8,128)(2,1)S(1)} %get-tuple-element.78), channel_id=1, source_target_pairs={{0,4},{1,5},{2,3},{3,2},{4,0},{5,1},{6,7},{7,6},{8,12},{9,13},{10,... | collective-permute-start | bytes 442376 | tf_op jit(solution)/shard_map/ppermute | solution.py:491
  49.4 1.6 %collective-permute-start.13 = (bf16[9,64,128]{2,1,0:T(8,128)(2,1)S(1)}, bf16[9,64,128]{2,1,0:T(8,128)(2,1)S(1)}, u32[]{:S(2)}, u32[]{:S(2)}) collective-permute-start(bf16[9,64,128]{2,1,0:T(8,128)(2,1)S(1)} %add_convert_fusion.5), channel_id=1, source_target_pairs={{0,8},{2,18},{4,12},{6,22},{8,0},{10,26},{12,4},{14,30},{16,24},{1... | collective-permute-start | bytes 442376 | tf_op jit(solution)/shard_map/ppermute | solution.py:347
  52.5 1.8 %collective-permute-start.19 = (bf16[9,64,128]{2,1,0:T(8,128)(2,1)S(1)}, bf16[9,64,128]{2,1,0:T(8,128)(2,1)S(1)}, u32[]{:S(2)}, u32[]{:S(2)}) collective-permute-start(bf16[9,64,128]{2,1,0:T(8,128)(2,1)S(1)} %add_convert_fusion.2), channel_id=1, source_target_pairs={{0,8},{2,18},{4,12},{6,22},{8,0},{10,26},{12,4},{14,30},{16,24},{1... | collective-permute-start | bytes 442376 | tf_op jit(solution)/shard_map/ppermute | solution.py:347
  54.3 1.0 %collective-permute-done.13 = bf16[9,64,128]{2,1,0:T(8,128)(2,1)S(1)} collective-permute-done((bf16[9,64,128]{2,1,0:T(8,128)(2,1)S(1)}, bf16[9,64,128]{2,1,0:T(8,128)(2,1)S(1)}, u32[]{:S(2)}, u32[]{:S(2)}) %collective-permute-start.13) | collective-permute-done | bytes 147488 | tf_op jit(solution)/shard_map/ppermute | solution.py:347
  55.3 2.7 %collective-permute-start.14 = (bf16[9,64,128]{2,1,0:T(8,128)(2,1)S(1)}, bf16[9,64,128]{2,1,0:T(8,128)(2,1)S(1)}, u32[]{:S(2)}, u32[]{:S(2)}) collective-permute-start(bf16[9,64,128]{2,1,0:T(8,128)(2,1)S(1)} %add_convert_fusion.4), channel_id=1, source_target_pairs={{0,16},{2,10},{4,20},{6,14},{8,24},{10,2},{12,28},{14,6},{16,0},{1... | collective-permute-start | bytes 442376 | tf_op jit(solution)/shard_map/ppermute | solution.py:347
  58.7 3.2 %collective-permute-start.20 = (bf16[9,64,128]{2,1,0:T(8,128)(2,1)S(1)}, bf16[9,64,128]{2,1,0:T(8,128)(2,1)S(1)}, u32[]{:S(2)}, u32[]{:S(2)}) collective-permute-start(bf16[9,64,128]{2,1,0:T(8,128)(2,1)S(1)} %add_convert_fusion.1), channel_id=1, source_target_pairs={{0,16},{2,10},{4,20},{6,14},{8,24},{10,2},{12,28},{14,6},{16,0},{1... | collective-permute-start | bytes 442376 | tf_op jit(solution)/shard_map/ppermute | solution.py:347
  62.2 3.1 %collective-permute-start.15 = (bf16[9,64,128]{2,1,0:T(8,128)(2,1)S(1)}, bf16[9,64,128]{2,1,0:T(8,128)(2,1)S(1)}, u32[]{:S(2)}, u32[]{:S(2)}) collective-permute-start(bf16[9,64,128]{2,1,0:T(8,128)(2,1)S(1)} %add_convert_fusion.3), channel_id=1, source_target_pairs={{0,4},{2,6},{4,0},{6,2},{8,12},{10,14},{12,8},{14,10},{16,20},{18,... | collective-permute-start | bytes 442376 | tf_op jit(solution)/shard_map/ppermute | solution.py:512
  65.2 1.9 %collective-permute-done.20 = bf16[9,64,128]{2,1,0:T(8,128)(2,1)S(1)} collective-permute-done((bf16[9,64,128]{2,1,0:T(8,128)(2,1)S(1)}, bf16[9,64,128]{2,1,0:T(8,128)(2,1)S(1)}, u32[]{:S(2)}, u32[]{:S(2)}) %collective-permute-start.20) | collective-permute-done | bytes 147488 | tf_op jit(solution)/shard_map/ppermute | solution.py:347
  67.2 1.5 %collective-permute-start.21 = (bf16[9,64,128]{2,1,0:T(8,128)(2,1)S(1)}, bf16[9,64,128]{2,1,0:T(8,128)(2,1)S(1)}, u32[]{:S(2)}, u32[]{:S(2)}) collective-permute-start(bf16[9,64,128]{2,1,0:T(8,128)(2,1)S(1)} %add_convert_fusion), channel_id=1, source_target_pairs={{0,4},{2,6},{4,0},{6,2},{8,12},{10,14},{12,8},{14,10},{16,20},{18,... | collective-permute-start | bytes 442376 | tf_op jit(solution)/shard_map/ppermute | solution.py:513
  68.9 3.5 %collective-permute-done.21 = bf16[9,64,128]{2,1,0:T(8,128)(2,1)S(1)} collective-permute-done((bf16[9,64,128]{2,1,0:T(8,128)(2,1)S(1)}, bf16[9,64,128]{2,1,0:T(8,128)(2,1)S(1)}, u32[]{:S(2)}, u32[]{:S(2)}) %collective-permute-start.21) | collective-permute-done | bytes 147488 | tf_op jit(solution)/shard_map/ppermute | solution.py:513
  72.6 1.7 %shard_map.86 = f32[9,128,256]{2,1,0:T(8,128)} custom-call(s32[2]{0:T(128)S(1)} %pad_add_fusion.where, bf16[9,128,128]{2,1,0:T(8,128)(2,1)S(1)} %pad_maximum_fusion.1.here, bf16[9,128,128]{2,1,0:T(8,128)(2,1)S(1)} %collective-permute-done.16.there), custom_call_target="tpu_custom_call" | custom-call | tf_op jit(solution)/shard_map/pallas_call | solution.py:26
  74.2 1.7 %shard_map.88 = f32[9,128,256]{2,1,0:T(8,128)} custom-call(s32[2]{0:T(128)S(1)} %pad_add_fusion.where, bf16[9,128,128]{2,1,0:T(8,128)(2,1)S(1)} %pad_maximum_fusion.2.here, bf16[9,128,128]{2,1,0:T(8,128)(2,1)S(1)} %collective-permute-done.22.there), custom_call_target="tpu_custom_call" | custom-call | tf_op jit(solution)/shard_map/pallas_call | solution.py:26
  (58 shorter events, 7.1 us)
Async XLA Ops:
  0.6 9.0 %copy-start.2 = (bf16[48,16,256]{2,1,0:T(8,128)(2,1)S(1)}, bf16[48,16,256]{2,1,0:T(8,128)(2,1)}, u32[]{:S(2)}) copy-start(bf16[48,16,256]{2,1,0:T(8,128)(2,1)} %features.1) | copy-start | bytes 1179652
  2.3 4.9 %collective-permute-start = (bf16[4,16,256]{2,0,1:T(4,128)(2,1)S(1)}, bf16[4,16,256]{2,0,1:T(4,128)(2,1)S(1)}, u32[]{:S(2)}, u32[]{:S(2)}) collective-permute-start(bf16[4,16,256]{2,0,1:T(4,128)(2,1)S(1)} %bitcast.50), channel_id=1, source_target_pairs={{0,1},{1,0},{2,3},{3,2},{4,5},{5,4},{6,7},{7,6},{8,9},{9,8},{10,11... | collective-permute-start | bytes 98312 | tf_op jit(solution)/shard_map/ppermute | solution.py:374
  5.3 10.4 %collective-permute-start.4 = (bf16[9,64,256]{2,1,0:T(8,128)(2,1)S(1)}, bf16[9,64,256]{2,1,0:T(8,128)(2,1)S(1)}, u32[]{:S(2)}, u32[]{:S(2)}) collective-permute-start(bf16[9,64,256]{2,1,0:T(8,128)(2,1)S(1)} %get-tuple-element.52), channel_id=1, source_target_pairs={{0,1},{1,0},{2,3},{3,2},{4,5},{5,4},{6,7},{7,6},{8,9},{9,8},{10,11... | collective-permute-start | bytes 884744 | tf_op jit(solution)/shard_map/ppermute | solution.py:374
  5.4 10.3 %copy-start.3 = (bf16[128,16,96]{0,2,1:T(8,128)(2,1)S(1)}, bf16[128,16,96]{0,2,1:T(8,128)(2,1)}, u32[]{:S(2)}) copy-start(bf16[128,16,96]{0,2,1:T(8,128)(2,1)} %param.7) | copy-start | bytes 1179652
  7.2 12.9 %collective-permute-start.3 = (bf16[9,64,256]{2,1,0:T(8,128)(2,1)S(1)}, bf16[9,64,256]{2,1,0:T(8,128)(2,1)S(1)}, u32[]{:S(2)}, u32[]{:S(2)}) collective-permute-start(bf16[9,64,256]{2,1,0:T(8,128)(2,1)S(1)} %get-tuple-element.50), channel_id=1, source_target_pairs={{0,1},{1,0},{2,3},{3,2},{4,5},{5,4},{6,7},{7,6},{8,9},{9,8},{10,11... | collective-permute-start | bytes 884744 | tf_op jit(solution)/shard_map/ppermute | solution.py:374
  10.3 4.4 %collective-permute-start.2 = (bf16[640,128]{1,0:T(8,128)(2,1)S(1)}, bf16[640,128]{1,0:T(8,128)(2,1)S(1)}, u32[]{:S(2)}, u32[]{:S(2)}) collective-permute-start(bf16[640,128]{1,0:T(8,128)(2,1)S(1)} %get-tuple-element.48), channel_id=1, source_target_pairs={{2,0},{4,2},{6,4},{8,6},{10,8},{12,10},{14,12},{16,14},{18,16},{20... | collective-permute-start | bytes 491528 | tf_op jit(solution)/shard_map/ppermute | solution.py:422
  11.6 4.0 %collective-permute-start.1 = (bf16[640,128]{1,0:T(8,128)(2,1)S(1)}, bf16[640,128]{1,0:T(8,128)(2,1)S(1)}, u32[]{:S(2)}, u32[]{:S(2)}) collective-permute-start(bf16[640,128]{1,0:T(8,128)(2,1)S(1)} %get-tuple-element.47), channel_id=1, source_target_pairs={{0,2},{2,4},{4,6},{6,8},{8,10},{10,12},{12,14},{14,16},{16,18},{18... | collective-permute-start | bytes 491528 | tf_op jit(solution)/shard_map/ppermute | solution.py:421
  14.7 6.6 %copy-start = (bf16[128,3,3,256]{3,0,2,1:T(8,128)(2,1)S(1)}, bf16[128,3,3,256]{3,0,2,1:T(8,128)(2,1)}, u32[]{:S(2)}) copy-start(bf16[128,3,3,256]{3,0,2,1:T(8,128)(2,1)} %param.5) | copy-start | bytes 1769476
  15.8 5.5 %collective-permute-start.5 = (bf16[1,1,9,64,256]{4,3,2,1,0:T(8,128)(2,1)S(1)}, bf16[1,1,9,64,256]{4,3,2,1,0:T(8,128)(2,1)S(1)}, u32[]{:S(2)}, u32[]{:S(2)}) collective-permute-start(bf16[1,1,9,64,256]{4,3,2,1,0:T(8,128)(2,1)S(1)} %bitcast.34), channel_id=1, source_target_pairs={{0,2},{2,0},{4,6},{6,4},{8,10},{10,8},{12,14},{14,12},{16,18},{18,... | collective-permute-start | bytes 884744 | tf_op jit(solution)/shard_map/ppermute | solution.py:383
  20.1 4.1 %collective-permute-start.6 = (bf16[1,1,9,64,256]{4,3,2,1,0:T(8,128)(2,1)S(1)}, bf16[1,1,9,64,256]{4,3,2,1,0:T(8,128)(2,1)S(1)}, u32[]{:S(2)}, u32[]{:S(2)}) collective-permute-start(bf16[1,1,9,64,256]{4,3,2,1,0:T(8,128)(2,1)S(1)} %bitcast.41), channel_id=1, source_target_pairs={{0,2},{2,0},{4,6},{6,4},{8,10},{10,8},{12,14},{14,12},{16,18},{18,... | collective-permute-start | bytes 884744 | tf_op jit(solution)/shard_map/ppermute | solution.py:383
  20.2 4.0 %copy-start.1 = (bf16[128,3,3,256]{3,0,2,1:T(8,128)(2,1)S(1)}, bf16[128,3,3,256]{3,0,2,1:T(8,128)(2,1)}, u32[]{:S(2)}) copy-start(bf16[128,3,3,256]{3,0,2,1:T(8,128)(2,1)} %param.6) | copy-start | bytes 1769476
  20.2 9.3 %collective-permute-start.7 = (bf16[20,56,128]{2,1,0:T(8,128)(2,1)S(1)}, bf16[20,56,128]{2,1,0:T(8,128)(2,1)S(1)}, u32[]{:S(2)}, u32[]{:S(2)}) collective-permute-start(bf16[20,56,128]{2,1,0:T(8,128)(2,1)S(1)} %get-tuple-element.81), channel_id=1, source_target_pairs={{0,1},{1,0},{2,3},{3,2},{4,5},{5,4},{6,7},{7,6},{8,9},{9,8},{10,11... | collective-permute-start | bytes 860168 | tf_op jit(solution)/shard_map/ppermute | solution.py:374
  33.0 2.6 %collective-permute-start.8 = (bf16[9,256,128]{2,1,0:T(8,128)(2,1)S(1)}, bf16[9,256,128]{2,1,0:T(8,128)(2,1)S(1)}, u32[]{:S(2)}, u32[]{:S(2)}) collective-permute-start(bf16[9,256,128]{2,1,0:T(8,128)(2,1)S(1)} %get-tuple-element.61), channel_id=1, source_target_pairs={{0,2},{2,0},{4,6},{6,4},{8,10},{10,8},{12,14},{14,12},{16,18},{18,... | collective-permute-start | bytes 1769480 | tf_op jit(solution)/shard_map/ppermute | solution.py:383
  35.1 2.3 %collective-permute-start.10 = (bf16[9,256,128]{2,1,0:T(8,128)(2,1)S(1)}, bf16[9,256,128]{2,1,0:T(8,128)(2,1)S(1)}, u32[]{:S(2)}, u32[]{:S(2)}) collective-permute-start(bf16[9,256,128]{2,1,0:T(8,128)(2,1)S(1)} %get-tuple-element.68), channel_id=1, source_target_pairs={{0,2},{2,0},{4,6},{6,4},{8,10},{10,8},{12,14},{14,12},{16,18},{18,... | collective-permute-start | bytes 1769480 | tf_op jit(solution)/shard_map/ppermute | solution.py:383
  36.3 6.8 %collective-permute-start.9 = (bf16[9,128,128]{2,1,0:T(8,128)(2,1)S(1)}, bf16[9,128,128]{2,1,0:T(8,128)(2,1)S(1)}, u32[]{:S(2)}, u32[]{:S(2)}) collective-permute-start(bf16[9,128,128]{2,1,0:T(8,128)(2,1)S(1)} %get-tuple-element.64), channel_id=1, source_target_pairs={{0,1},{1,0},{2,6},{3,7},{4,5},{5,4},{6,2},{7,3},{8,9},{9,8},{10,14... | collective-permute-start | bytes 884744 | tf_op jit(solution)/shard_map/ppermute | solution.py:484
  38.0 8.8 %collective-permute-start.17 = (bf16[9,128,128]{2,1,0:T(8,128)(2,1)S(1)}, bf16[9,128,128]{2,1,0:T(8,128)(2,1)S(1)}, u32[]{:S(2)}, u32[]{:S(2)}) collective-permute-start(bf16[9,128,128]{2,1,0:T(8,128)(2,1)S(1)} %get-tuple-element.71), channel_id=1, source_target_pairs={{0,1},{1,0},{2,6},{3,7},{4,5},{5,4},{6,2},{7,3},{8,9},{9,8},{10,14... | collective-permute-start | bytes 884744 | tf_op jit(solution)/shard_map/ppermute | solution.py:485
  43.1 6.2 %collective-permute-start.11 = (bf16[9,64,128]{2,1,0:T(8,128)(2,1)S(1)}, bf16[9,64,128]{2,1,0:T(8,128)(2,1)S(1)}, u32[]{:S(2)}, u32[]{:S(2)}) collective-permute-start(bf16[9,64,128]{2,1,0:T(8,128)(2,1)S(1)} %get-tuple-element.75), channel_id=1, source_target_pairs={{0,4},{1,5},{2,3},{3,2},{4,0},{5,1},{6,7},{7,6},{8,12},{9,13},{10,... | collective-permute-start | bytes 442376 | tf_op jit(solution)/shard_map/ppermute | solution.py:490
  46.8 5.6 %collective-permute-start.18 = (bf16[9,64,128]{2,1,0:T(8,128)(2,1)S(1)}, bf16[9,64,128]{2,1,0:T(8,128)(2,1)S(1)}, u32[]{:S(2)}, u32[]{:S(2)}) collective-permute-start(bf16[9,64,128]{2,1,0:T(8,128)(2,1)S(1)} %get-tuple-element.78), channel_id=1, source_target_pairs={{0,4},{1,5},{2,3},{3,2},{4,0},{5,1},{6,7},{7,6},{8,12},{9,13},{10,... | collective-permute-start | bytes 442376 | tf_op jit(solution)/shard_map/ppermute | solution.py:491
  49.4 5.9 %collective-permute-start.13 = (bf16[9,64,128]{2,1,0:T(8,128)(2,1)S(1)}, bf16[9,64,128]{2,1,0:T(8,128)(2,1)S(1)}, u32[]{:S(2)}, u32[]{:S(2)}) collective-permute-start(bf16[9,64,128]{2,1,0:T(8,128)(2,1)S(1)} %add_convert_fusion.5), channel_id=1, source_target_pairs={{0,8},{2,18},{4,12},{6,22},{8,0},{10,26},{12,4},{14,30},{16,24},{1... | collective-permute-start | bytes 442376 | tf_op jit(solution)/shard_map/ppermute | solution.py:347
  51.2 10.8 %collective-permute-start.12 = (bf16[16,48,128]{2,1,0:T(8,128)(2,1)S(1)}, bf16[16,48,128]{2,1,0:T(8,128)(2,1)S(1)}, u32[]{:S(2)}, u32[]{:S(2)}) collective-permute-start(bf16[16,48,128]{2,1,0:T(8,128)(2,1)S(1)} %get-tuple-element.82), channel_id=1, source_target_pairs={{0,1},{1,0},{2,3},{3,2},{4,5},{5,4},{6,7},{7,6},{8,9},{9,8},{10,11... | collective-permute-start | bytes 589832 | tf_op jit(solution)/shard_map/ppermute | solution.py:374
  52.5 6.2 %collective-permute-start.19 = (bf16[9,64,128]{2,1,0:T(8,128)(2,1)S(1)}, bf16[9,64,128]{2,1,0:T(8,128)(2,1)S(1)}, u32[]{:S(2)}, u32[]{:S(2)}) collective-permute-start(bf16[9,64,128]{2,1,0:T(8,128)(2,1)S(1)} %add_convert_fusion.2), channel_id=1, source_target_pairs={{0,8},{2,18},{4,12},{6,22},{8,0},{10,26},{12,4},{14,30},{16,24},{1... | collective-permute-start | bytes 442376 | tf_op jit(solution)/shard_map/ppermute | solution.py:347
  55.3 6.8 %collective-permute-start.14 = (bf16[9,64,128]{2,1,0:T(8,128)(2,1)S(1)}, bf16[9,64,128]{2,1,0:T(8,128)(2,1)S(1)}, u32[]{:S(2)}, u32[]{:S(2)}) collective-permute-start(bf16[9,64,128]{2,1,0:T(8,128)(2,1)S(1)} %add_convert_fusion.4), channel_id=1, source_target_pairs={{0,16},{2,10},{4,20},{6,14},{8,24},{10,2},{12,28},{14,6},{16,0},{1... | collective-permute-start | bytes 442376 | tf_op jit(solution)/shard_map/ppermute | solution.py:347
  58.7 8.4 %collective-permute-start.20 = (bf16[9,64,128]{2,1,0:T(8,128)(2,1)S(1)}, bf16[9,64,128]{2,1,0:T(8,128)(2,1)S(1)}, u32[]{:S(2)}, u32[]{:S(2)}) collective-permute-start(bf16[9,64,128]{2,1,0:T(8,128)(2,1)S(1)} %add_convert_fusion.1), channel_id=1, source_target_pairs={{0,16},{2,10},{4,20},{6,14},{8,24},{10,2},{12,28},{14,6},{16,0},{1... | collective-permute-start | bytes 442376 | tf_op jit(solution)/shard_map/ppermute | solution.py:347
  62.0 10.5 %copy-start.4 = (bf16[16,96,128]{2,1,0:T(8,128)(2,1)}, bf16[16,96,128]{2,1,0:T(8,128)(2,1)S(1)}, u32[]{:S(2)}) copy-start(bf16[16,96,128]{2,1,0:T(8,128)(2,1)S(1)} %constant_dynamic-update-slice_fusion) | copy-start | bytes 1179652
  62.2 6.7 %collective-permute-start.15 = (bf16[9,64,128]{2,1,0:T(8,128)(2,1)S(1)}, bf16[9,64,128]{2,1,0:T(8,128)(2,1)S(1)}, u32[]{:S(2)}, u32[]{:S(2)}) collective-permute-start(bf16[9,64,128]{2,1,0:T(8,128)(2,1)S(1)} %add_convert_fusion.3), channel_id=1, source_target_pairs={{0,4},{2,6},{4,0},{6,2},{8,12},{10,14},{12,8},{14,10},{16,20},{18,... | collective-permute-start | bytes 442376 | tf_op jit(solution)/shard_map/ppermute | solution.py:512
  67.2 5.2 %collective-permute-start.21 = (bf16[9,64,128]{2,1,0:T(8,128)(2,1)S(1)}, bf16[9,64,128]{2,1,0:T(8,128)(2,1)S(1)}, u32[]{:S(2)}, u32[]{:S(2)}) collective-permute-start(bf16[9,64,128]{2,1,0:T(8,128)(2,1)S(1)} %add_convert_fusion), channel_id=1, source_target_pairs={{0,4},{2,6},{4,0},{6,2},{8,12},{10,14},{12,8},{14,10},{16,20},{18,... | collective-permute-start | bytes 442376 | tf_op jit(solution)/shard_map/ppermute | solution.py:513
  68.9 3.7 %collective-permute-start.16 = (bf16[9,128,128]{2,1,0:T(8,128)(2,1)S(1)}, bf16[9,128,128]{2,1,0:T(8,128)(2,1)S(1)}, u32[]{:S(2)}, u32[]{:S(2)}) collective-permute-start(bf16[9,128,128]{2,1,0:T(8,128)(2,1)S(1)} %pad_maximum_fusion.1.here), channel_id=1, source_target_pairs={{0,2},{2,0},{4,6},{6,4},{8,10},{10,8},{12,14},{14,12},{16,18},{18,... | collective-permute-start | bytes 884744 | tf_op jit(solution)/shard_map/ppermute | solution.py:353
  72.5 1.8 %collective-permute-start.22 = (bf16[9,128,128]{2,1,0:T(8,128)(2,1)S(1)}, bf16[9,128,128]{2,1,0:T(8,128)(2,1)S(1)}, u32[]{:S(2)}, u32[]{:S(2)}) collective-permute-start(bf16[9,128,128]{2,1,0:T(8,128)(2,1)S(1)} %pad_maximum_fusion.2.here), channel_id=1, source_target_pairs={{0,2},{2,0},{4,6},{6,4},{8,10},{10,8},{12,14},{14,12},{16,18},{18,... | collective-permute-start | bytes 884744 | tf_op jit(solution)/shard_map/ppermute | solution.py:353
